TPU v7x, 128 devices: a whole 4x4x4 slice. The times are simulated.
128 devices in a mesh: lat: 4 (over z_hi, core), lon: 32 (over x, z_lo, y).
Axes of the slice: x: 4, y: 4, z: 4 (z_hi: 2, z_lo: 2; z = z_hi * 2 + z_lo), core: 2. Of those that a mesh axis runs over, the one named last changes fastest.
Arguments:
- queries: bfloat16 [1, 128, 512, 3072], P(None, 'lat', 'lon'), may hold values from -11 to 11
- key_value: bfloat16 [2, 1, 128, 512, 3072], P(None, None, 'lat', 'lon'), may hold values from -11 to 11
- text_kv: bfloat16 [2, 1, 512, 3072], P(None, None, ('lat', 'lon')), may hold values from -6 to 6
Outputs:
- attended: bfloat16 [1, 128, 512, 3072], P(None, 'lat', 'lon')
All inputs are finite; a program needn't handle non-finite values.
Results may differ from a plain program's by a relative error of at most 0.005.
Values may be sent and summed in bfloat16 or wider, within the bound.
No kernel may reach another device: no remote copies, remote signals or barrier semaphores. Data moves between devices by JAX's collectives and lax.ppermute only.
A program may use at most 128 MiB of HBM per device.

v0:
```python
import math

import jax
import jax.numpy as jnp
from jax import lax
from jax.sharding import PartitionSpec as P

HD = 128
RADIUS = 8


def with_halo(x, sides, width, wrap):
    for axis, dim in sides:
        peers, length = (lax.axis_size(axis), x.shape[dim])
        up = [(i, (i + 1) % peers) for i in range(peers if wrap else peers - 1)]
        down = [(j, i) for i, j in up]
        last = lax.slice_in_dim(x, length - width, length, axis=dim)
        leading = lax.slice_in_dim(x, 0, width, axis=dim)
        before = lax.ppermute(last, axis, up)
        after = lax.ppermute(leading, axis, down)
        x = jnp.concatenate([before, x, after], axis=dim)
    return x


def neighbor_mask(rows, cols, first_row, total_rows):
    query_row = jnp.arange(rows, dtype=jnp.int32)[:, None, None, None]
    query_col = jnp.arange(cols, dtype=jnp.int32)[None, :, None, None]
    key_row = jnp.arange(rows + 2 * RADIUS, dtype=jnp.int32)[None, None, :, None]
    key_col = jnp.arange(cols + 2 * RADIUS, dtype=jnp.int32)[None, None, None, :]
    inside = (jnp.abs(key_row - RADIUS - query_row) <= RADIUS) & (
        jnp.abs(key_col - RADIUS - query_col) <= RADIUS
    )
    global_row = first_row + key_row
    inside = inside & (global_row >= 0) & (global_row < total_rows)
    return inside.reshape(rows * cols, (rows + 2 * RADIUS) * (cols + 2 * RADIUS))


def on_device(queries, key_value, text_kv):
    panos, rows, cols, channels = queries.shape
    heads = channels // HD
    widened = with_halo(key_value, (("lon", 3),), RADIUS, True)
    padded = with_halo(widened, (("lat", 2),), RADIUS, False)
    prompt = lax.all_gather(text_kv, ("lat", "lon"), axis=2, tiled=True)
    text_len = prompt.shape[2]
    text_keys = prompt[0].reshape(panos, text_len, heads, HD)
    text_values = prompt[1].reshape(panos, text_len, heads, HD)
    span_cols = cols + 2 * RADIUS
    block_rows = math.gcd(rows, 8)
    block_span = block_rows + 2 * RADIUS
    block_count = rows // block_rows
    first_row = lax.axis_index("lat") * rows - RADIUS
    total_rows = lax.axis_size("lat") * rows
    scale = 1.0 / math.sqrt(HD)

    def one_block(block, output):
        row_start = (block * block_rows).astype(jnp.int32)
        zero = jnp.zeros((), jnp.int32)
        query_block = lax.dynamic_slice(
            queries, (zero, row_start, zero, zero), (panos, block_rows, cols, channels)
        )
        query_block = query_block.reshape(panos, block_rows * cols, heads, HD)
        region = lax.dynamic_slice(
            padded, (zero, zero, row_start, zero, zero), (2, panos, block_span, span_cols, channels)
        )
        near_keys = region[0].reshape(panos, block_span * span_cols, heads, HD)
        near_values = region[1].reshape(panos, block_span * span_cols, heads, HD)
        allowed = neighbor_mask(block_rows, cols, first_row + row_start, total_rows)
        near = (
            jnp.einsum(
                "pqhd,pkhd->phqk", query_block, near_keys, preferred_element_type=jnp.float32
            )
            * scale
        )
        far = (
            jnp.einsum(
                "pqhd,pkhd->phqk", query_block, text_keys, preferred_element_type=jnp.float32
            )
            * scale
        )
        near = jnp.where(allowed[None, None], near, -jnp.inf)
        top = jnp.maximum(
            jnp.max(near, axis=-1, keepdims=True), jnp.max(far, axis=-1, keepdims=True)
        )
        near_exp = jnp.exp(near - top)
        far_exp = jnp.exp(far - top)
        total = jnp.sum(near_exp, axis=-1, keepdims=True) + jnp.sum(far_exp, axis=-1, keepdims=True)
        near_weight = (near_exp / total).astype(jnp.bfloat16)
        far_weight = (far_exp / total).astype(jnp.bfloat16)
        result = jnp.einsum(
            "phqk,pkhd->pqhd", near_weight, near_values, preferred_element_type=jnp.float32
        )
        result = result + jnp.einsum(
            "phqk,pkhd->pqhd", far_weight, text_values, preferred_element_type=jnp.float32
        )
        result = result.astype(jnp.bfloat16).reshape(panos, block_rows, cols, channels)
        return lax.dynamic_update_slice(output, result, (zero, row_start, zero, zero))

    output = jnp.zeros((panos, rows, cols, channels), jnp.bfloat16)
    return lax.fori_loop(0, block_count, one_block, output)


def solution(mesh):
    in_specs = (
        P(None, "lat", "lon", None),
        P(None, None, "lat", "lon", None),
        P(None, None, ("lat", "lon"), None),
    )
    out_specs = P(None, "lat", "lon", None)
    return jax.shard_map(
        on_device, mesh=mesh, in_specs=in_specs, out_specs=out_specs, check_vma=False
    )
```

profile of v0, /device:TPU:1, one launch (start us, length us, event | category | flops | bytes accessed | tf_op | source)
XLA Modules:
  0.0 661.8 jit_solution(6051796220610429859)
XLA Ops:
  8.0 5.3 fusion.27
  15.4 5.0 collective-permute-start.1
  20.4 67.8 %collective-permute-done = bf16[2,1,32,8,3072]{4,3,2,1,0:T(8,128)(2,1)S(1)} collective-permute-done((bf16[2,1,32,8,3072]{4,3,2,1,0:T(8,128)(2,1)S(1)}, bf16[2,1,32,8,3072]{4,3,2,1,0:T(8,128)(2,1)S(1)}, u32[]{:S(2)}, u32[]{:S(2)}) %collective-permute-start) | collective-permute-done | bytes 3145760 | tf_op jit(solution)/shard_map/ppermute | solution.py:19
  91.1 3.4 fusion.25
  94.5 3.0 copy-done.1
  97.6 3.2 collective-permute-start.3
  100.8 5.1 collective-permute-start.2
  106.0 35.1 %collective-permute-done.3 = bf16[2,1,8,32,3072]{4,3,2,1,0:T(8,128)(2,1)S(1)} collective-permute-done((bf16[2,1,8,32,3072]{4,3,2,1,0:T(8,128)(2,1)}, bf16[2,1,8,32,3072]{4,3,2,1,0:T(8,128)(2,1)S(1)}, u32[]{:S(2)}, u32[]{:S(2)}) %collective-permute-start.3) | collective-permute-done | bytes 3145760 | tf_op jit(solution)/shard_map/ppermute | solution.py:20
  142.4 15.5 %pad_maximum_fusion = bf16[2,1,48,32,3072]{4,3,2,1,0:T(8,128)(2,1)} fusion(bf16[2,1,8,32,3072]{4,3,2,1,0:T(8,128)(2,1)S(1)} %collective-permute-done.3, bf16[2,1,32,32,3072]{4,3,2,1,0:T(8,128)(2,1)} %copy-done.1, bf16[2,1,8,32,3072]{4,3,2,1,0:T(8,128)(2,1)} %collective-permute-done.2), kind=kLoop, calls=%fused_computation.39 | loop fusion | flops 18874368 | bytes 37748736 | tf_op jit(solution)/shard_map/concatenate | solution.py:21
  158.0 241.6 %all-gather.2.cloned.1.call-done = bf16[2,1,512,3072]{3,0,1,2:T(2,128)(2,1)} async-done(((bf16[2,1,4,3072]{3,0,1,2:T(2,128)(2,1)}), bf16[2,1,512,3072]{3,0,1,2:T(2,128)(2,1)}) %all-gather.2.cloned.1.call-update) | async-done | bytes 6291472 | tf_op jit(solution)/shard_map/all_gather | solution.py:43
  399.6 13.4 %fusion.26 = (bf16[1,1,512,3072]{3,0,1,2:T(2,128)(2,1)}, bf16[1,1,512,3072]{3,0,1,2:T(2,128)(2,1)}) fusion(bf16[2,1,512,3072]{3,0,1,2:T(2,128)(2,1)} %all-gather.2.cloned.1.call-done), kind=kLoop, calls=%fused_computation.44 | loop fusion | bytes 12582912 | tf_op jit(solution)/shard_map/slice | solution.py:46
  413.0 13.5 %copy.30 = bf16[1,1,512,3072]{2,3,1,0:T(8,128)(2,1)} copy(bf16[1,1,512,3072]{3,0,1,2:T(2,128)(2,1)} %get-tuple-element.241) | data formatting | bytes 6291456
  426.5 3.5 copy.27
  429.9 13.5 %copy.31 = bf16[1,1,512,3072]{2,3,1,0:T(8,128)(2,1)} copy(bf16[1,1,512,3072]{3,0,1,2:T(2,128)(2,1)} %get-tuple-element.240) | data formatting | bytes 6291456
  443.4 4.7 copy.28
  450.2 204.8 %while.16 = (s32[]{:T(128)}, bf16[1,32,16,3072]{3,2,1,0:T(8,128)(2,1)}, bf16[2,1,48,32,3072]{4,3,2,1,0:T(8,128)(2,1)}, s32[]{:T(128)}, bf16[1,32,16,3072]{3,2,1,...) while((s32[]{:T(128)}, ...), condition=%wide.region_5.6_spmd, body=%wide.region_0.5_spmd.sunk | while | flops 2056810752 | bytes 140189872 | solution.py:99
  450.2 7.1 %constant_dynamic-slice_fusion.5 = (bf16[1,1,24,32,3072]{4,3,2,1,0:T(8,128)(2,1)}, bf16[1,1,24,32,3072]{4,3,2,1,0:T(8,128)(2,1)S(1)}) fusion(bf16[2,1,48,32,3072]{4,3,2,1,0:T(8,128)(2,1)} %get-tuple-element.331, s32[]{:T(128)S(6)} %select_n.54, s32[]{:T(128)S(6)} %add.165), kind=kLoop, calls=%fused_computation.30.clone.1 | loop fusion | bytes 18874376 | tf_op jit(solution)/shard_map/while/body/eval_jaxpr/slice | solution.py:65
  457.3 3.6 copy.61
  463.6 5.8 copy.62
  470.8 4.7 fusion.39
  476.6 2.3 fusion.40
  480.6 6.7 %fusion.42 = f32[24,128,128]{2,1,0:T(8,128)} fusion(bf16[768,24,128]{2,1,0:T(8,128)(2,1)} %bitcast.65, f32[24,128,768]{2,1,0:T(8,128)S(1)} %get-tuple-element.299, f32[24,128]{1,0:T(8,128)S(1)} %add.168, f32[24,128]{1,0:T(8,128)S(1)} %max.17, pred[128,768]{1,0:T(8,128)(4,1)S(1)} %and_and_fusion.2), kind=kOutput, calls=%fused_computation.9.clone.1 | convolution fusion | flops 615776256 | bytes 15851520 | tf_op jit(solution)/shard_map/while/body/eval_jaxpr/phqk,pkhd->pqhd/dot_general | solution.py:89
  487.2 7.5 %fusion.43 = bf16[1,128,24,128]{1,3,2,0:T(8,128)(2,1)} fusion(f32[24,128,128]{2,1,0:T(8,128)} %fusion.42, bf16[1,512,24,128]{3,1,2,0:T(8,128)(2,1)} %get-tuple-element.335, f32[24,128,512]{2,1,0:T(8,128)} %copy-done, f32[24,128]{1,0:T(8,128)S(1)} %add.168, f32[24,128]{1,0:T(8,128)S(1)} %max.17), kind=kOutput, calls=%fused_computation.20.clone.1 | convolution fusion | flops 409731072 | bytes 11821056 | tf_op jit(solution)/shard_map/while/body/eval_jaxpr/phqk,pkhd->pqhd/dot_general | solution.py:92
  494.7 2.4 copy.64
  501.4 7.1 %constant_dynamic-slice_fusion.5 = (bf16[1,1,24,32,3072]{4,3,2,1,0:T(8,128)(2,1)}, bf16[1,1,24,32,3072]{4,3,2,1,0:T(8,128)(2,1)S(1)}) fusion(bf16[2,1,48,32,3072]{4,3,2,1,0:T(8,128)(2,1)} %get-tuple-element.331, s32[]{:T(128)S(6)} %select_n.54, s32[]{:T(128)S(6)} %add.165), kind=kLoop, calls=%fused_computation.30.clone.1 | loop fusion | bytes 18874376 | tf_op jit(solution)/shard_map/while/body/eval_jaxpr/slice | solution.py:65
  508.5 3.6 copy.61
  514.8 5.8 copy.62
  522.0 4.7 fusion.39
  527.8 2.3 fusion.40
  531.8 6.7 %fusion.42 = f32[24,128,128]{2,1,0:T(8,128)} fusion(bf16[768,24,128]{2,1,0:T(8,128)(2,1)} %bitcast.65, f32[24,128,768]{2,1,0:T(8,128)S(1)} %get-tuple-element.299, f32[24,128]{1,0:T(8,128)S(1)} %add.168, f32[24,128]{1,0:T(8,128)S(1)} %max.17, pred[128,768]{1,0:T(8,128)(4,1)S(1)} %and_and_fusion.2), kind=kOutput, calls=%fused_computation.9.clone.1 | convolution fusion | flops 615776256 | bytes 15851520 | tf_op jit(solution)/shard_map/while/body/eval_jaxpr/phqk,pkhd->pqhd/dot_general | solution.py:89
  538.4 7.5 %fusion.43 = bf16[1,128,24,128]{1,3,2,0:T(8,128)(2,1)} fusion(f32[24,128,128]{2,1,0:T(8,128)} %fusion.42, bf16[1,512,24,128]{3,1,2,0:T(8,128)(2,1)} %get-tuple-element.335, f32[24,128,512]{2,1,0:T(8,128)} %copy-done, f32[24,128]{1,0:T(8,128)S(1)} %add.168, f32[24,128]{1,0:T(8,128)S(1)} %max.17), kind=kOutput, calls=%fused_computation.20.clone.1 | convolution fusion | flops 409731072 | bytes 11821056 | tf_op jit(solution)/shard_map/while/body/eval_jaxpr/phqk,pkhd->pqhd/dot_general | solution.py:92
  545.9 2.4 copy.64
  552.6 7.1 %constant_dynamic-slice_fusion.5 = (bf16[1,1,24,32,3072]{4,3,2,1,0:T(8,128)(2,1)}, bf16[1,1,24,32,3072]{4,3,2,1,0:T(8,128)(2,1)S(1)}) fusion(bf16[2,1,48,32,3072]{4,3,2,1,0:T(8,128)(2,1)} %get-tuple-element.331, s32[]{:T(128)S(6)} %select_n.54, s32[]{:T(128)S(6)} %add.165), kind=kLoop, calls=%fused_computation.30.clone.1 | loop fusion | bytes 18874376 | tf_op jit(solution)/shard_map/while/body/eval_jaxpr/slice | solution.py:65
  559.7 3.6 copy.61
  566.1 5.8 copy.62
  573.2 4.7 fusion.39
  579.0 2.3 fusion.40
  583.0 6.7 %fusion.42 = f32[24,128,128]{2,1,0:T(8,128)} fusion(bf16[768,24,128]{2,1,0:T(8,128)(2,1)} %bitcast.65, f32[24,128,768]{2,1,0:T(8,128)S(1)} %get-tuple-element.299, f32[24,128]{1,0:T(8,128)S(1)} %add.168, f32[24,128]{1,0:T(8,128)S(1)} %max.17, pred[128,768]{1,0:T(8,128)(4,1)S(1)} %and_and_fusion.2), kind=kOutput, calls=%fused_computation.9.clone.1 | convolution fusion | flops 615776256 | bytes 15851520 | tf_op jit(solution)/shard_map/while/body/eval_jaxpr/phqk,pkhd->pqhd/dot_general | solution.py:89
  589.6 7.5 %fusion.43 = bf16[1,128,24,128]{1,3,2,0:T(8,128)(2,1)} fusion(f32[24,128,128]{2,1,0:T(8,128)} %fusion.42, bf16[1,512,24,128]{3,1,2,0:T(8,128)(2,1)} %get-tuple-element.335, f32[24,128,512]{2,1,0:T(8,128)} %copy-done, f32[24,128]{1,0:T(8,128)S(1)} %add.168, f32[24,128]{1,0:T(8,128)S(1)} %max.17), kind=kOutput, calls=%fused_computation.20.clone.1 | convolution fusion | flops 409731072 | bytes 11821056 | tf_op jit(solution)/shard_map/while/body/eval_jaxpr/phqk,pkhd->pqhd/dot_general | solution.py:92
  597.1 2.4 copy.64
  603.8 7.1 %constant_dynamic-slice_fusion.5 = (bf16[1,1,24,32,3072]{4,3,2,1,0:T(8,128)(2,1)}, bf16[1,1,24,32,3072]{4,3,2,1,0:T(8,128)(2,1)S(1)}) fusion(bf16[2,1,48,32,3072]{4,3,2,1,0:T(8,128)(2,1)} %get-tuple-element.331, s32[]{:T(128)S(6)} %select_n.54, s32[]{:T(128)S(6)} %add.165), kind=kLoop, calls=%fused_computation.30.clone.1 | loop fusion | bytes 18874376 | tf_op jit(solution)/shard_map/while/body/eval_jaxpr/slice | solution.py:65
  610.9 3.6 copy.61
  617.3 5.8 copy.62
  624.4 4.7 fusion.39
  630.2 2.3 fusion.40
  634.2 6.7 %fusion.42 = f32[24,128,128]{2,1,0:T(8,128)} fusion(bf16[768,24,128]{2,1,0:T(8,128)(2,1)} %bitcast.65, f32[24,128,768]{2,1,0:T(8,128)S(1)} %get-tuple-element.299, f32[24,128]{1,0:T(8,128)S(1)} %add.168, f32[24,128]{1,0:T(8,128)S(1)} %max.17, pred[128,768]{1,0:T(8,128)(4,1)S(1)} %and_and_fusion.2), kind=kOutput, calls=%fused_computation.9.clone.1 | convolution fusion | flops 615776256 | bytes 15851520 | tf_op jit(solution)/shard_map/while/body/eval_jaxpr/phqk,pkhd->pqhd/dot_general | solution.py:89
  640.8 7.5 %fusion.43 = bf16[1,128,24,128]{1,3,2,0:T(8,128)(2,1)} fusion(f32[24,128,128]{2,1,0:T(8,128)} %fusion.42, bf16[1,512,24,128]{3,1,2,0:T(8,128)(2,1)} %get-tuple-element.335, f32[24,128,512]{2,1,0:T(8,128)} %copy-done, f32[24,128]{1,0:T(8,128)S(1)} %add.168, f32[24,128]{1,0:T(8,128)S(1)} %max.17), kind=kOutput, calls=%fused_computation.20.clone.1 | convolution fusion | flops 409731072 | bytes 11821056 | tf_op jit(solution)/shard_map/while/body/eval_jaxpr/phqk,pkhd->pqhd/dot_general | solution.py:92
  648.3 2.4 copy.64
  (104 shorter events, 54.3 us)
Async XLA Ops:
  6.5 393.0 %all-gather.2.cloned.1.call-start = ((), (), s32[]{:S(2)}) async-start(), calls=%async_computation | async-start | bytes 6340608 | tf_op jit(solution)/shard_map/all_gather | solution.py:43
  8.0 80.5 %slice-start = ((s8[6291456]{0:T(1024)(128)(4,1)}), s8[2097152]{0:T(1024)(128)(4,1)S(1)}, s32[]{:S(2)}) async-start(s8[6291456]{0:T(1024)(128)(4,1)} %bitcast.67), calls=%async_computation.1 | async-start | bytes 4194304
  8.0 80.5 %slice-start.1 = ((s8[6291456]{0:T(1024)(128)(4,1)}), s8[4194304]{0:T(1024)(128)(4,1)S(1)}, s32[]{:S(2)}) async-start(s8[6291456]{0:T(1024)(128)(4,1)} %bitcast.67), calls=%async_computation.2 | async-start | bytes 8388608
  13.3 74.9 %collective-permute-start = (bf16[2,1,32,8,3072]{4,3,2,1,0:T(8,128)(2,1)S(1)}, bf16[2,1,32,8,3072]{4,3,2,1,0:T(8,128)(2,1)S(1)}, u32[]{:S(2)}, u32[]{:S(2)}) collective-permute-start(bf16[2,1,32,8,3072]{4,3,2,1,0:T(8,128)(2,1)S(1)} %get-tuple-element.243), channel_id=1, source_target_pairs={{0,1},{1,2},{2,3},{3,4},{4,5},{5,6},{6,7},{7,8},{8,9},{9,10},{10,1... | collective-permute-start | bytes 9437192 | tf_op jit(solution)/shard_map/ppermute | solution.py:19
  15.4 73.5 %collective-permute-start.1 = (bf16[2,1,32,8,3072]{4,3,2,1,0:T(8,128)(2,1)}, bf16[2,1,32,8,3072]{4,3,2,1,0:T(8,128)(2,1)}, u32[]{:S(2)}, u32[]{:S(2)}) collective-permute-start(bf16[2,1,32,8,3072]{4,3,2,1,0:T(8,128)(2,1)} %get-tuple-element.242), channel_id=1, source_target_pairs={{1,0},{2,1},{3,2},{4,3},{5,4},{6,5},{7,6},{8,7},{9,8},{10,9},{11,1... | collective-permute-start | bytes 9437192 | tf_op jit(solution)/shard_map/ppermute | solution.py:20
  91.1 6.5 copy-start.1
  97.6 43.5 %collective-permute-start.3 = (bf16[2,1,8,32,3072]{4,3,2,1,0:T(8,128)(2,1)}, bf16[2,1,8,32,3072]{4,3,2,1,0:T(8,128)(2,1)S(1)}, u32[]{:S(2)}, u32[]{:S(2)}) collective-permute-start(bf16[2,1,8,32,3072]{4,3,2,1,0:T(8,128)(2,1)} %get-tuple-element.239), channel_id=1, source_target_pairs={{32,0},{64,32},{96,64},{33,1},{65,33},{97,65},{34,2},{66,34},{98,6... | collective-permute-start | bytes 9437192 | tf_op jit(solution)/shard_map/ppermute | solution.py:20
  100.8 41.6 %collective-permute-start.2 = (bf16[2,1,8,32,3072]{4,3,2,1,0:T(8,128)(2,1)}, bf16[2,1,8,32,3072]{4,3,2,1,0:T(8,128)(2,1)}, u32[]{:S(2)}, u32[]{:S(2)}) collective-permute-start(bf16[2,1,8,32,3072]{4,3,2,1,0:T(8,128)(2,1)} %get-tuple-element.238), channel_id=1, source_target_pairs={{0,32},{32,64},{64,96},{1,33},{33,65},{65,97},{2,34},{34,66},{66,9... | collective-permute-start | bytes 9437192 | tf_op jit(solution)/shard_map/ppermute | solution.py:19
  476.6 4.0 copy-start
  527.8 4.0 copy-start
  579.0 4.0 copy-start
  630.2 4.0 copy-start
Sparse Core Ops, SparseCore 0:
  9.0 390.4 all-gather.1
where the time goes:
time: 664 us; the launch traced here: 662 us
  waiting for transfers between devices  346 us (52%)
  local copies, waits for them, and re-layouts  171 us (26%)
  matrix products  79.5 us (12%)
  other arithmetic  36.4 us (5%)
  starting transfers between devices  15.5 us (2%)
  between operations  13.5 us (2%)
    all_gather x1, waiting for transfers between devices, on_device(): prompt = lax.all_gather(text_kv, ('lat', 'lon'), axis=2, tiled=True)  242 us
    ppermute x2, waiting for transfers between devices, with_halo(): before = lax.ppermute(last, axis, up)  69.2 us
    while x20, local copies, waits for them, and re-layouts  38.3 us
    ppermute x2, waiting for transfers between devices, with_halo(): after = lax.ppermute(leading, axis, down)  35.1 us
    unnamed x11, local copies, waits for them, and re-layouts  32.1 us
    dot_general x4, matrix products, one_block(): jnp.einsum('phqk,pkhd->pqhd', far_weight, text_values, preferred_element_...  30 us
    slice x4, local copies, waits for them, and re-layouts, one_block(): near_keys = region[0].reshape(panos, block_span * span_cols, heads, HD)  28.4 us
    dot_general x4, matrix products, one_block(): jnp.einsum('phqk,pkhd->pqhd', near_weight, near_values, preferred_element...  26.6 us
  transfers between devices with their start and end apart: 5, of which 4 were waited for; matrix products, arithmetic and copies ran while one was open for 4% of the time, Pallas kernels for 0%

commit v1 on v0

v1 whole, which is shorter than its diff:
```python
import functools
import math

import jax
import jax.numpy as jnp
import numpy as np
from jax import lax
from jax.experimental import pallas as pl
from jax.experimental.pallas import tpu as pltpu
from jax.sharding import PartitionSpec as P

HD = 128
RADIUS = 8
NEG = -1e30
ZH, CORE, NX, ZL, NY = 2, 2, 4, 2, 4
N_LAT, N_LON = ZH * CORE, NX * ZL * NY
CHUNKS = (8, 8, 6, 2)
PER_STEP = 2
WIDE = PER_STEP * HD
BLOCK = 16


def send(x, zh=0, core=0, x_=0, zl=0, y=0):
    pairs = []
    for i in range(N_LAT * N_LON):
        c = list(np.unravel_index(i, (ZH, CORE, NX, ZL, NY)))
        t = [(a + b) % n for a, b, n in zip(c, (zh, core, x_, zl, y), (ZH, CORE, NX, ZL, NY))]
        pairs.append((i, int(np.ravel_multi_index(t, (ZH, CORE, NX, ZL, NY)))))
    return lax.ppermute(x, ("lat", "lon"), pairs)


def send_lon(x, step):
    return lax.ppermute(x, "lon", [(i, (i + step) % N_LON) for i in range(N_LON)])


def send_lat(x, step):
    return lax.ppermute(
        x, "lat", [(i, i + step) for i in range(N_LAT) if 0 <= i + step < N_LAT]
    )


def gather_prompt(text_kv):
    core = lax.axis_index("lat") % CORE
    text = text_kv[:, 0]
    mine = lax.dynamic_index_in_dim(text, core, 0, keepdims=False)
    theirs = lax.dynamic_index_in_dim(text, 1 - core, 0, keepdims=False)
    other = send(theirs, core=1)
    first = core == 0
    block = jnp.concatenate([jnp.where(first, mine, other), jnp.where(first, other, mine)], 0)[None]
    block = jnp.concatenate([block, send(block, y=1), send(block, y=3), send(block, y=2)], 0)
    block = jnp.concatenate(
        [block, send(block, zl=1), send(block, zh=1), send(block, zh=1, zl=1)], 0
    )
    up, down = send(block, x_=1), send(block, x_=3)
    half = block.shape[0] // 2
    far_a, far_b = send(up[:half], x_=1), send(down[half:], x_=3)
    own = jnp.concatenate([block, up, down, far_a, far_b], 0)
    return own, send(own, core=1)


def pack_body(own_ref, r_ref, l_ref):
    l_ref[...] = own_ref[:, 0, :, :RADIUS]
    r_ref[...] = own_ref[:, 0, :, RADIUS:]


def pack_tall_body(own_ref, top_ref, bot_ref, r_ref, l_ref):
    for ref, cols in ((l_ref, slice(0, RADIUS)), (r_ref, slice(RADIUS, 2 * RADIUS))):
        ref[:, :RADIUS] = top_ref[:, :, cols]
        ref[:, RADIUS : RADIUS + 32] = own_ref[:, 0, :, cols]
        ref[:, RADIUS + 32 :] = bot_ref[:, :, cols]


def pack(own, head, heads, edges=None):
    at = head // PER_STEP
    rows = 32 if edges is None else 48
    out = jax.ShapeDtypeStruct((2, rows, RADIUS, heads * HD), jnp.bfloat16)
    specs = [pl.BlockSpec((2, 1, 32, 16, WIDE), lambda i: (0, 0, 0, 0, at + i))]
    if edges is not None:
        specs += [pl.BlockSpec((2, RADIUS, 16, WIDE), lambda i: (0, 0, 0, at + i))] * 2
    return pl.pallas_call(
        pack_body if edges is None else pack_tall_body,
        grid=(heads // PER_STEP,),
        in_specs=specs,
        out_specs=[pl.BlockSpec((2, rows, RADIUS, WIDE), lambda i: (0, 0, 0, i))] * 2,
        out_shape=[out, out],
        compiler_params=pltpu.CompilerParams(vmem_limit_bytes=40 << 20),
    )(own, *(edges or ()))


def attend_body(tall, first_call, *refs):
    refs = list(refs)
    flip_ref, q_ref, own_ref, left_ref, right_ref, top_ref, bot_ref = refs[:7]
    del refs[:7]
    if not tall:
        tc_ref, bc_ref = refs[:2]
        del refs[:2]
    ta_ref, tb_ref, e_ref, f_ref = refs[:4]
    del refs[:4]
    if not first_call:
        del refs[:1]
    o_ref, keys_s, vals_s, tvals_s = refs
    rows, cols = 32, 16

    @pl.when(pl.program_id(0) == 0)
    def _():
        keys_s[:, :, HD:] = f_ref[...]
        vals_s[:, :, HD:] = jnp.ones((48, 32, HD), jnp.bfloat16)
        tvals_s[:, HD:] = jnp.ones((512, HD), jnp.bfloat16)

    scale = math.log2(math.e) / math.sqrt(HD)
    nt = (((1,), (1,)), ((), ()))
    flip = flip_ref[0] == 1
    for head in range(PER_STEP):
        hs = slice(head * HD, (head + 1) * HD)
        for kv, dst in ((0, keys_s), (1, vals_s)):
            left, right = left_ref[kv, :, :, hs], right_ref[kv, :, :, hs]
            top, bot, own = top_ref[kv, :, :, hs], bot_ref[kv, :, :, hs], own_ref[kv, 0, :, :, hs]
            if tall:
                middle = jnp.concatenate([top, own, bot], axis=0)
                dst[:, :, :HD] = jnp.concatenate([left, middle, right], axis=1)
            else:
                dst[8:40, :, :HD] = jnp.concatenate([left, own, right], axis=1)
                dst[0:8, :, :HD] = jnp.concatenate(
                    [tc_ref[0, kv, :, :, hs], top, tc_ref[1, kv, :, :, hs]], axis=1
                )
                dst[40:48, :, :HD] = jnp.concatenate(
                    [bc_ref[0, kv, :, :, hs], bot, bc_ref[1, kv, :, :, hs]], axis=1
                )
        a, b = ta_ref[:, :, hs].reshape(512, HD), tb_ref[:, :, hs].reshape(512, HD)
        text_keys = jnp.where(flip, b, a)
        tvals_s[:, :HD] = jnp.where(flip, a, b)
        for r in range(rows // BLOCK):
            q = q_ref[0, r * BLOCK : (r + 1) * BLOCK, :, hs].reshape(BLOCK * cols, HD)
            q_wide = jnp.concatenate([q, e_ref[r * BLOCK * cols : (r + 1) * BLOCK * cols]], axis=1)
            span = BLOCK + 2 * RADIUS
            keys = keys_s[r * BLOCK : r * BLOCK + span].reshape(span * 32, 2 * HD)
            vals = vals_s[r * BLOCK : r * BLOCK + span].reshape(span * 32, 2 * HD)
            near = lax.dot_general(q_wide, keys, nt, preferred_element_type=jnp.float32)
            far = lax.dot_general(q, text_keys, nt, preferred_element_type=jnp.float32)
            top = jnp.maximum(
                jnp.max(near, -1, keepdims=True), jnp.max(far, -1, keepdims=True)
            )
            near = jnp.exp2((near - top) * scale).astype(jnp.bfloat16)
            far = jnp.exp2((far - top) * scale).astype(jnp.bfloat16)
            out = jnp.dot(near, vals, preferred_element_type=jnp.float32)
            out = out + jnp.dot(far, tvals_s[...], preferred_element_type=jnp.float32)
            out = (out[:, :HD] / out[:, HD:]).astype(jnp.bfloat16)
            o_ref[0, r * BLOCK : (r + 1) * BLOCK, :, hs] = out.reshape(BLOCK, cols, HD)


def attend(flip, queries, own, left, right, top, bot, corners, text, feats, output, head, heads):
    at = head // PER_STEP
    tall = corners is None
    rows = 48 if tall else 32
    spec = pl.BlockSpec
    in_specs = [
        spec(memory_space=pltpu.SMEM),
        spec((1, 32, 16, WIDE), lambda i: (0, 0, 0, at + i)),
        spec((2, 1, 32, 16, WIDE), lambda i: (0, 0, 0, 0, at + i)),
        spec((2, rows, RADIUS, WIDE), lambda i: (0, 0, 0, i)),
        spec((2, rows, RADIUS, WIDE), lambda i: (0, 0, 0, i)),
        spec((2, RADIUS, 16, WIDE), lambda i: (0, 0, 0, at + i)),
        spec((2, RADIUS, 16, WIDE), lambda i: (0, 0, 0, at + i)),
    ]
    args = [flip, queries, own, left, right, top, bot]
    if not tall:
        in_specs += [spec((2, 2, RADIUS, RADIUS, WIDE), lambda i: (0, 0, 0, 0, i))] * 2
        args += corners
    in_specs += [
        spec((64, 8, WIDE), lambda i: (0, 0, at + i)),
        spec((64, 8, WIDE), lambda i: (0, 0, at + i)),
        spec((512, HD), lambda i: (0, 0)),
        spec((48, 32, HD), lambda i: (0, 0, 0)),
    ]
    args += [*text, *feats]
    aliases = {}
    if output is not None:
        aliases = {len(args): 0}
        in_specs.append(spec(memory_space=pl.ANY))
        args.append(output)
    return pl.pallas_call(
        functools.partial(attend_body, tall, output is None),
        grid=(heads // PER_STEP,),
        in_specs=in_specs,
        out_specs=spec((1, 32, 16, WIDE), lambda i: (0, 0, 0, at + i)),
        out_shape=jax.ShapeDtypeStruct(queries.shape, jnp.bfloat16),
        scratch_shapes=[
            pltpu.VMEM((48, 32, 2 * HD), jnp.bfloat16),
            pltpu.VMEM((48, 32, 2 * HD), jnp.bfloat16),
            pltpu.VMEM((512, 2 * HD), jnp.bfloat16),
        ],
        input_output_aliases=aliases,
        compiler_params=pltpu.CompilerParams(vmem_limit_bytes=40 << 20),
        cost_estimate=pl.CostEstimate(
            flops=heads * 1_500_000_000, bytes_accessed=heads << 20, transcendentals=0
        ),
    )(*args)


def features():
    query = np.arange(512)
    lane = np.arange(HD)
    hot = (
        (lane[None] == (query % 16)[:, None])
        | (lane[None] - 16 == (query // 16)[:, None])
        | (lane[None] == 48)
    )
    row = jnp.arange(48, dtype=jnp.int32)[:, None, None] - RADIUS
    col = jnp.arange(32, dtype=jnp.int32)[None, :, None] - RADIUS
    lane = jnp.arange(HD, dtype=jnp.int32)[None, None, :]
    grid_row = lax.axis_index("lat") * 32 + row
    bad = (lane < 16) & (jnp.abs(col - lane) > RADIUS)
    bad |= (lane >= 16) & (lane < 48) & (jnp.abs(row - (lane - 16)) > RADIUS)
    bad |= (lane == 48) & ((grid_row < 0) | (grid_row >= N_LAT * 32))
    return jnp.asarray(hot, jnp.bfloat16), jnp.where(bad, NEG, 0.0).astype(jnp.bfloat16)


def on_device(queries, key_value, text_kv):
    flip = (lax.axis_index("lat") % CORE).astype(jnp.int32)[None]
    starts = [sum(CHUNKS[:i]) for i in range(len(CHUNKS))]
    feats = features()
    top = send_lat(key_value[:, 0, -RADIUS:], 1)
    bot = send_lat(key_value[:, 0, :RADIUS], -1)
    sides = []
    for head, heads in zip(starts, CHUNKS):
        last = head == starts[-1]
        r, l = pack(key_value, head, heads, (top, bot) if last else None)
        sides.append((send_lon(r, 1), send_lon(l, -1)))
    text = gather_prompt(text_kv)
    output = None
    for head, heads, (left, right) in zip(starts, CHUNKS, sides):
        corners = None
        if head != starts[-1]:
            down = jnp.stack([left[:, -RADIUS:], right[:, -RADIUS:]])
            up = jnp.stack([left[:, :RADIUS], right[:, :RADIUS]])
            corners = [send_lat(down, 1), send_lat(up, -1)]
        output = attend(
            flip, queries, key_value, left, right, top, bot, corners, text, feats, output, head, heads
        )
    return output


def solution(mesh):
    in_specs = (
        P(None, "lat", "lon", None),
        P(None, None, "lat", "lon", None),
        P(None, None, ("lat", "lon"), None),
    )
    out_specs = P(None, "lat", "lon", None)
    return jax.shard_map(
        on_device, mesh=mesh, in_specs=in_specs, out_specs=out_specs, check_vma=False
    )
```

time: 664 us -> 224 us (0.34)
  waiting for transfers between devices: 346 us -> 73.5 us
  local copies, waits for them, and re-layouts: 171 us -> 23.8 us
  matrix products: 79.5 us -> 0 us
  starting transfers between devices: 15.5 us -> 74.8 us
  Pallas kernels: 0 us -> 47.1 us
  other arithmetic: 36.4 us -> 3.81 us
  between operations: 13.5 us -> 0.42 us
    all_gather x1 -> x0, waiting for transfers between devices: 242 us -> none  [on_device(): prompt = lax.all_gather(text_kv, ('lat', 'lon'), axis=2, tiled=True)]
    dot_general x16 -> x0, matrix products: 79.5 us -> none  [the longest x4 30 us: one_block(): jnp.einsum('phqk,pkhd->pqhd', far_weight, text_values, preferred_element_...]
    ppermute x4 -> x28, starting transfers between devices: 15.5 us -> 74.8 us  [the longest x8 27.3 us: send_lat(): lax.ppermute(x, 'lat', [(i, i + step) for i in range(N_LAT) if 0 <= i + s...]
    slice x7 -> x2, local copies, waits for them, and re-layouts: 50.6 us -> 0.05 us  [gather_prompt(): far_a, far_b = (send(up[:half], x_=1), send(down[half:], x_=3))]
    pallas_call x0 -> x8, Pallas kernels: none -> 47.1 us  [the longest x4 42 us: attend(): pl.pallas_call(functools.partial(attend_body, tall, output is None), grid...]
    while x22 -> x0, local copies, waits for them, and re-layouts: 46.5 us -> none
    ppermute x4 -> x28, waiting for transfers between devices: 104 us -> 73.5 us  [the longest x12 58 us: send(): return lax.ppermute(x, ('lat', 'lon'), pairs)]
    unnamed x11 -> x32, local copies, waits for them, and re-layouts: 32.1 us -> 13.6 us
  transfers between devices with their start and end apart: 5 -> 28, of which waited for: 4 -> 10; matrix products, arithmetic and copies ran while one was open for 4% -> 9% of each run, Pallas kernels for 0% -> 19%
where the time goes in v1:
time: 224 us; the launch traced here: 223 us
  starting transfers between devices  74.8 us (33%)
  waiting for transfers between devices  73.5 us (33%)
  Pallas kernels  47.1 us (21%)
  local copies, waits for them, and re-layouts  23.8 us (11%)
  other arithmetic  3.81 us (2%)
    ppermute x12, waiting for transfers between devices, send(): return lax.ppermute(x, ('lat', 'lon'), pairs)  58 us
    pallas_call x4, Pallas kernels, attend(): pl.pallas_call(functools.partial(attend_body, tall, output is None), grid...  42 us
    ppermute x8, starting transfers between devices, send_lat(): lax.ppermute(x, 'lat', [(i, i + step) for i in range(N_LAT) if 0 <= i + s...  27.3 us
    ppermute x8, starting transfers between devices, send_lon(): lax.ppermute(x, 'lon', [(i, (i + step) % N_LON) for i in range(N_LON)])  26.7 us
    ppermute x12, starting transfers between devices, send(): return lax.ppermute(x, ('lat', 'lon'), pairs)  20.9 us
    ppermute x8, waiting for transfers between devices, send_lon(): lax.ppermute(x, 'lon', [(i, (i + step) % N_LON) for i in range(N_LON)])  15.5 us
    unnamed x32, local copies, waits for them, and re-layouts  13.6 us
    pallas_call x4, Pallas kernels, pack(): pl.pallas_call(pack_body if edges is None else pack_tall_body, grid=(head...  5.04 us
  transfers between devices with their start and end apart: 28, of which 10 were waited for; matrix products, arithmetic and copies ran while one was open for 9% of the time, Pallas kernels for 19%

profile of v1, /device:TPU:1, one launch (start us, length us, event | category | flops | bytes accessed | tf_op | source)
XLA Modules:
  0.0 223.5 jit_solution(15156511709681563076)
XLA Ops:
  0.8 1.5 collective-permute-start.4
  2.3 2.8 %copy-done = bf16[2,1,32,16,3072]{4,3,2,1,0:T(8,128)(2,1)S(1)} copy-done((bf16[2,1,32,16,3072]{4,3,2,1,0:T(8,128)(2,1)S(1)}, bf16[2,1,32,16,3072]{4,3,2,1,0:T(8,128)(2,1)}, u32[]{:S(2)}) %copy-start) | copy-done | bytes 6291480
  5.0 2.2 shard_map.49
  7.2 1.4 collective-permute-start.24
  8.6 5.0 %collective-permute-start.25 = (bf16[2,32,8,1024]{3,2,1,0:T(8,128)(2,1)}, bf16[2,32,8,1024]{3,2,1,0:T(8,128)(2,1)}, u32[]{:S(2)}, u32[]{:S(2)}) collective-permute-start(bf16[2,32,8,1024]{3,2,1,0:T(8,128)(2,1)} %get-tuple-element.20), channel_id=1, source_target_pairs={{0,31},{1,0},{2,1},{3,2},{4,3},{5,4},{6,5},{7,6},{8,7},{9,8},{10,9... | collective-permute-start | bytes 3145736 | tf_op jit(solution)/shard_map/ppermute | solution.py:33
  13.8 2.8 %copy-done.1 = bf16[2,1,32,16,3072]{4,3,2,1,0:T(8,128)(2,1)S(1)} copy-done((bf16[2,1,32,16,3072]{4,3,2,1,0:T(8,128)(2,1)S(1)}, bf16[2,1,32,16,3072]{4,3,2,1,0:T(8,128)(2,1)}, u32[]{:S(2)}) %copy-start.1) | copy-done | bytes 6291480
  16.5 2.0 shard_map.47
  18.7 2.7 %collective-permute-start.6 = (bf16[1,8,3072]{2,1,0:T(8,128)(2,1)S(1)}, bf16[1,8,3072]{2,1,0:T(8,128)(2,1)S(1)}, u32[]{:S(2)}, u32[]{:S(2)}) collective-permute-start(bf16[1,8,3072]{2,1,0:T(8,128)(2,1)S(1)} %maximum_bitcast_fusion), channel_id=1, source_target_pairs={{0,3},{1,0},{2,1},{3,2},{4,7},{5,4},{6,5},{7,6},{8,11},{9,8},{10,9... | collective-permute-start | bytes 147464 | tf_op jit(solution)/shard_map/ppermute | solution.py:29
  22.0 14.1 %collective-permute-done.5 = bf16[1,8,3072]{2,1,0:T(8,128)(2,1)S(1)} collective-permute-done((bf16[1,8,3072]{2,1,0:T(8,128)(2,1)S(1)}, bf16[1,8,3072]{2,1,0:T(8,128)(2,1)S(1)}, u32[]{:S(2)}, u32[]{:S(2)}) %collective-permute-start.5) | collective-permute-done | bytes 49184 | tf_op jit(solution)/shard_map/ppermute | solution.py:29
  36.0 1.7 collective-permute-done.6
  37.8 2.1 collective-permute-start.8
  40.0 3.3 %collective-permute-start.9 = (bf16[4,8,3072]{2,1,0:T(8,128)(2,1)S(1)}, bf16[4,8,3072]{2,1,0:T(8,128)(2,1)S(1)}, u32[]{:S(2)}, u32[]{:S(2)}) collective-permute-start(bf16[4,8,3072]{2,1,0:T(8,128)(2,1)S(1)} %pad_maximum_fusion.6), channel_id=1, source_target_pairs={{0,64},{1,65},{2,66},{3,67},{4,68},{5,69},{6,70},{7,71},{8,72},{9,... | collective-permute-start | bytes 589832 | tf_op jit(solution)/shard_map/ppermute | solution.py:29
  45.1 16.5 %collective-permute-done.8 = bf16[4,8,3072]{2,1,0:T(8,128)(2,1)S(1)} collective-permute-done((bf16[4,8,3072]{2,1,0:T(8,128)(2,1)S(1)}, bf16[4,8,3072]{2,1,0:T(8,128)(2,1)S(1)}, u32[]{:S(2)}, u32[]{:S(2)}) %collective-permute-start.8) | collective-permute-done | bytes 196640 | tf_op jit(solution)/shard_map/ppermute | solution.py:29
  61.7 3.3 %collective-permute-start.10 = (bf16[4,8,3072]{2,1,0:T(8,128)(2,1)S(1)}, bf16[4,8,3072]{2,1,0:T(8,128)(2,1)S(1)}, u32[]{:S(2)}, u32[]{:S(2)}) collective-permute-start(bf16[4,8,3072]{2,1,0:T(8,128)(2,1)S(1)} %pad_maximum_fusion.6), channel_id=1, source_target_pairs={{0,68},{1,69},{2,70},{3,71},{4,64},{5,65},{6,66},{7,67},{8,76},{9,... | collective-permute-start | bytes 589832 | tf_op jit(solution)/shard_map/ppermute | solution.py:29
  65.6 3.3 %collective-permute-done.9 = bf16[4,8,3072]{2,1,0:T(8,128)(2,1)S(1)} collective-permute-done((bf16[4,8,3072]{2,1,0:T(8,128)(2,1)S(1)}, bf16[4,8,3072]{2,1,0:T(8,128)(2,1)S(1)}, u32[]{:S(2)}, u32[]{:S(2)}) %collective-permute-start.9) | collective-permute-done | bytes 196640 | tf_op jit(solution)/shard_map/ppermute | solution.py:29
  69.6 3.9 %collective-permute-done.10 = bf16[4,8,3072]{2,1,0:T(8,128)(2,1)S(1)} collective-permute-done((bf16[4,8,3072]{2,1,0:T(8,128)(2,1)S(1)}, bf16[4,8,3072]{2,1,0:T(8,128)(2,1)S(1)}, u32[]{:S(2)}, u32[]{:S(2)}) %collective-permute-start.10) | collective-permute-done | bytes 196640 | tf_op jit(solution)/shard_map/ppermute | solution.py:29
  74.3 2.7 %collective-permute-start.12 = (bf16[16,8,3072]{2,1,0:T(8,128)(2,1)S(1)}, bf16[16,8,3072]{2,1,0:T(8,128)(2,1)S(1)}, u32[]{:S(2)}, u32[]{:S(2)}) collective-permute-start(bf16[16,8,3072]{2,1,0:T(8,128)(2,1)S(1)} %get-tuple-element.35), channel_id=1, source_target_pairs={{0,24},{1,25},{2,26},{3,27},{4,28},{5,29},{6,30},{7,31},{8,0},{9,1... | collective-permute-start | bytes 2359304 | tf_op jit(solution)/shard_map/ppermute | solution.py:29
  76.9 4.1 %slice_bitcast_fusion = (bf16[2,8,16,3072]{3,2,1,0:T(8,128)(2,1)}, bf16[2,8,16,3072]{3,2,1,0:T(8,128)(2,1)}) fusion(bf16[2,1,32,16,3072]{4,3,2,0,1:T(8,128)(2,1)} %bitcast.41), kind=kLoop, calls=%fused_computation | loop fusion | bytes 6291456 | tf_op jit(solution)/shard_map/squeeze | solution.py:223
  81.0 12.8 %collective-permute-done.11 = bf16[16,8,3072]{2,1,0:T(8,128)(2,1)S(1)} collective-permute-done((bf16[16,8,3072]{2,1,0:T(8,128)(2,1)S(1)}, bf16[16,8,3072]{2,1,0:T(8,128)(2,1)S(1)}, u32[]{:S(2)}, u32[]{:S(2)}) %collective-permute-start.11) | collective-permute-done | bytes 786464 | tf_op jit(solution)/shard_map/ppermute | solution.py:29
  94.0 2.7 %collective-permute-start.14 = (bf16[8,8,3072]{2,1,0:T(8,128)(2,1)S(1)}, bf16[8,8,3072]{2,1,0:T(8,128)(2,1)S(1)}, u32[]{:S(2)}, u32[]{:S(2)}) collective-permute-start(bf16[8,8,3072]{2,1,0:T(8,128)(2,1)S(1)} %slice.67), channel_id=1, source_target_pairs={{0,24},{1,25},{2,26},{3,27},{4,28},{5,29},{6,30},{7,31},{8,0},{9,1... | collective-permute-start | bytes 1179656 | tf_op jit(solution)/shard_map/ppermute | solution.py:29
  96.7 1.0 constant_dynamic-update-slice_fusion.10
  97.7 0.9 constant_dynamic-update-slice_fusion.9
  98.7 5.6 %collective-permute-done.13 = bf16[8,8,3072]{2,1,0:T(8,128)(2,1)S(1)} collective-permute-done((bf16[8,8,3072]{2,1,0:T(8,128)(2,1)S(1)}, bf16[8,8,3072]{2,1,0:T(8,128)(2,1)S(1)}, u32[]{:S(2)}, u32[]{:S(2)}) %collective-permute-start.13) | collective-permute-done | bytes 393248 | tf_op jit(solution)/shard_map/ppermute | solution.py:29
  105.8 2.5 %collective-permute-start.15 = (bf16[64,8,3072]{2,1,0:T(8,128)(2,1)}, bf16[64,8,3072]{2,1,0:T(8,128)(2,1)}, u32[]{:S(2)}, u32[]{:S(2)}) collective-permute-start(bf16[64,8,3072]{2,1,0:T(8,128)(2,1)} %constant_dynamic-update-slice_fusion.7.refs_9_.refs_7_), channel_id=1, source_target_pairs={{0,32},{1,33},{2,34},{3,35},{4,36},{5,37},{6,38},{7,39},{8,40},{9,... | collective-permute-start | bytes 9437192 | tf_op jit(solution)/shard_map/ppermute | solution.py:29
  109.1 1.0 copy-done.5
  110.1 1.0 copy-done.6
  111.5 1.8 collective-permute-start.20
  113.3 1.0 slice_bitcast_fusion.11
  114.4 6.8 %collective-permute-done.17.refs_4_ = bf16[2,32,8,768]{3,2,1,0:T(8,128)(2,1)} collective-permute-done((bf16[2,32,8,768]{3,2,1,0:T(8,128)(2,1)}, bf16[2,32,8,768]{3,2,1,0:T(8,128)(2,1)}, u32[]{:S(2)}, u32[]{:S(2)}) %collective-permute-start.17) | collective-permute-done | bytes 786464 | tf_op jit(solution)/shard_map/ppermute | solution.py:33
  121.1 5.9 %collective-permute-start.21 = (bf16[2,32,8,1024]{3,2,1,0:T(8,128)(2,1)}, bf16[2,32,8,1024]{3,2,1,0:T(8,128)(2,1)S(1)}, u32[]{:S(2)}, u32[]{:S(2)}) collective-permute-start(bf16[2,32,8,1024]{3,2,1,0:T(8,128)(2,1)} %copy-done.5), channel_id=1, source_target_pairs={{0,31},{1,0},{2,1},{3,2},{4,3},{5,4},{6,5},{7,6},{8,7},{9,8},{10,9... | collective-permute-start | bytes 3145736 | tf_op jit(solution)/shard_map/ppermute | solution.py:33
  127.1 1.0 slice_bitcast_fusion.10
  128.2 3.7 %collective-permute-start = (bf16[2,8,16,3072]{3,2,1,0:T(8,128)(2,1)}, bf16[2,8,16,3072]{3,2,1,0:T(8,128)(2,1)S(1)}, u32[]{:S(2)}, u32[]{:S(2)}) collective-permute-start(bf16[2,8,16,3072]{3,2,1,0:T(8,128)(2,1)} %get-tuple-element.22), channel_id=1, source_target_pairs={{0,32},{32,64},{64,96},{1,33},{33,65},{65,97},{2,34},{34,66},{66,9... | collective-permute-start | bytes 4718600 | tf_op jit(solution)/shard_map/ppermute | solution.py:37
  131.9 2.2 %collective-permute-start.1 = (bf16[2,8,16,3072]{3,2,1,0:T(8,128)(2,1)}, bf16[2,8,16,3072]{3,2,1,0:T(8,128)(2,1)S(1)}, u32[]{:S(2)}, u32[]{:S(2)}) collective-permute-start(bf16[2,8,16,3072]{3,2,1,0:T(8,128)(2,1)} %get-tuple-element.21), channel_id=1, source_target_pairs={{32,0},{64,32},{96,64},{33,1},{65,33},{97,65},{34,2},{66,34},{98,6... | collective-permute-start | bytes 4718600 | tf_op jit(solution)/shard_map/ppermute | solution.py:37
  135.0 1.6 slice_bitcast_fusion.2
  136.8 4.0 %collective-permute-done.20.refs_3_ = bf16[2,32,8,1024]{3,2,1,0:T(8,128)(2,1)S(1)} collective-permute-done((bf16[2,32,8,1024]{3,2,1,0:T(8,128)(2,1)}, bf16[2,32,8,1024]{3,2,1,0:T(8,128)(2,1)S(1)}, u32[]{:S(2)}, u32[]{:S(2)}) %collective-permute-start.20) | collective-permute-done | bytes 1048608 | tf_op jit(solution)/shard_map/ppermute | solution.py:33
  140.8 1.9 collective-permute-start.26
  142.7 4.7 %collective-permute-done.21.refs_4_ = bf16[2,32,8,1024]{3,2,1,0:T(8,128)(2,1)S(1)} collective-permute-done((bf16[2,32,8,1024]{3,2,1,0:T(8,128)(2,1)}, bf16[2,32,8,1024]{3,2,1,0:T(8,128)(2,1)S(1)}, u32[]{:S(2)}, u32[]{:S(2)}) %collective-permute-start.21) | collective-permute-done | bytes 1048608 | tf_op jit(solution)/shard_map/ppermute | solution.py:33
  147.4 5.2 %collective-permute-start.27 = (bf16[2,2,8,8,1024]{4,3,2,1,0:T(8,128)(2,1)S(1)}, bf16[2,2,8,8,1024]{4,3,2,1,0:T(8,128)(2,1)S(1)}, u32[]{:S(2)}, u32[]{:S(2)}) collective-permute-start(bf16[2,2,8,8,1024]{4,3,2,1,0:T(8,128)(2,1)S(1)} %pad_maximum_fusion.3), channel_id=1, source_target_pairs={{32,0},{64,32},{96,64},{33,1},{65,33},{97,65},{34,2},{66,34},{98,6... | collective-permute-start | bytes 1572872 | tf_op jit(solution)/shard_map/ppermute | solution.py:37
  153.6 0.9 pad_maximum_fusion.1
  154.5 5.2 %collective-permute-start.18 = (bf16[2,2,8,8,768]{4,3,2,1,0:T(8,128)(2,1)S(1)}, bf16[2,2,8,8,768]{4,3,2,1,0:T(8,128)(2,1)S(1)}, u32[]{:S(2)}, u32[]{:S(2)}) collective-permute-start(bf16[2,2,8,8,768]{4,3,2,1,0:T(8,128)(2,1)S(1)} %pad_maximum_fusion.4), channel_id=1, source_target_pairs={{0,32},{32,64},{64,96},{1,33},{33,65},{65,97},{2,34},{34,66},{66,9... | collective-permute-start | bytes 1179656 | tf_op jit(solution)/shard_map/ppermute | solution.py:37
  159.6 1.9 collective-permute-start.19
  161.7 5.1 %collective-permute-start.22 = (bf16[2,2,8,8,1024]{4,3,2,1,0:T(8,128)(2,1)}, bf16[2,2,8,8,1024]{4,3,2,1,0:T(8,128)(2,1)S(1)}, u32[]{:S(2)}, u32[]{:S(2)}) collective-permute-start(bf16[2,2,8,8,1024]{4,3,2,1,0:T(8,128)(2,1)} %pad_maximum_fusion), channel_id=1, source_target_pairs={{0,32},{32,64},{64,96},{1,33},{33,65},{65,97},{2,34},{34,66},{66,9... | collective-permute-start | bytes 1572872 | tf_op jit(solution)/shard_map/ppermute | solution.py:37
  166.9 1.9 collective-permute-start.23
  169.1 13.4 %shard_map.50.refs_13_ = bf16[1,32,16,3072]{3,2,1,0:T(8,128)(2,1)} custom-call(s32[1]{0:T(128)} %bitcast.refs_0_, bf16[1,32,16,3072]{3,2,1,0:T(8,128)(2,1)S(1)} %copy-done.2, bf16[2,1,32,16,3072]{4,3,2,1,0:T(8,128)(2,1)} %refs_2_.7, bf16[2,32,8,1024]{3,2,1,0:T(8,128)(2,1)S(1)} %collective-permute-done.24.refs_3_, ...), custom_call_target="tpu_custom_call" | custom-call | flops 12000000000 | bytes 8388608 | tf_op jit(solution)/shard_map/pallas_call | solution.py:181
  182.5 12.3 %collective-permute-start.3 = (bf16[2,48,8,256]{3,2,1,0:T(8,128)(2,1)S(1)}, bf16[2,48,8,256]{3,2,1,0:T(8,128)(2,1)S(1)}, u32[]{:S(2)}, u32[]{:S(2)}) collective-permute-start(bf16[2,48,8,256]{3,2,1,0:T(8,128)(2,1)S(1)} %get-tuple-element.14), channel_id=1, source_target_pairs={{0,31},{1,0},{2,1},{3,2},{4,3},{5,4},{6,5},{7,6},{8,7},{9,8},{10,9... | collective-permute-start | bytes 1179656 | tf_op jit(solution)/shard_map/ppermute | solution.py:33
  194.8 13.3 %shard_map.51.refs_13_ = bf16[1,32,16,3072]{3,2,1,0:T(8,128)(2,1)} custom-call(s32[1]{0:T(128)} %bitcast.refs_0_, bf16[1,32,16,3072]{3,2,1,0:T(8,128)(2,1)S(1)} %copy-done.2, bf16[2,1,32,16,3072]{4,3,2,1,0:T(8,128)(2,1)} %refs_2_.7, bf16[2,32,8,1024]{3,2,1,0:T(8,128)(2,1)S(1)} %collective-permute-done.20.refs_3_, ...), custom_call_target="tpu_custom_call", output_to_operand_aliasing={{}: (13, {})} | custom-call | flops 12000000000 | bytes 8388608 | tf_op jit(solution)/shard_map/pallas_call | solution.py:181
  208.1 10.7 %shard_map.52.refs_11_ = bf16[1,32,16,3072]{3,2,1,0:T(8,128)(2,1)} custom-call(s32[1]{0:T(128)} %bitcast.refs_0_, bf16[1,32,16,3072]{3,2,1,0:T(8,128)(2,1)S(1)} %copy-done.2, bf16[2,1,32,16,3072]{4,3,2,1,0:T(8,128)(2,1)} %refs_2_.7, bf16[2,32,8,768]{3,2,1,0:T(8,128)(2,1)} %collective-permute-done.16.refs_3_, ...), custom_call_target="tpu_custom_call", output_to_operand_aliasing={{}: (13, {})} | custom-call | flops 8999999488 | bytes 6291456 | tf_op jit(solution)/shard_map/pallas_call | solution.py:181
  218.8 4.7 %shard_map.53 = bf16[1,32,16,3072]{3,2,1,0:T(8,128)(2,1)} custom-call(s32[1]{0:T(128)} %bitcast.refs_0_, bf16[1,32,16,3072]{3,2,1,0:T(8,128)(2,1)S(1)} %copy-done.3, bf16[2,1,32,16,3072]{4,3,2,1,0:T(8,128)(2,1)} %refs_2_.7, bf16[2,48,8,256]{3,2,1,0:T(8,128)(2,1)S(1)} %collective-permute-done.2.refs_3_, ...), custom_call_target="tpu_custom_call", output_to_operand_aliasing={{}: (11, {})} | custom-call | flops 3000000000 | bytes 2097152 | tf_op jit(solution)/shard_map/pallas_call | solution.py:181
  (83 shorter events, 10.8 us)
Async XLA Ops:
  0.8 17.7 %collective-permute-start.4 = (bf16[4,3072]{1,0:T(4,128)(2,1)S(1)}, bf16[4,3072]{1,0:T(4,128)(2,1)S(1)}, u32[]{:S(2)}, u32[]{:S(2)}) collective-permute-start(bf16[4,3072]{1,0:T(4,128)(2,1)S(1)} %dynamic-slice_bitcast_fusion), channel_id=1, source_target_pairs={{0,32},{1,33},{2,34},{3,35},{4,36},{5,37},{6,38},{7,39},{8,40},{9,... | collective-permute-start | bytes 73736 | tf_op jit(solution)/shard_map/ppermute | solution.py:29
  2.3 2.8 %copy-start = (bf16[2,1,32,16,3072]{4,3,2,1,0:T(8,128)(2,1)S(1)}, bf16[2,1,32,16,3072]{4,3,2,1,0:T(8,128)(2,1)}, u32[]{:S(2)}) copy-start(bf16[2,1,32,16,3072]{4,3,2,1,0:T(8,128)(2,1)} %refs_2_.7) | copy-start | bytes 18874372
  7.2 120.9 %collective-permute-start.24 = (bf16[2,32,8,1024]{3,2,1,0:T(8,128)(2,1)}, bf16[2,32,8,1024]{3,2,1,0:T(8,128)(2,1)S(1)}, u32[]{:S(2)}, u32[]{:S(2)}) collective-permute-start(bf16[2,32,8,1024]{3,2,1,0:T(8,128)(2,1)} %get-tuple-element.19), channel_id=1, source_target_pairs={{0,1},{1,2},{2,3},{3,4},{4,5},{5,6},{6,7},{7,8},{8,9},{9,10},{10,1... | collective-permute-start | bytes 3145736 | tf_op jit(solution)/shard_map/ppermute | solution.py:33
  8.6 123.3 %collective-permute-start.25 = (bf16[2,32,8,1024]{3,2,1,0:T(8,128)(2,1)}, bf16[2,32,8,1024]{3,2,1,0:T(8,128)(2,1)}, u32[]{:S(2)}, u32[]{:S(2)}) collective-permute-start(bf16[2,32,8,1024]{3,2,1,0:T(8,128)(2,1)} %get-tuple-element.20), channel_id=1, source_target_pairs={{0,31},{1,0},{2,1},{3,2},{4,3},{5,4},{6,5},{7,6},{8,7},{9,8},{10,9... | collective-permute-start | bytes 3145736 | tf_op jit(solution)/shard_map/ppermute | solution.py:33
  13.7 2.8 %copy-start.1 = (bf16[2,1,32,16,3072]{4,3,2,1,0:T(8,128)(2,1)S(1)}, bf16[2,1,32,16,3072]{4,3,2,1,0:T(8,128)(2,1)}, u32[]{:S(2)}) copy-start(bf16[2,1,32,16,3072]{4,3,2,1,0:T(8,128)(2,1)} %refs_2_.7) | copy-start | bytes 18874372
  16.5 2.0 copy-start.7
  18.6 17.5 %collective-permute-start.5 = (bf16[1,8,3072]{2,1,0:T(8,128)(2,1)S(1)}, bf16[1,8,3072]{2,1,0:T(8,128)(2,1)S(1)}, u32[]{:S(2)}, u32[]{:S(2)}) collective-permute-start(bf16[1,8,3072]{2,1,0:T(8,128)(2,1)S(1)} %maximum_bitcast_fusion), channel_id=1, source_target_pairs={{0,1},{1,2},{2,3},{3,0},{4,5},{5,6},{6,7},{7,4},{8,9},{9,10},{10,1... | collective-permute-start | bytes 147464 | tf_op jit(solution)/shard_map/ppermute | solution.py:29
  18.7 19.1 %collective-permute-start.6 = (bf16[1,8,3072]{2,1,0:T(8,128)(2,1)S(1)}, bf16[1,8,3072]{2,1,0:T(8,128)(2,1)S(1)}, u32[]{:S(2)}, u32[]{:S(2)}) collective-permute-start(bf16[1,8,3072]{2,1,0:T(8,128)(2,1)S(1)} %maximum_bitcast_fusion), channel_id=1, source_target_pairs={{0,3},{1,0},{2,1},{3,2},{4,7},{5,4},{6,5},{7,6},{8,11},{9,8},{10,9... | collective-permute-start | bytes 147464 | tf_op jit(solution)/shard_map/ppermute | solution.py:29
  21.3 16.5 %collective-permute-start.7 = (bf16[1,8,3072]{2,1,0:T(8,128)(2,1)S(1)}, bf16[1,8,3072]{2,1,0:T(8,128)(2,1)S(1)}, u32[]{:S(2)}, u32[]{:S(2)}) collective-permute-start(bf16[1,8,3072]{2,1,0:T(8,128)(2,1)S(1)} %maximum_bitcast_fusion), channel_id=1, source_target_pairs={{0,2},{1,3},{2,0},{3,1},{4,6},{5,7},{6,4},{7,5},{8,10},{9,11},{10,... | collective-permute-start | bytes 147464 | tf_op jit(solution)/shard_map/ppermute | solution.py:29
  36.0 75.4 %collective-permute-start.16 = (bf16[2,32,8,768]{3,2,1,0:T(8,128)(2,1)}, bf16[2,32,8,768]{3,2,1,0:T(8,128)(2,1)}, u32[]{:S(2)}, u32[]{:S(2)}) collective-permute-start(bf16[2,32,8,768]{3,2,1,0:T(8,128)(2,1)} %get-tuple-element.15), channel_id=1, source_target_pairs={{0,1},{1,2},{2,3},{3,4},{4,5},{5,6},{6,7},{7,8},{8,9},{9,10},{10,1... | collective-permute-start | bytes 2359304 | tf_op jit(solution)/shard_map/ppermute | solution.py:33
  37.8 23.8 %collective-permute-start.8 = (bf16[4,8,3072]{2,1,0:T(8,128)(2,1)S(1)}, bf16[4,8,3072]{2,1,0:T(8,128)(2,1)S(1)}, u32[]{:S(2)}, u32[]{:S(2)}) collective-permute-start(bf16[4,8,3072]{2,1,0:T(8,128)(2,1)S(1)} %pad_maximum_fusion.6), channel_id=1, source_target_pairs={{0,4},{1,5},{2,6},{3,7},{4,0},{5,1},{6,2},{7,3},{8,12},{9,13},{10,... | collective-permute-start | bytes 589832 | tf_op jit(solution)/shard_map/ppermute | solution.py:29
  40.0 28.9 %collective-permute-start.9 = (bf16[4,8,3072]{2,1,0:T(8,128)(2,1)S(1)}, bf16[4,8,3072]{2,1,0:T(8,128)(2,1)S(1)}, u32[]{:S(2)}, u32[]{:S(2)}) collective-permute-start(bf16[4,8,3072]{2,1,0:T(8,128)(2,1)S(1)} %pad_maximum_fusion.6), channel_id=1, source_target_pairs={{0,64},{1,65},{2,66},{3,67},{4,68},{5,69},{6,70},{7,71},{8,72},{9,... | collective-permute-start | bytes 589832 | tf_op jit(solution)/shard_map/ppermute | solution.py:29
  61.7 11.9 %collective-permute-start.10 = (bf16[4,8,3072]{2,1,0:T(8,128)(2,1)S(1)}, bf16[4,8,3072]{2,1,0:T(8,128)(2,1)S(1)}, u32[]{:S(2)}, u32[]{:S(2)}) collective-permute-start(bf16[4,8,3072]{2,1,0:T(8,128)(2,1)S(1)} %pad_maximum_fusion.6), channel_id=1, source_target_pairs={{0,68},{1,69},{2,70},{3,71},{4,64},{5,65},{6,66},{7,67},{8,76},{9,... | collective-permute-start | bytes 589832 | tf_op jit(solution)/shard_map/ppermute | solution.py:29
  73.5 34.8 %slice-start = ((s8[6291456]{0:T(1024)(128)(4,1)}), s8[4194304]{0:T(1024)(128)(4,1)S(1)}, s32[]{:S(2)}) async-start(s8[6291456]{0:T(1024)(128)(4,1)} %bitcast.42), calls=%async_computation | async-start | bytes 8388608
  74.2 19.6 %collective-permute-start.11 = (bf16[16,8,3072]{2,1,0:T(8,128)(2,1)S(1)}, bf16[16,8,3072]{2,1,0:T(8,128)(2,1)S(1)}, u32[]{:S(2)}, u32[]{:S(2)}) collective-permute-start(bf16[16,8,3072]{2,1,0:T(8,128)(2,1)S(1)} %get-tuple-element.35), channel_id=1, source_target_pairs={{0,8},{1,9},{2,10},{3,11},{4,12},{5,13},{6,14},{7,15},{8,16},{9,17... | collective-permute-start | bytes 2359304 | tf_op jit(solution)/shard_map/ppermute | solution.py:29
  74.3 19.7 %collective-permute-start.12 = (bf16[16,8,3072]{2,1,0:T(8,128)(2,1)S(1)}, bf16[16,8,3072]{2,1,0:T(8,128)(2,1)S(1)}, u32[]{:S(2)}, u32[]{:S(2)}) collective-permute-start(bf16[16,8,3072]{2,1,0:T(8,128)(2,1)S(1)} %get-tuple-element.35), channel_id=1, source_target_pairs={{0,24},{1,25},{2,26},{3,27},{4,28},{5,29},{6,30},{7,31},{8,0},{9,1... | collective-permute-start | bytes 2359304 | tf_op jit(solution)/shard_map/ppermute | solution.py:29
  76.9 31.4 %slice-start.1 = ((s8[6291456]{0:T(1024)(128)(4,1)}), s8[2097152]{0:T(1024)(128)(4,1)S(1)}, s32[]{:S(2)}) async-start(s8[6291456]{0:T(1024)(128)(4,1)} %bitcast.42), calls=%async_computation.1 | async-start | bytes 4194304
  93.9 10.3 %collective-permute-start.13 = (bf16[8,8,3072]{2,1,0:T(8,128)(2,1)S(1)}, bf16[8,8,3072]{2,1,0:T(8,128)(2,1)S(1)}, u32[]{:S(2)}, u32[]{:S(2)}) collective-permute-start(bf16[8,8,3072]{2,1,0:T(8,128)(2,1)S(1)} %slice.66), channel_id=1, source_target_pairs={{0,8},{1,9},{2,10},{3,11},{4,12},{5,13},{6,14},{7,15},{8,16},{9,17... | collective-permute-start | bytes 1179656 | tf_op jit(solution)/shard_map/ppermute | solution.py:29
  94.0 11.0 %collective-permute-start.14 = (bf16[8,8,3072]{2,1,0:T(8,128)(2,1)S(1)}, bf16[8,8,3072]{2,1,0:T(8,128)(2,1)S(1)}, u32[]{:S(2)}, u32[]{:S(2)}) collective-permute-start(bf16[8,8,3072]{2,1,0:T(8,128)(2,1)S(1)} %slice.67), channel_id=1, source_target_pairs={{0,24},{1,25},{2,26},{3,27},{4,28},{5,29},{6,30},{7,31},{8,0},{9,1... | collective-permute-start | bytes 1179656 | tf_op jit(solution)/shard_map/ppermute | solution.py:29
  104.2 16.9 %collective-permute-start.17 = (bf16[2,32,8,768]{3,2,1,0:T(8,128)(2,1)}, bf16[2,32,8,768]{3,2,1,0:T(8,128)(2,1)}, u32[]{:S(2)}, u32[]{:S(2)}) collective-permute-start(bf16[2,32,8,768]{3,2,1,0:T(8,128)(2,1)} %get-tuple-element.16), channel_id=1, source_target_pairs={{0,31},{1,0},{2,1},{3,2},{4,3},{5,4},{6,5},{7,6},{8,7},{9,8},{10,9... | collective-permute-start | bytes 2359304 | tf_op jit(solution)/shard_map/ppermute | solution.py:33
  105.8 63.0 %collective-permute-start.15 = (bf16[64,8,3072]{2,1,0:T(8,128)(2,1)}, bf16[64,8,3072]{2,1,0:T(8,128)(2,1)}, u32[]{:S(2)}, u32[]{:S(2)}) collective-permute-start(bf16[64,8,3072]{2,1,0:T(8,128)(2,1)} %constant_dynamic-update-slice_fusion.7.refs_9_.refs_7_), channel_id=1, source_target_pairs={{0,32},{1,33},{2,34},{3,35},{4,36},{5,37},{6,38},{7,39},{8,40},{9,... | collective-permute-start | bytes 9437192 | tf_op jit(solution)/shard_map/ppermute | solution.py:29
  108.3 53.2 %slice-start.2 = ((s8[6291456]{0:T(1024)(128)(4,1)}), s8[2097152]{0:T(1024)(128)(4,1)S(1)}, s32[]{:S(2)}) async-start(s8[6291456]{0:T(1024)(128)(4,1)} %bitcast.44), calls=%async_computation.2 | async-start | bytes 4194304
  109.1 1.0 copy-start.5
  110.1 1.0 copy-start.6
  111.5 29.3 %collective-permute-start.20 = (bf16[2,32,8,1024]{3,2,1,0:T(8,128)(2,1)}, bf16[2,32,8,1024]{3,2,1,0:T(8,128)(2,1)S(1)}, u32[]{:S(2)}, u32[]{:S(2)}) collective-permute-start(bf16[2,32,8,1024]{3,2,1,0:T(8,128)(2,1)} %copy-done.6), channel_id=1, source_target_pairs={{0,1},{1,2},{2,3},{3,4},{4,5},{5,6},{6,7},{7,8},{8,9},{9,10},{10,1... | collective-permute-start | bytes 3145736 | tf_op jit(solution)/shard_map/ppermute | solution.py:33
  121.1 26.3 %collective-permute-start.21 = (bf16[2,32,8,1024]{3,2,1,0:T(8,128)(2,1)}, bf16[2,32,8,1024]{3,2,1,0:T(8,128)(2,1)S(1)}, u32[]{:S(2)}, u32[]{:S(2)}) collective-permute-start(bf16[2,32,8,1024]{3,2,1,0:T(8,128)(2,1)} %copy-done.5), channel_id=1, source_target_pairs={{0,31},{1,0},{2,1},{3,2},{4,3},{5,4},{6,5},{7,6},{8,7},{9,8},{10,9... | collective-permute-start | bytes 3145736 | tf_op jit(solution)/shard_map/ppermute | solution.py:33
  128.2 26.3 %collective-permute-start = (bf16[2,8,16,3072]{3,2,1,0:T(8,128)(2,1)}, bf16[2,8,16,3072]{3,2,1,0:T(8,128)(2,1)S(1)}, u32[]{:S(2)}, u32[]{:S(2)}) collective-permute-start(bf16[2,8,16,3072]{3,2,1,0:T(8,128)(2,1)} %get-tuple-element.22), channel_id=1, source_target_pairs={{0,32},{32,64},{64,96},{1,33},{33,65},{65,97},{2,34},{34,66},{66,9... | collective-permute-start | bytes 4718600 | tf_op jit(solution)/shard_map/ppermute | solution.py:37
  131.9 27.7 %collective-permute-start.1 = (bf16[2,8,16,3072]{3,2,1,0:T(8,128)(2,1)}, bf16[2,8,16,3072]{3,2,1,0:T(8,128)(2,1)S(1)}, u32[]{:S(2)}, u32[]{:S(2)}) collective-permute-start(bf16[2,8,16,3072]{3,2,1,0:T(8,128)(2,1)} %get-tuple-element.21), channel_id=1, source_target_pairs={{32,0},{64,32},{96,64},{33,1},{65,33},{97,65},{34,2},{66,34},{98,6... | collective-permute-start | bytes 4718600 | tf_op jit(solution)/shard_map/ppermute | solution.py:37
  134.2 27.4 %slice-start.3 = ((s8[6291456]{0:T(1024)(128)(4,1)}), s8[4194304]{0:T(1024)(128)(4,1)S(1)}, s32[]{:S(2)}) async-start(s8[6291456]{0:T(1024)(128)(4,1)} %bitcast.44), calls=%async_computation.3 | async-start | bytes 8388608
  140.8 20.9 %collective-permute-start.26 = (bf16[2,2,8,8,1024]{4,3,2,1,0:T(8,128)(2,1)S(1)}, bf16[2,2,8,8,1024]{4,3,2,1,0:T(8,128)(2,1)S(1)}, u32[]{:S(2)}, u32[]{:S(2)}) collective-permute-start(bf16[2,2,8,8,1024]{4,3,2,1,0:T(8,128)(2,1)S(1)} %pad_maximum_fusion.2), channel_id=1, source_target_pairs={{0,32},{32,64},{64,96},{1,33},{33,65},{65,97},{2,34},{34,66},{66,9... | collective-permute-start | bytes 1572872 | tf_op jit(solution)/shard_map/ppermute | solution.py:37
  147.4 19.4 %collective-permute-start.27 = (bf16[2,2,8,8,1024]{4,3,2,1,0:T(8,128)(2,1)S(1)}, bf16[2,2,8,8,1024]{4,3,2,1,0:T(8,128)(2,1)S(1)}, u32[]{:S(2)}, u32[]{:S(2)}) collective-permute-start(bf16[2,2,8,8,1024]{4,3,2,1,0:T(8,128)(2,1)S(1)} %pad_maximum_fusion.3), channel_id=1, source_target_pairs={{32,0},{64,32},{96,64},{33,1},{65,33},{97,65},{34,2},{66,34},{98,6... | collective-permute-start | bytes 1572872 | tf_op jit(solution)/shard_map/ppermute | solution.py:37
  154.4 14.6 %copy-start.2 = (bf16[1,32,16,3072]{3,2,1,0:T(8,128)(2,1)S(1)}, bf16[1,32,16,3072]{3,2,1,0:T(8,128)(2,1)}, u32[]{:S(2)}) copy-start(bf16[1,32,16,3072]{3,2,1,0:T(8,128)(2,1)} %refs_1_.7) | copy-start | bytes 9437188
  154.4 14.6 %copy-start.4 = (bf16[512,128]{1,0:T(8,128)(2,1)S(1)}, bf16[512,128]{1,0:T(8,128)(2,1)}, u32[]{:S(2)}) copy-start(bf16[512,128]{1,0:T(8,128)(2,1)} %constant.58.clone.refs_11_.refs_9_) | copy-start | bytes 393220
  154.5 53.7 %collective-permute-start.18 = (bf16[2,2,8,8,768]{4,3,2,1,0:T(8,128)(2,1)S(1)}, bf16[2,2,8,8,768]{4,3,2,1,0:T(8,128)(2,1)S(1)}, u32[]{:S(2)}, u32[]{:S(2)}) collective-permute-start(bf16[2,2,8,8,768]{4,3,2,1,0:T(8,128)(2,1)S(1)} %pad_maximum_fusion.4), channel_id=1, source_target_pairs={{0,32},{32,64},{64,96},{1,33},{33,65},{65,97},{2,34},{34,66},{66,9... | collective-permute-start | bytes 1179656 | tf_op jit(solution)/shard_map/ppermute | solution.py:37
  159.6 48.5 %collective-permute-start.19 = (bf16[2,2,8,8,768]{4,3,2,1,0:T(8,128)(2,1)}, bf16[2,2,8,8,768]{4,3,2,1,0:T(8,128)(2,1)S(1)}, u32[]{:S(2)}, u32[]{:S(2)}) collective-permute-start(bf16[2,2,8,8,768]{4,3,2,1,0:T(8,128)(2,1)} %pad_maximum_fusion.5), channel_id=1, source_target_pairs={{32,0},{64,32},{96,64},{33,1},{65,33},{97,65},{34,2},{66,34},{98,6... | collective-permute-start | bytes 1179656 | tf_op jit(solution)/shard_map/ppermute | solution.py:37
  161.7 20.8 %collective-permute-start.22 = (bf16[2,2,8,8,1024]{4,3,2,1,0:T(8,128)(2,1)}, bf16[2,2,8,8,1024]{4,3,2,1,0:T(8,128)(2,1)S(1)}, u32[]{:S(2)}, u32[]{:S(2)}) collective-permute-start(bf16[2,2,8,8,1024]{4,3,2,1,0:T(8,128)(2,1)} %pad_maximum_fusion), channel_id=1, source_target_pairs={{0,32},{32,64},{64,96},{1,33},{33,65},{65,97},{2,34},{34,66},{66,9... | collective-permute-start | bytes 1572872 | tf_op jit(solution)/shard_map/ppermute | solution.py:37
  166.9 27.9 %collective-permute-start.23 = (bf16[2,2,8,8,1024]{4,3,2,1,0:T(8,128)(2,1)}, bf16[2,2,8,8,1024]{4,3,2,1,0:T(8,128)(2,1)S(1)}, u32[]{:S(2)}, u32[]{:S(2)}) collective-permute-start(bf16[2,2,8,8,1024]{4,3,2,1,0:T(8,128)(2,1)} %pad_maximum_fusion.1), channel_id=1, source_target_pairs={{32,0},{64,32},{96,64},{33,1},{65,33},{97,65},{34,2},{66,34},{98,6... | collective-permute-start | bytes 1572872 | tf_op jit(solution)/shard_map/ppermute | solution.py:37
  168.8 50.0 %collective-permute-start.2 = (bf16[2,48,8,256]{3,2,1,0:T(8,128)(2,1)S(1)}, bf16[2,48,8,256]{3,2,1,0:T(8,128)(2,1)S(1)}, u32[]{:S(2)}, u32[]{:S(2)}) collective-permute-start(bf16[2,48,8,256]{3,2,1,0:T(8,128)(2,1)S(1)} %get-tuple-element.13), channel_id=1, source_target_pairs={{0,1},{1,2},{2,3},{3,4},{4,5},{5,6},{6,7},{7,8},{8,9},{9,10},{10,1... | collective-permute-start | bytes 1179656 | tf_op jit(solution)/shard_map/ppermute | solution.py:33
  182.5 36.3 %collective-permute-start.3 = (bf16[2,48,8,256]{3,2,1,0:T(8,128)(2,1)S(1)}, bf16[2,48,8,256]{3,2,1,0:T(8,128)(2,1)S(1)}, u32[]{:S(2)}, u32[]{:S(2)}) collective-permute-start(bf16[2,48,8,256]{3,2,1,0:T(8,128)(2,1)S(1)} %get-tuple-element.14), channel_id=1, source_target_pairs={{0,31},{1,0},{2,1},{3,2},{4,3},{5,4},{6,5},{7,6},{8,7},{9,8},{10,9... | collective-permute-start | bytes 1179656 | tf_op jit(solution)/shard_map/ppermute | solution.py:33
  208.1 10.7 %copy-start.3 = (bf16[1,32,16,3072]{3,2,1,0:T(8,128)(2,1)S(1)}, bf16[1,32,16,3072]{3,2,1,0:T(8,128)(2,1)}, u32[]{:S(2)}) copy-start(bf16[1,32,16,3072]{3,2,1,0:T(8,128)(2,1)} %refs_1_.7) | copy-start | bytes 9437188

commit v2 on v1

v2 whole, which is shorter than its diff:
```python
import functools
import math

import jax
import jax.numpy as jnp
import numpy as np
from jax import lax
from jax.experimental import pallas as pl
from jax.experimental.pallas import tpu as pltpu
from jax.sharding import PartitionSpec as P

HD = 128
RADIUS = 8
NEG = -1e30
ZH, CORE, NX, ZL, NY = 2, 2, 4, 2, 4
N_LAT, N_LON = ZH * CORE, NX * ZL * NY
CHUNKS = (4, 8, 8, 4)
PER_STEP = 4
WIDE = PER_STEP * HD
BLOCK = 16
VMEM_LIMIT = 60 << 20
PIECES = 8


def send_where(x, use, zh=0, core=0, lon=0):
    pairs = []
    for i in range(N_LAT * N_LON):
        lat, at = divmod(i, N_LON)
        a, b = divmod(lat, CORE)
        if use(a, b):
            lat = (a + zh) % ZH * CORE + (b + core) % CORE
            pairs.append((i, lat * N_LON + (at + lon) % N_LON))
    return lax.ppermute(x, ("lat", "lon"), pairs)


def send(x, zh=0, core=0, x_=0, zl=0, y=0):
    pairs = []
    for i in range(N_LAT * N_LON):
        c = list(np.unravel_index(i, (ZH, CORE, NX, ZL, NY)))
        t = [(a + b) % n for a, b, n in zip(c, (zh, core, x_, zl, y), (ZH, CORE, NX, ZL, NY))]
        pairs.append((i, int(np.ravel_multi_index(t, (ZH, CORE, NX, ZL, NY)))))
    return lax.ppermute(x, ("lat", "lon"), pairs)


def send_lon(x, step):
    return lax.ppermute(x, "lon", [(i, (i + step) % N_LON) for i in range(N_LON)])


def glue(body, out_shapes, args, deps, specs=None, out_specs=None, grid=None):
    if specs is None:
        specs = [pl.BlockSpec(memory_space=pltpu.VMEM)] * len(args)
        out_specs = [pl.BlockSpec(memory_space=pltpu.VMEM)] * len(out_shapes)
    count = len(args)

    def kernel(*refs):
        body(*refs[:count], *refs[count + len(deps) :])

    return pl.pallas_call(
        kernel,
        grid=grid or (),
        in_specs=list(specs) + [pl.BlockSpec(memory_space=pl.ANY)] * len(deps),
        out_specs=out_specs,
        out_shape=[jax.ShapeDtypeStruct(shape, jnp.bfloat16) for shape in out_shapes],
        compiler_params=pltpu.CompilerParams(vmem_limit_bytes=VMEM_LIMIT),
        cost_estimate=pl.CostEstimate(flops=1000, bytes_accessed=1000, transcendentals=0),
    )(*args, *deps)


def pack_sides(own, head, heads, deps):
    wide = 4 * HD
    at = head * HD // wide

    def body(own_ref, r_ref, l_ref):
        r_ref[...] = own_ref[:, 0, :, RADIUS:]
        l_ref[...] = own_ref[:, 0, :, :RADIUS]

    specs = [pl.BlockSpec((2, 1, 32, 16, wide), lambda i: (0, 0, 0, 0, at + i))]
    out_specs = [pl.BlockSpec((2, 32, RADIUS, wide), lambda i: (0, 0, 0, i))] * 2
    shape = (2, 32, RADIUS, heads * HD)
    return glue(body, [shape] * 2, [own], deps, specs, out_specs, (heads * HD // wide,))


def carry(arrays, deps):
    def body(*refs):
        for src, dst in zip(refs[: len(arrays)], refs[len(arrays) :]):
            dst[...] = src[...]

    return glue(body, [x.shape for x in arrays], list(arrays), deps)


def pack_far_sides(far, deps):
    def body(far_ref, r_ref, l_ref):
        r_ref[...] = far_ref[:, :, RADIUS:]
        l_ref[...] = far_ref[:, :, :RADIUS]

    specs = [pl.BlockSpec((2, RADIUS, 16, 3072), lambda i: (0, 0, 0, i))]
    out_specs = [pl.BlockSpec((2, RADIUS, RADIUS, 3072), lambda i: (0, 0, 0, i))] * 2
    return glue(body, [(2, RADIUS, RADIUS, 3072)] * 2, [far], deps, specs, out_specs, (1,))


def pack_rows(flip, own, deps):
    def body(flip_ref, first_ref, last_ref, near_ref, far_ref):
        odd = flip_ref[0] == 1
        near_ref[...] = jnp.where(odd, first_ref[:, 0], last_ref[:, 0])
        far_ref[...] = jnp.where(odd, last_ref[:, 0], first_ref[:, 0])

    specs = [
        pl.BlockSpec(memory_space=pltpu.SMEM),
        pl.BlockSpec((2, 1, RADIUS, 16, 1024), lambda i: (0, 0, 0, 0, i)),
        pl.BlockSpec((2, 1, RADIUS, 16, 1024), lambda i: (0, 0, 3, 0, i)),
    ]
    out_specs = [pl.BlockSpec((2, RADIUS, 16, 1024), lambda i: (0, 0, 0, i))] * 2
    return glue(body, [(2, RADIUS, 16, 3072)] * 2, [flip, own, own], deps, specs, out_specs, (3,))


def pack_corners(flip, left, right, deps):
    width = left.shape[-1]

    def body(flip_ref, lt_ref, lb_ref, rt_ref, rb_ref, out_ref):
        odd = flip_ref[0] == 1
        out_ref[0] = jnp.where(odd, lt_ref[...], lb_ref[...])
        out_ref[1] = jnp.where(odd, rt_ref[...], rb_ref[...])

    at_first = pl.BlockSpec((2, RADIUS, RADIUS, width), lambda i: (0, 0, 0, i))
    at_last = pl.BlockSpec((2, RADIUS, RADIUS, width), lambda i: (0, 3, 0, i))
    return glue(
        body,
        [(2, 2, RADIUS, RADIUS, width)],
        [flip, left, left, right, right],
        deps,
        [pl.BlockSpec(memory_space=pltpu.SMEM), at_first, at_last, at_first, at_last],
        [pl.BlockSpec((2, 2, RADIUS, RADIUS, width), lambda i: (0, 0, 0, 0, i))],
        (1,),
    )[0]


def prompt_stack(text, others, deps):
    def body(*refs):
        for i, ref in enumerate(refs[:-1]):
            refs[-1][i] = ref[:, 0]

    return glue(body, [(4, 2, 4, 3072)], [text, *others], deps)[0]


def prompt_split(flip, block, others, deps):
    def body(flip_ref, *refs):
        mine_ref, theirs_ref = refs[-2:]
        odd = flip_ref[0] == 1
        for half in (0, 1):
            a_ref, b_ref = refs[2 * half : 2 * half + 2]
            for i in range(4):
                keys = jnp.concatenate([a_ref[i, 0], b_ref[i, 0]], axis=0)
                values = jnp.concatenate([a_ref[i, 1], b_ref[i, 1]], axis=0)
                mine_ref[4 * half + i] = jnp.where(odd, values, keys)
                theirs_ref[4 * half + i] = jnp.where(odd, keys, values)

    whole = pl.BlockSpec(memory_space=pltpu.VMEM)
    return glue(
        body,
        [(8, 8, 3072)] * 2,
        [flip, block, *others],
        deps,
        [pl.BlockSpec(memory_space=pltpu.SMEM)] + [whole] * 4,
        [whole] * 2,
    )


def attend_body(unused, *refs):
    refs = list(refs)
    flip_ref, q_ref, own_ref, left_ref, right_ref, near_ref, far_ref = refs[:7]
    corner_ref, far_left_ref, far_right_ref = refs[7:10]
    del refs[:10]
    ta_refs, tb_refs = refs[:PIECES], refs[PIECES : 2 * PIECES]
    del refs[: 2 * PIECES]
    e_ref, f_ref = refs[:2]
    del refs[:2]
    del refs[:unused]
    o_ref, keys_s, vals_s, tvals_s = refs
    rows, cols = 32, 16

    @pl.when(pl.program_id(0) == 0)
    def _():
        keys_s[:, :, HD:] = f_ref[...]
        vals_s[:, :, HD:] = jnp.ones((48, 32, HD), jnp.bfloat16)
        tvals_s[:, HD:] = jnp.ones((512, HD), jnp.bfloat16)

    scale = math.log2(math.e) / math.sqrt(HD)
    nt = (((1,), (1,)), ((), ()))
    flip = flip_ref[0] == 1
    for head in range(PER_STEP):
        hs = slice(head * HD, (head + 1) * HD)
        for kv, dst in ((0, keys_s), (1, vals_s)):
            left, right = left_ref[kv, :, :, hs], right_ref[kv, :, :, hs]
            own = own_ref[kv, 0, :, :, hs]
            dst[8:40, :, :HD] = jnp.concatenate([left, own, right], axis=1)
            near = [corner_ref[0, kv, :, :, hs], near_ref[kv, :, :, hs], corner_ref[1, kv, :, :, hs]]
            far = [far_left_ref[kv, :, :, hs], far_ref[kv, :, :, hs], far_right_ref[kv, :, :, hs]]
            near, far = jnp.concatenate(near, axis=1), jnp.concatenate(far, axis=1)
            dst[0:8, :, :HD] = jnp.where(flip, near, far)
            dst[40:48, :, :HD] = jnp.where(flip, far, near)
        a = jnp.concatenate([ref[:, :, hs].reshape(64, HD) for ref in ta_refs], axis=0)
        b = jnp.concatenate([ref[:, :, hs].reshape(64, HD) for ref in tb_refs], axis=0)
        text_keys = jnp.where(flip, b, a)
        tvals_s[:, :HD] = jnp.where(flip, a, b)
        for r in range(rows // BLOCK):
            q = q_ref[0, r * BLOCK : (r + 1) * BLOCK, :, hs].reshape(BLOCK * cols, HD)
            q_wide = jnp.concatenate([q, e_ref[r * BLOCK * cols : (r + 1) * BLOCK * cols]], axis=1)
            span = BLOCK + 2 * RADIUS
            keys = keys_s[r * BLOCK : r * BLOCK + span].reshape(span * 32, 2 * HD)
            vals = vals_s[r * BLOCK : r * BLOCK + span].reshape(span * 32, 2 * HD)
            near = lax.dot_general(q_wide, keys, nt, preferred_element_type=jnp.float32)
            far = lax.dot_general(q, text_keys, nt, preferred_element_type=jnp.float32)
            top = jnp.maximum(
                jnp.max(near, -1, keepdims=True), jnp.max(far, -1, keepdims=True)
            )
            near = jnp.exp2((near - top) * scale).astype(jnp.bfloat16)
            far = jnp.exp2((far - top) * scale).astype(jnp.bfloat16)
            out = jnp.dot(near, vals, preferred_element_type=jnp.float32)
            out = out + jnp.dot(far, tvals_s[...], preferred_element_type=jnp.float32)
            out = (out[:, :HD] / out[:, HD:]).astype(jnp.bfloat16)
            o_ref[0, r * BLOCK : (r + 1) * BLOCK, :, hs] = out.reshape(BLOCK, cols, HD)


def attend(flip, queries, own, sides, rows, corner, far_sides, text, feats, output, head, heads, deps):
    at = head // PER_STEP
    spec = pl.BlockSpec
    in_specs = [
        spec(memory_space=pltpu.SMEM),
        spec((1, 32, 16, WIDE), lambda i: (0, 0, 0, at + i)),
        spec((2, 1, 32, 16, WIDE), lambda i: (0, 0, 0, 0, at + i)),
        spec((2, 32, RADIUS, WIDE), lambda i: (0, 0, 0, i)),
        spec((2, 32, RADIUS, WIDE), lambda i: (0, 0, 0, i)),
        spec((2, RADIUS, 16, WIDE), lambda i: (0, 0, 0, at + i)),
        spec((2, RADIUS, 16, WIDE), lambda i: (0, 0, 0, at + i)),
        spec((2, 2, RADIUS, RADIUS, WIDE), lambda i: (0, 0, 0, 0, i)),
        spec((2, RADIUS, RADIUS, WIDE), lambda i: (0, 0, 0, at + i)),
        spec((2, RADIUS, RADIUS, WIDE), lambda i: (0, 0, 0, at + i)),
    ]
    args = [flip, queries, own, *sides, *rows, corner, *far_sides]
    in_specs += [spec((8, 8, WIDE), lambda i: (0, 0, at + i))] * (2 * PIECES)
    in_specs += [
        spec((512, HD), lambda i: (0, 0)),
        spec((48, 32, HD), lambda i: (0, 0, 0)),
    ]
    args += [*text, *feats]
    aliases = {}
    if output is not None:
        aliases = {len(args): 0}
        in_specs.append(spec(memory_space=pl.ANY))
        args.append(output)
    in_specs += [spec(memory_space=pl.ANY)] * len(deps)
    args += deps
    return pl.pallas_call(
        functools.partial(attend_body, len(deps) + (output is not None)),
        grid=(heads // PER_STEP,),
        in_specs=in_specs,
        out_specs=spec((1, 32, 16, WIDE), lambda i: (0, 0, 0, at + i)),
        out_shape=jax.ShapeDtypeStruct(queries.shape, jnp.bfloat16),
        scratch_shapes=[
            pltpu.VMEM((48, 32, 2 * HD), jnp.bfloat16),
            pltpu.VMEM((48, 32, 2 * HD), jnp.bfloat16),
            pltpu.VMEM((512, 2 * HD), jnp.bfloat16),
        ],
        input_output_aliases=aliases,
        compiler_params=pltpu.CompilerParams(vmem_limit_bytes=VMEM_LIMIT),
        cost_estimate=pl.CostEstimate(
            flops=1000, bytes_accessed=1000, transcendentals=0
        ),
    )(*args)


def features():
    query = np.arange(512)
    lane = np.arange(HD)
    hot = (
        (lane[None] == (query % 16)[:, None])
        | (lane[None] - 16 == (query // 16)[:, None])
        | (lane[None] == 48)
    )
    row = jnp.arange(48, dtype=jnp.int32)[:, None, None] - RADIUS
    col = jnp.arange(32, dtype=jnp.int32)[None, :, None] - RADIUS
    lane = jnp.arange(HD, dtype=jnp.int32)[None, None, :]
    grid_row = lax.axis_index("lat") * 32 + row
    bad = (lane < 16) & (jnp.abs(col - lane) > RADIUS)
    bad |= (lane >= 16) & (lane < 48) & (jnp.abs(row - (lane - 16)) > RADIUS)
    bad |= (lane == 48) & ((grid_row < 0) | (grid_row >= N_LAT * 32))
    return jnp.asarray(hot, jnp.bfloat16), jnp.where(bad, NEG, 0.0).astype(jnp.bfloat16)


def on_device(queries, key_value, text_kv):
    flip = (lax.axis_index("lat") % CORE).astype(jnp.int32)[None]
    starts = [sum(CHUNKS[:i]) for i in range(len(CHUNKS))]
    feats = features()
    corners = [None] * len(CHUNKS)

    def inner(a, b):
        return a != b

    def send_corners(i, deps):
        rows = pack_corners(flip, *sides[i], deps)
        corners[i] = send(rows, core=1)
        return rows

    sides = []

    def send_sides(i, deps):
        r, l = pack_sides(key_value, starts[i], CHUNKS[i], deps)
        sides.append((send_lon(r, 1), send_lon(l, -1)))
        return r

    by_z = [send(text_kv, zl=1), send(text_kv, zh=1), send(text_kv, zh=1, zl=1)]
    block = prompt_stack(text_kv, by_z, ())
    by_y = [send(block, y=step) for step in (1, 3, 2)]
    near, far = pack_rows(flip, key_value, (block,))
    mine, theirs = prompt_split(flip, block, by_y, (near,))
    other = send(theirs, core=1)
    near, far = send(near, core=1), send_where(far, inner, zh=1, core=1)
    up, down = [send(x, x_=1) for x in (mine, other)], [send(x, x_=3) for x in (mine, other)]
    pieces = [mine, other, *up, *down, send(up[0], x_=1), send(down[1], x_=3)]
    swapped = [send(piece, core=1) for piece in pieces]
    text = pieces + [swapped[i ^ 1] for i in range(PIECES)]
    token = send_sides(0, (up[0], down[1]))
    token = send_sides(1, (token,))
    r, l = pack_far_sides(far, (token,))
    far_sides = (send_where(r, inner, lon=1), send_where(l, inner, lon=-1))
    token = send_sides(2, (r,))
    token = send_sides(3, (token,))
    output = None
    for i in range(len(CHUNKS)):
        token = send_corners(i, (token,))
        output = token = attend(
            flip, queries, key_value, sides[i], (near, far), corners[i], far_sides, text, feats,
            output, starts[i], CHUNKS[i], (),
        )
    return output


def solution(mesh):
    in_specs = (
        P(None, "lat", "lon", None),
        P(None, None, "lat", "lon", None),
        P(None, None, ("lat", "lon"), None),
    )
    out_specs = P(None, "lat", "lon", None)
    return jax.shard_map(
        on_device, mesh=mesh, in_specs=in_specs, out_specs=out_specs, check_vma=False
    )
```

time: 224 us -> 194 us (0.87); the launches traced: 223 us -> 191 us
  Pallas kernels: 47.1 us -> 71.4 us
  starting transfers between devices: 74.8 us -> 51.4 us
  local copies, waits for them, and re-layouts: 23.8 us -> 6.1 us
  waiting for transfers between devices: 73.5 us -> 60.1 us
    pallas_call x8 -> x16, Pallas kernels: 47.1 us -> 71.4 us  [the longest x4 42.7 us: attend(): pl.pallas_call(functools.partial(attend_body, len(deps) + (output is not...]
    ppermute x12 -> x26, waiting for transfers between devices: 58 us -> 38.9 us  [send(): return lax.ppermute(x, ('lat', 'lon'), pairs)]
    ppermute x8 -> x3, waiting for transfers between devices: 0.02 us -> 17 us  [send_where(): return lax.ppermute(x, ('lat', 'lon'), pairs)]
    ppermute x8 -> x3, starting transfers between devices: 27.3 us -> 10.4 us  [send_where(): return lax.ppermute(x, ('lat', 'lon'), pairs)]
    ppermute x8, starting transfers between devices: 26.7 us -> 12.5 us  [send_lon(): lax.ppermute(x, 'lon', [(i, (i + step) % N_LON) for i in range(N_LON)])]
    ppermute x8, waiting for transfers between devices: 15.5 us -> 4.25 us  [send_lon(): lax.ppermute(x, 'lon', [(i, (i + step) % N_LON) for i in range(N_LON)])]
    ppermute x12 -> x26, starting transfers between devices: 20.9 us -> 28.5 us  [send(): return lax.ppermute(x, ('lat', 'lon'), pairs)]
    unnamed x32 -> x58, local copies, waits for them, and re-layouts: 13.6 us -> 6.1 us
  transfers between devices with their start and end apart: 28 -> 37, of which waited for: 10 -> 16; matrix products, arithmetic and copies ran while one was open for 9% -> 1% of each run, Pallas kernels for 19% -> 29%
where the time goes in v2:
time: 194 us; the launch traced here: 191 us
  Pallas kernels  71.4 us (37%)
  waiting for transfers between devices  60.1 us (31%)
  starting transfers between devices  51.4 us (26%)
  local copies, waits for them, and re-layouts  6.1 us (3%)
    pallas_call x4, Pallas kernels, attend(): pl.pallas_call(functools.partial(attend_body, len(deps) + (output is not...  42.7 us
    ppermute x26, waiting for transfers between devices, send(): return lax.ppermute(x, ('lat', 'lon'), pairs)  38.9 us
    pallas_call x12, Pallas kernels, glue(): pl.pallas_call(kernel, grid=grid or (), in_specs=list(specs) + [pl.BlockS...  28.7 us
    ppermute x26, starting transfers between devices, send(): return lax.ppermute(x, ('lat', 'lon'), pairs)  28.5 us
    ppermute x3, waiting for transfers between devices, send_where(): return lax.ppermute(x, ('lat', 'lon'), pairs)  17 us
    ppermute x8, starting transfers between devices, send_lon(): lax.ppermute(x, 'lon', [(i, (i + step) % N_LON) for i in range(N_LON)])  12.5 us
    ppermute x3, starting transfers between devices, send_where(): return lax.ppermute(x, ('lat', 'lon'), pairs)  10.4 us
    unnamed x58, local copies, waits for them, and re-layouts  6.1 us
  transfers between devices with their start and end apart: 37, of which 16 were waited for; matrix products, arithmetic and copies ran while one was open for 1% of the time, Pallas kernels for 29%

profile of v2, /device:TPU:1, one launch (start us, length us, event | category | flops | bytes accessed | tf_op | source)
XLA Modules:
  0.0 191.1 jit_solution(5666316389640378677)
XLA Ops:
  0.0 4.4 %collective-permute-start.1 = (bf16[2,1,4,3072]{3,2,1,0:T(4,128)(2,1)}, bf16[2,1,4,3072]{3,2,1,0:T(4,128)(2,1)S(1)}, u32[]{:S(2)}, u32[]{:S(2)}) collective-permute-start(bf16[2,1,4,3072]{3,2,1,0:T(4,128)(2,1)} %refs_0_.5), channel_id=1, source_target_pairs={{0,64},{1,65},{2,66},{3,67},{4,68},{5,69},{6,70},{7,71},{8,72},{9,... | collective-permute-start | bytes 147464 | tf_op jit(solution)/shard_map/ppermute | solution.py:42
  5.2 0.9 collective-permute-done.1.refs_2_
  6.1 1.7 collective-permute-done.refs_1_
  7.8 1.7 collective-permute-done.2.refs_3_
  10.1 1.6 shard_map.46.refs_3_.refs_1_
  11.7 2.9 %collective-permute-start.6 = (bf16[4,2,4,3072]{3,2,1,0:T(4,128)(2,1)}, bf16[4,2,4,3072]{3,2,1,0:T(4,128)(2,1)S(1)}, u32[]{:S(2)}, u32[]{:S(2)}) collective-permute-start(bf16[4,2,4,3072]{3,2,1,0:T(4,128)(2,1)} %shard_map.46.refs_3_.refs_1_), channel_id=1, source_target_pairs={{0,2},{1,3},{2,0},{3,1},{4,6},{5,7},{6,4},{7,5},{8,10},{9,11},{10,... | collective-permute-start | bytes 589832 | tf_op jit(solution)/shard_map/ppermute | solution.py:42
  16.1 4.4 %shard_map.47 = (bf16[2,8,16,3072]{3,2,1,0:T(8,128)(2,1)}, bf16[2,8,16,3072]{3,2,1,0:T(8,128)(2,1)}) custom-call(s32[1]{0:T(128)} %bitcast.refs_0_, bf16[2,1,32,16,3072]{4,3,2,1,0:T(8,128)(2,1)} %refs_2_.9, bf16[2,1,32,16,3072]{4,3,2,1,0:T(8,128)(2,1)} %refs_2_.9, bf16[4,2,4,3072]{3,2,1,0:T(4,128)(2,1)} %shard_map.46.refs_3_.refs_1_), custom_call_target="tpu_custom_call" | custom-call | flops 1000 | bytes 1000 | tf_op jit(solution)/shard_map/pallas_call | solution.py:58
  20.5 2.0 %collective-permute-done.5.refs_3_ = bf16[4,2,4,3072]{3,2,1,0:T(4,128)(2,1)S(1)} collective-permute-done((bf16[4,2,4,3072]{3,2,1,0:T(4,128)(2,1)}, bf16[4,2,4,3072]{3,2,1,0:T(4,128)(2,1)S(1)}, u32[]{:S(2)}, u32[]{:S(2)}) %collective-permute-start.5) | collective-permute-done | bytes 196640 | tf_op jit(solution)/shard_map/ppermute | solution.py:42
  22.5 1.3 collective-permute-done.4.refs_2_
  24.6 2.4 %shard_map.48 = (bf16[8,8,3072]{2,1,0:T(8,128)(2,1)}, bf16[8,8,3072]{2,1,0:T(8,128)(2,1)}) custom-call(s32[1]{0:T(128)} %bitcast.refs_0_, bf16[4,2,4,3072]{3,2,1,0:T(4,128)(2,1)} %shard_map.46.refs_3_.refs_1_, bf16[4,2,4,3072]{3,2,1,0:T(4,128)(2,1)} %copy-done.23, bf16[4,2,4,3072]{3,2,1,0:T(4,128)(2,1)} %copy-done.22, bf16[4,2,4,3072]{3,2,1,0:T(4,128)(2,1)} %copy-done.21, ...), custom_call_target="tpu_custom_call" | custom-call | flops 1000 | bytes 1000 | tf_op jit(solution)/shard_map/pallas_call | solution.py:58
  26.9 2.1 %collective-permute-start.8 = (bf16[8,8,3072]{2,1,0:T(8,128)(2,1)}, bf16[8,8,3072]{2,1,0:T(8,128)(2,1)S(1)}, u32[]{:S(2)}, u32[]{:S(2)}) collective-permute-start(bf16[8,8,3072]{2,1,0:T(8,128)(2,1)} %get-tuple-element.22), channel_id=1, source_target_pairs={{0,32},{1,33},{2,34},{3,35},{4,36},{5,37},{6,38},{7,39},{8,40},{9,... | collective-permute-start | bytes 1179656 | tf_op jit(solution)/shard_map/ppermute | solution.py:42
  29.0 2.3 %collective-permute-start.3 = (bf16[2,8,16,3072]{3,2,1,0:T(8,128)(2,1)}, bf16[2,8,16,3072]{3,2,1,0:T(8,128)(2,1)S(1)}, u32[]{:S(2)}, u32[]{:S(2)}) collective-permute-start(bf16[2,8,16,3072]{3,2,1,0:T(8,128)(2,1)} %get-tuple-element.19), channel_id=1, source_target_pairs={{32,64},{33,65},{34,66},{35,67},{36,68},{37,69},{38,70},{39,71},{4... | collective-permute-start | bytes 4718600 | tf_op jit(solution)/shard_map/ppermute | solution.py:33
  31.3 2.5 %collective-permute-start.23 = (bf16[8,8,3072]{2,1,0:T(8,128)(2,1)}, bf16[8,8,3072]{2,1,0:T(8,128)(2,1)S(1)}, u32[]{:S(2)}, u32[]{:S(2)}) collective-permute-start(bf16[8,8,3072]{2,1,0:T(8,128)(2,1)} %get-tuple-element.21.refs_10_), channel_id=1, source_target_pairs={{0,24},{1,25},{2,26},{3,27},{4,28},{5,29},{6,30},{7,31},{8,0},{9,1... | collective-permute-start | bytes 1179656 | tf_op jit(solution)/shard_map/ppermute | solution.py:42
  34.1 8.4 %collective-permute-done.23.refs_14_ = bf16[8,8,3072]{2,1,0:T(8,128)(2,1)S(1)} collective-permute-done((bf16[8,8,3072]{2,1,0:T(8,128)(2,1)}, bf16[8,8,3072]{2,1,0:T(8,128)(2,1)S(1)}, u32[]{:S(2)}, u32[]{:S(2)}) %collective-permute-start.23) | collective-permute-done | bytes 393248 | tf_op jit(solution)/shard_map/ppermute | solution.py:42
  42.5 3.0 %collective-permute-start.9 = (bf16[8,8,3072]{2,1,0:T(8,128)(2,1)S(1)}, bf16[8,8,3072]{2,1,0:T(8,128)(2,1)S(1)}, u32[]{:S(2)}, u32[]{:S(2)}) collective-permute-start(bf16[8,8,3072]{2,1,0:T(8,128)(2,1)S(1)} %collective-permute-done.8.refs_11_), channel_id=1, source_target_pairs={{0,24},{1,25},{2,26},{3,27},{4,28},{5,29},{6,30},{7,31},{8,0},{9,1... | collective-permute-start | bytes 1179656 | tf_op jit(solution)/shard_map/ppermute | solution.py:42
  45.5 1.0 collective-permute-done.7.refs_1_.refs_12_
  47.0 7.3 %collective-permute-done.22.refs_13_ = bf16[8,8,3072]{2,1,0:T(8,128)(2,1)} collective-permute-done((bf16[8,8,3072]{2,1,0:T(8,128)(2,1)S(1)}, bf16[8,8,3072]{2,1,0:T(8,128)(2,1)}, u32[]{:S(2)}, u32[]{:S(2)}) %collective-permute-start.22) | collective-permute-done | bytes 393248 | tf_op jit(solution)/shard_map/ppermute | solution.py:42
  55.2 0.9 collective-permute-done.29.refs_21_
  56.5 9.6 %collective-permute-done.24.refs_16_ = bf16[8,8,3072]{2,1,0:T(8,128)(2,1)S(1)} collective-permute-done((bf16[8,8,3072]{2,1,0:T(8,128)(2,1)S(1)}, bf16[8,8,3072]{2,1,0:T(8,128)(2,1)S(1)}, u32[]{:S(2)}, u32[]{:S(2)}) %collective-permute-start.24) | collective-permute-done | bytes 393248 | tf_op jit(solution)/shard_map/ppermute | solution.py:42
  66.8 0.9 collective-permute-start.25
  67.7 2.3 %shard_map.49 = (bf16[2,32,8,512]{3,2,1,0:T(8,128)(2,1)}, bf16[2,32,8,512]{3,2,1,0:T(8,128)(2,1)}) custom-call(bf16[2,1,32,16,3072]{4,3,2,1,0:T(8,128)(2,1)} %refs_2_.9, bf16[8,8,3072]{2,1,0:T(8,128)(2,1)} %copy-done.4, bf16[8,8,3072]{2,1,0:T(8,128)(2,1)} %copy-done.5), custom_call_target="tpu_custom_call" | custom-call | flops 1000 | bytes 1000 | tf_op jit(solution)/shard_map/pallas_call | solution.py:58
  70.0 1.6 collective-permute-start.18
  71.6 2.6 %collective-permute-start.33 = (bf16[8,8,3072]{2,1,0:T(8,128)(2,1)}, bf16[8,8,3072]{2,1,0:T(8,128)(2,1)S(1)}, u32[]{:S(2)}, u32[]{:S(2)}) collective-permute-start(bf16[8,8,3072]{2,1,0:T(8,128)(2,1)} %copy-done.12), channel_id=1, source_target_pairs={{0,32},{1,33},{2,34},{3,35},{4,36},{5,37},{6,38},{7,39},{8,40},{9,... | collective-permute-start | bytes 1179656 | tf_op jit(solution)/shard_map/ppermute | solution.py:42
  74.3 2.7 %shard_map.50 = (bf16[2,32,8,1024]{3,2,1,0:T(8,128)(2,1)}, bf16[2,32,8,1024]{3,2,1,0:T(8,128)(2,1)}) custom-call(bf16[2,1,32,16,3072]{4,3,2,1,0:T(8,128)(2,1)} %refs_2_.9, bf16[2,32,8,512]{3,2,1,0:T(8,128)(2,1)} %get-tuple-element.23.refs_1_), custom_call_target="tpu_custom_call" | custom-call | flops 1000 | bytes 1000 | tf_op jit(solution)/shard_map/pallas_call | solution.py:58
  77.0 2.6 %shard_map.51 = (bf16[2,8,8,3072]{3,2,1,0:T(8,128)(2,1)}, bf16[2,8,8,3072]{3,2,1,0:T(8,128)(2,1)}) custom-call(bf16[2,8,16,3072]{3,2,1,0:T(8,128)(2,1)} %copy-done, bf16[2,32,8,1024]{3,2,1,0:T(8,128)(2,1)} %get-tuple-element.24.refs_1_), custom_call_target="tpu_custom_call" | custom-call | flops 1000 | bytes 1000 | tf_op jit(solution)/shard_map/pallas_call | solution.py:58
  79.6 6.2 %collective-permute-start.21 = (bf16[2,8,8,3072]{3,2,1,0:T(8,128)(2,1)}, bf16[2,8,8,3072]{3,2,1,0:T(8,128)(2,1)S(1)}, u32[]{:S(2)}, u32[]{:S(2)}) collective-permute-start(bf16[2,8,8,3072]{3,2,1,0:T(8,128)(2,1)} %get-tuple-element.32), channel_id=1, source_target_pairs={{32,63},{33,32},{34,33},{35,34},{36,35},{37,36},{38,37},{39,38},{4... | collective-permute-start | bytes 2359304 | tf_op jit(solution)/shard_map/ppermute | solution.py:33
  86.0 2.6 %collective-permute-done.17.refs_1_.refs_2_.refs_3_ = bf16[2,32,8,512]{3,2,1,0:T(8,128)(2,1)} collective-permute-done((bf16[2,32,8,512]{3,2,1,0:T(8,128)(2,1)}, bf16[2,32,8,512]{3,2,1,0:T(8,128)(2,1)}, u32[]{:S(2)}, u32[]{:S(2)}) %collective-permute-start.17) | collective-permute-done | bytes 524320 | tf_op jit(solution)/shard_map/ppermute | solution.py:46
  88.6 3.4 %collective-permute-start.16 = (bf16[2,32,8,1024]{3,2,1,0:T(8,128)(2,1)}, bf16[2,32,8,1024]{3,2,1,0:T(8,128)(2,1)}, u32[]{:S(2)}, u32[]{:S(2)}) collective-permute-start(bf16[2,32,8,1024]{3,2,1,0:T(8,128)(2,1)} %get-tuple-element.30), channel_id=1, source_target_pairs={{0,31},{1,0},{2,1},{3,2},{4,3},{5,4},{6,5},{7,6},{8,7},{9,8},{10,9... | collective-permute-start | bytes 3145736 | tf_op jit(solution)/shard_map/ppermute | solution.py:46
  92.6 2.7 %shard_map.52 = (bf16[2,32,8,1024]{3,2,1,0:T(8,128)(2,1)}, bf16[2,32,8,1024]{3,2,1,0:T(8,128)(2,1)}) custom-call(bf16[2,1,32,16,3072]{4,3,2,1,0:T(8,128)(2,1)} %refs_2_.9, bf16[2,8,8,3072]{3,2,1,0:T(8,128)(2,1)} %get-tuple-element.25.refs_1_), custom_call_target="tpu_custom_call" | custom-call | flops 1000 | bytes 1000 | tf_op jit(solution)/shard_map/pallas_call | solution.py:58
  95.3 2.2 %shard_map.53 = (bf16[2,32,8,512]{3,2,1,0:T(8,128)(2,1)}, bf16[2,32,8,512]{3,2,1,0:T(8,128)(2,1)}) custom-call(bf16[2,1,32,16,3072]{4,3,2,1,0:T(8,128)(2,1)} %refs_2_.9, bf16[2,32,8,1024]{3,2,1,0:T(8,128)(2,1)} %get-tuple-element.26.refs_1_), custom_call_target="tpu_custom_call" | custom-call | flops 1000 | bytes 1000 | tf_op jit(solution)/shard_map/pallas_call | solution.py:58
  97.5 1.8 shard_map.54
  99.4 4.4 %collective-permute-start.19 = (bf16[2,2,8,8,512]{4,3,2,1,0:T(8,128)(2,1)}, bf16[2,2,8,8,512]{4,3,2,1,0:T(8,128)(2,1)S(1)}, u32[]{:S(2)}, u32[]{:S(2)}) collective-permute-start(bf16[2,2,8,8,512]{4,3,2,1,0:T(8,128)(2,1)} %shard_map.54), channel_id=1, source_target_pairs={{0,32},{1,33},{2,34},{3,35},{4,36},{5,37},{6,38},{7,39},{8,40},{9,... | collective-permute-start | bytes 786440 | tf_op jit(solution)/shard_map/ppermute | solution.py:42
  103.8 1.9 %collective-permute-start.20 = (bf16[2,8,8,3072]{3,2,1,0:T(8,128)(2,1)}, bf16[2,8,8,3072]{3,2,1,0:T(8,128)(2,1)S(1)}, u32[]{:S(2)}, u32[]{:S(2)}) collective-permute-start(bf16[2,8,8,3072]{3,2,1,0:T(8,128)(2,1)} %get-tuple-element.25.refs_1_), channel_id=1, source_target_pairs={{32,33},{33,34},{34,35},{35,36},{36,37},{37,38},{38,39},{39,40},{4... | collective-permute-start | bytes 2359304 | tf_op jit(solution)/shard_map/ppermute | solution.py:33
  105.9 5.9 %collective-permute-start.14 = (bf16[2,32,8,1024]{3,2,1,0:T(8,128)(2,1)}, bf16[2,32,8,1024]{3,2,1,0:T(8,128)(2,1)}, u32[]{:S(2)}, u32[]{:S(2)}) collective-permute-start(bf16[2,32,8,1024]{3,2,1,0:T(8,128)(2,1)} %get-tuple-element.29), channel_id=1, source_target_pairs={{0,31},{1,0},{2,1},{3,2},{4,3},{5,4},{6,5},{7,6},{8,7},{9,8},{10,9... | collective-permute-start | bytes 3145736 | tf_op jit(solution)/shard_map/ppermute | solution.py:46
  112.0 0.9 select_convert_fusion.refs_27_
  112.9 17.0 %collective-permute-done.20.refs_8_ = bf16[2,8,8,3072]{3,2,1,0:T(8,128)(2,1)S(1)} collective-permute-done((bf16[2,8,8,3072]{3,2,1,0:T(8,128)(2,1)}, bf16[2,8,8,3072]{3,2,1,0:T(8,128)(2,1)S(1)}, u32[]{:S(2)}, u32[]{:S(2)}) %collective-permute-start.20) | collective-permute-done | bytes 786464 | tf_op jit(solution)/shard_map/ppermute | solution.py:33
  130.7 8.2 %shard_map.55.refs_5_.refs_28_ = bf16[1,32,16,3072]{3,2,1,0:T(8,128)(2,1)} custom-call(s32[1]{0:T(128)} %bitcast.refs_0_, bf16[1,32,16,3072]{3,2,1,0:T(8,128)(2,1)} %refs_1_.9, bf16[2,1,32,16,3072]{4,3,2,1,0:T(8,128)(2,1)} %refs_2_.9, bf16[2,32,8,512]{3,2,1,0:T(8,128)(2,1)} %collective-permute-done.17.refs_1_.refs_2_.refs_3_, ...), custom_call_target="tpu_custom_call" | custom-call | flops 1000 | bytes 1000 | tf_op jit(solution)/shard_map/pallas_call | solution.py:253
  138.9 2.0 %shard_map.56 = bf16[2,2,8,8,1024]{4,3,2,1,0:T(8,128)(2,1)} custom-call(s32[1]{0:T(128)} %bitcast.refs_0_, bf16[2,32,8,1024]{3,2,1,0:T(8,128)(2,1)} %collective-permute-done.15.refs_1_.refs_2_.refs_3_, bf16[2,32,8,1024]{3,2,1,0:T(8,128)(2,1)} %collective-permute-done.15.refs_1_.refs_2_.refs_3_, ...), custom_call_target="tpu_custom_call" | custom-call | flops 1000 | bytes 1000 | tf_op jit(solution)/shard_map/pallas_call | solution.py:58
  141.0 2.1 %collective-permute-done.34.refs_7_ = bf16[2,2,8,8,1024]{4,3,2,1,0:T(8,128)(2,1)S(1)} collective-permute-done((bf16[2,2,8,8,1024]{4,3,2,1,0:T(8,128)(2,1)}, bf16[2,2,8,8,1024]{4,3,2,1,0:T(8,128)(2,1)S(1)}, u32[]{:S(2)}, u32[]{:S(2)}) %collective-permute-start.34) | collective-permute-done | bytes 524320 | tf_op jit(solution)/shard_map/ppermute | solution.py:42
  143.9 13.2 %shard_map.57.refs_5_.refs_28_ = bf16[1,32,16,3072]{3,2,1,0:T(8,128)(2,1)} custom-call(s32[1]{0:T(128)} %bitcast.refs_0_, bf16[1,32,16,3072]{3,2,1,0:T(8,128)(2,1)} %refs_1_.9, bf16[2,1,32,16,3072]{4,3,2,1,0:T(8,128)(2,1)} %refs_2_.9, bf16[2,32,8,1024]{3,2,1,0:T(8,128)(2,1)} %collective-permute-done.15.refs_1_.refs_2_.refs_3_, ...), custom_call_target="tpu_custom_call", output_to_operand_aliasing={{}: (28, {})} | custom-call | flops 1000 | bytes 1000 | tf_op jit(solution)/shard_map/pallas_call | solution.py:253
  157.1 2.1 %shard_map.58 = bf16[2,2,8,8,1024]{4,3,2,1,0:T(8,128)(2,1)} custom-call(s32[1]{0:T(128)} %bitcast.refs_0_, bf16[2,32,8,1024]{3,2,1,0:T(8,128)(2,1)} %collective-permute-done.13.refs_1_.refs_2_.refs_3_, bf16[2,32,8,1024]{3,2,1,0:T(8,128)(2,1)} %collective-permute-done.13.refs_1_.refs_2_.refs_3_, ...), custom_call_target="tpu_custom_call" | custom-call | flops 1000 | bytes 1000 | tf_op jit(solution)/shard_map/pallas_call | solution.py:58
  159.4 1.5 collective-permute-start.10
  162.1 13.2 %shard_map.59.refs_5_.refs_28_ = bf16[1,32,16,3072]{3,2,1,0:T(8,128)(2,1)} custom-call(s32[1]{0:T(128)} %bitcast.refs_0_, bf16[1,32,16,3072]{3,2,1,0:T(8,128)(2,1)} %refs_1_.9, bf16[2,1,32,16,3072]{4,3,2,1,0:T(8,128)(2,1)} %refs_2_.9, bf16[2,32,8,1024]{3,2,1,0:T(8,128)(2,1)} %collective-permute-done.13.refs_1_.refs_2_.refs_3_, ...), custom_call_target="tpu_custom_call", output_to_operand_aliasing={{}: (28, {})} | custom-call | flops 1000 | bytes 1000 | tf_op jit(solution)/shard_map/pallas_call | solution.py:253
  175.3 1.7 collective-permute-done.10.refs_1_.refs_2_.refs_3_
  177.8 1.8 shard_map.60
  179.6 1.2 collective-permute-start.36
  180.8 1.4 collective-permute-done.36.refs_7_
  182.9 8.2 %shard_map.61 = bf16[1,32,16,3072]{3,2,1,0:T(8,128)(2,1)} custom-call(s32[1]{0:T(128)} %bitcast.refs_0_, bf16[1,32,16,3072]{3,2,1,0:T(8,128)(2,1)} %refs_1_.9, bf16[2,1,32,16,3072]{4,3,2,1,0:T(8,128)(2,1)} %refs_2_.9, bf16[2,32,8,512]{3,2,1,0:T(8,128)(2,1)} %copy-done.15, bf16[2,32,8,512]{3,2,1,0:T(8,128)(2,1)} %copy-done.14, ...), custom_call_target="tpu_custom_call", output_to_operand_aliasing={{}: (28, {})} | custom-call | flops 1000 | bytes 1000 | tf_op jit(solution)/shard_map/pallas_call | solution.py:253
  (110 shorter events, 11.9 us)
Async XLA Ops:
  0.0 6.1 %collective-permute-start.1 = (bf16[2,1,4,3072]{3,2,1,0:T(4,128)(2,1)}, bf16[2,1,4,3072]{3,2,1,0:T(4,128)(2,1)S(1)}, u32[]{:S(2)}, u32[]{:S(2)}) collective-permute-start(bf16[2,1,4,3072]{3,2,1,0:T(4,128)(2,1)} %refs_0_.5), channel_id=1, source_target_pairs={{0,64},{1,65},{2,66},{3,67},{4,68},{5,69},{6,70},{7,71},{8,72},{9,... | collective-permute-start | bytes 147464 | tf_op jit(solution)/shard_map/ppermute | solution.py:42
  4.4 3.4 %collective-permute-start = (bf16[2,1,4,3072]{3,2,1,0:T(4,128)(2,1)}, bf16[2,1,4,3072]{3,2,1,0:T(4,128)(2,1)S(1)}, u32[]{:S(2)}, u32[]{:S(2)}) collective-permute-start(bf16[2,1,4,3072]{3,2,1,0:T(4,128)(2,1)} %refs_0_.5), channel_id=1, source_target_pairs={{0,4},{1,5},{2,6},{3,7},{4,0},{5,1},{6,2},{7,3},{8,12},{9,13},{10,... | collective-permute-start | bytes 147464 | tf_op jit(solution)/shard_map/ppermute | solution.py:42
  5.2 4.4 %collective-permute-start.2 = (bf16[2,1,4,3072]{3,2,1,0:T(4,128)(2,1)}, bf16[2,1,4,3072]{3,2,1,0:T(4,128)(2,1)S(1)}, u32[]{:S(2)}, u32[]{:S(2)}) collective-permute-start(bf16[2,1,4,3072]{3,2,1,0:T(4,128)(2,1)} %refs_0_.5), channel_id=1, source_target_pairs={{0,68},{1,69},{2,70},{3,71},{4,64},{5,65},{6,66},{7,67},{8,76},{9,... | collective-permute-start | bytes 147464 | tf_op jit(solution)/shard_map/ppermute | solution.py:42
  11.7 8.8 %collective-permute-start.6 = (bf16[4,2,4,3072]{3,2,1,0:T(4,128)(2,1)}, bf16[4,2,4,3072]{3,2,1,0:T(4,128)(2,1)S(1)}, u32[]{:S(2)}, u32[]{:S(2)}) collective-permute-start(bf16[4,2,4,3072]{3,2,1,0:T(4,128)(2,1)} %shard_map.46.refs_3_.refs_1_), channel_id=1, source_target_pairs={{0,2},{1,3},{2,0},{3,1},{4,6},{5,7},{6,4},{7,5},{8,10},{9,11},{10,... | collective-permute-start | bytes 589832 | tf_op jit(solution)/shard_map/ppermute | solution.py:42
  14.6 7.9 %collective-permute-start.5 = (bf16[4,2,4,3072]{3,2,1,0:T(4,128)(2,1)}, bf16[4,2,4,3072]{3,2,1,0:T(4,128)(2,1)S(1)}, u32[]{:S(2)}, u32[]{:S(2)}) collective-permute-start(bf16[4,2,4,3072]{3,2,1,0:T(4,128)(2,1)} %shard_map.46.refs_3_.refs_1_), channel_id=1, source_target_pairs={{0,3},{1,0},{2,1},{3,2},{4,7},{5,4},{6,5},{7,6},{8,11},{9,8},{10,9... | collective-permute-start | bytes 589832 | tf_op jit(solution)/shard_map/ppermute | solution.py:42
  15.4 8.5 %collective-permute-start.4 = (bf16[4,2,4,3072]{3,2,1,0:T(4,128)(2,1)}, bf16[4,2,4,3072]{3,2,1,0:T(4,128)(2,1)S(1)}, u32[]{:S(2)}, u32[]{:S(2)}) collective-permute-start(bf16[4,2,4,3072]{3,2,1,0:T(4,128)(2,1)} %shard_map.46.refs_3_.refs_1_), channel_id=1, source_target_pairs={{0,1},{1,2},{2,3},{3,0},{4,5},{5,6},{6,7},{7,4},{8,9},{9,10},{10,1... | collective-permute-start | bytes 589832 | tf_op jit(solution)/shard_map/ppermute | solution.py:42
  26.9 6.9 %collective-permute-start.8 = (bf16[8,8,3072]{2,1,0:T(8,128)(2,1)}, bf16[8,8,3072]{2,1,0:T(8,128)(2,1)S(1)}, u32[]{:S(2)}, u32[]{:S(2)}) collective-permute-start(bf16[8,8,3072]{2,1,0:T(8,128)(2,1)} %get-tuple-element.22), channel_id=1, source_target_pairs={{0,32},{1,33},{2,34},{3,35},{4,36},{5,37},{6,38},{7,39},{8,40},{9,... | collective-permute-start | bytes 1179656 | tf_op jit(solution)/shard_map/ppermute | solution.py:42
  29.0 5.0 %collective-permute-start.27 = (bf16[8,8,3072]{2,1,0:T(8,128)(2,1)}, bf16[8,8,3072]{2,1,0:T(8,128)(2,1)S(1)}, u32[]{:S(2)}, u32[]{:S(2)}) collective-permute-start(bf16[8,8,3072]{2,1,0:T(8,128)(2,1)} %get-tuple-element.21.refs_10_), channel_id=1, source_target_pairs={{0,32},{1,33},{2,34},{3,35},{4,36},{5,37},{6,38},{7,39},{8,40},{9,... | collective-permute-start | bytes 1179656 | tf_op jit(solution)/shard_map/ppermute | solution.py:42
  29.0 42.6 %collective-permute-start.3 = (bf16[2,8,16,3072]{3,2,1,0:T(8,128)(2,1)}, bf16[2,8,16,3072]{3,2,1,0:T(8,128)(2,1)S(1)}, u32[]{:S(2)}, u32[]{:S(2)}) collective-permute-start(bf16[2,8,16,3072]{3,2,1,0:T(8,128)(2,1)} %get-tuple-element.19), channel_id=1, source_target_pairs={{32,64},{33,65},{34,66},{35,67},{36,68},{37,69},{38,70},{39,71},{4... | collective-permute-start | bytes 4718600 | tf_op jit(solution)/shard_map/ppermute | solution.py:33
  31.3 11.2 %collective-permute-start.23 = (bf16[8,8,3072]{2,1,0:T(8,128)(2,1)}, bf16[8,8,3072]{2,1,0:T(8,128)(2,1)S(1)}, u32[]{:S(2)}, u32[]{:S(2)}) collective-permute-start(bf16[8,8,3072]{2,1,0:T(8,128)(2,1)} %get-tuple-element.21.refs_10_), channel_id=1, source_target_pairs={{0,24},{1,25},{2,26},{3,27},{4,28},{5,29},{6,30},{7,31},{8,0},{9,1... | collective-permute-start | bytes 1179656 | tf_op jit(solution)/shard_map/ppermute | solution.py:42
  33.8 12.7 %collective-permute-start.7 = (bf16[8,8,3072]{2,1,0:T(8,128)(2,1)}, bf16[8,8,3072]{2,1,0:T(8,128)(2,1)S(1)}, u32[]{:S(2)}, u32[]{:S(2)}) collective-permute-start(bf16[8,8,3072]{2,1,0:T(8,128)(2,1)} %get-tuple-element.21.refs_10_), channel_id=1, source_target_pairs={{0,8},{1,9},{2,10},{3,11},{4,12},{5,13},{6,14},{7,15},{8,16},{9,17... | collective-permute-start | bytes 1179656 | tf_op jit(solution)/shard_map/ppermute | solution.py:42
  33.8 32.2 %copy-start.6 = (bf16[8,8,3072]{2,1,0:T(8,128)(2,1)}, bf16[8,8,3072]{2,1,0:T(8,128)(2,1)S(1)}, u32[]{:S(2)}) copy-start(bf16[8,8,3072]{2,1,0:T(8,128)(2,1)S(1)} %collective-permute-done.8.refs_11_) | copy-start | bytes 1179652
  33.8 12.7 %collective-permute-start.26 = (bf16[8,8,3072]{2,1,0:T(8,128)(2,1)S(1)}, bf16[8,8,3072]{2,1,0:T(8,128)(2,1)S(1)}, u32[]{:S(2)}, u32[]{:S(2)}) collective-permute-start(bf16[8,8,3072]{2,1,0:T(8,128)(2,1)S(1)} %collective-permute-done.8.refs_11_), channel_id=1, source_target_pairs={{0,32},{1,33},{2,34},{3,35},{4,36},{5,37},{6,38},{7,39},{8,40},{9,... | collective-permute-start | bytes 1179656 | tf_op jit(solution)/shard_map/ppermute | solution.py:42
  33.9 11.6 %copy-start.7 = (bf16[8,8,3072]{2,1,0:T(8,128)(2,1)}, bf16[8,8,3072]{2,1,0:T(8,128)(2,1)S(1)}, u32[]{:S(2)}) copy-start(bf16[8,8,3072]{2,1,0:T(8,128)(2,1)S(1)} %collective-permute-done.27.refs_19_) | copy-start | bytes 1179652
  34.0 20.4 %collective-permute-start.22 = (bf16[8,8,3072]{2,1,0:T(8,128)(2,1)S(1)}, bf16[8,8,3072]{2,1,0:T(8,128)(2,1)}, u32[]{:S(2)}, u32[]{:S(2)}) collective-permute-start(bf16[8,8,3072]{2,1,0:T(8,128)(2,1)S(1)} %collective-permute-done.8.refs_11_), channel_id=1, source_target_pairs={{0,8},{1,9},{2,10},{3,11},{4,12},{5,13},{6,14},{7,15},{8,16},{9,17... | collective-permute-start | bytes 1179656 | tf_op jit(solution)/shard_map/ppermute | solution.py:42
  42.5 23.5 %copy-start.8 = (bf16[8,8,3072]{2,1,0:T(8,128)(2,1)}, bf16[8,8,3072]{2,1,0:T(8,128)(2,1)S(1)}, u32[]{:S(2)}) copy-start(bf16[8,8,3072]{2,1,0:T(8,128)(2,1)S(1)} %collective-permute-done.23.refs_14_) | copy-start | bytes 1179652
  42.5 12.2 %collective-permute-start.9 = (bf16[8,8,3072]{2,1,0:T(8,128)(2,1)S(1)}, bf16[8,8,3072]{2,1,0:T(8,128)(2,1)S(1)}, u32[]{:S(2)}, u32[]{:S(2)}) collective-permute-start(bf16[8,8,3072]{2,1,0:T(8,128)(2,1)S(1)} %collective-permute-done.8.refs_11_), channel_id=1, source_target_pairs={{0,24},{1,25},{2,26},{3,27},{4,28},{5,29},{6,30},{7,31},{8,0},{9,1... | collective-permute-start | bytes 1179656 | tf_op jit(solution)/shard_map/ppermute | solution.py:42
  46.5 21.2 %copy-start.4 = (bf16[8,8,3072]{2,1,0:T(8,128)(2,1)}, bf16[8,8,3072]{2,1,0:T(8,128)(2,1)S(1)}, u32[]{:S(2)}) copy-start(bf16[8,8,3072]{2,1,0:T(8,128)(2,1)S(1)} %collective-permute-done.7.refs_1_.refs_12_) | copy-start | bytes 1179652
  46.5 52.9 %collective-permute-start.12 = (bf16[2,8,16,3072]{3,2,1,0:T(8,128)(2,1)}, bf16[2,8,16,3072]{3,2,1,0:T(8,128)(2,1)S(1)}, u32[]{:S(2)}, u32[]{:S(2)}) collective-permute-start(bf16[2,8,16,3072]{3,2,1,0:T(8,128)(2,1)} %get-tuple-element.20.refs_5_), channel_id=1, source_target_pairs={{0,32},{1,33},{2,34},{3,35},{4,36},{5,37},{6,38},{7,39},{8,40},{9,... | collective-permute-start | bytes 4718600 | tf_op jit(solution)/shard_map/ppermute | solution.py:42
  46.5 19.5 %copy-start.9 = (bf16[8,8,3072]{2,1,0:T(8,128)(2,1)}, bf16[8,8,3072]{2,1,0:T(8,128)(2,1)S(1)}, u32[]{:S(2)}) copy-start(bf16[8,8,3072]{2,1,0:T(8,128)(2,1)S(1)} %collective-permute-done.26.refs_18_) | copy-start | bytes 1179652
  46.5 8.2 %collective-permute-start.31 = (bf16[8,8,3072]{2,1,0:T(8,128)(2,1)S(1)}, bf16[8,8,3072]{2,1,0:T(8,128)(2,1)S(1)}, u32[]{:S(2)}, u32[]{:S(2)}) collective-permute-start(bf16[8,8,3072]{2,1,0:T(8,128)(2,1)S(1)} %collective-permute-done.23.refs_14_), channel_id=1, source_target_pairs={{0,32},{1,33},{2,34},{3,35},{4,36},{5,37},{6,38},{7,39},{8,40},{9,... | collective-permute-start | bytes 1179656 | tf_op jit(solution)/shard_map/ppermute | solution.py:42
  54.3 1.7 collective-permute-start.29
  54.7 13.0 %copy-start.5 = (bf16[8,8,3072]{2,1,0:T(8,128)(2,1)}, bf16[8,8,3072]{2,1,0:T(8,128)(2,1)S(1)}, u32[]{:S(2)}) copy-start(bf16[8,8,3072]{2,1,0:T(8,128)(2,1)S(1)} %collective-permute-done.9.refs_2_.refs_15_) | copy-start | bytes 1179652
  54.7 11.3 %collective-permute-start.24 = (bf16[8,8,3072]{2,1,0:T(8,128)(2,1)S(1)}, bf16[8,8,3072]{2,1,0:T(8,128)(2,1)S(1)}, u32[]{:S(2)}, u32[]{:S(2)}) collective-permute-start(bf16[8,8,3072]{2,1,0:T(8,128)(2,1)S(1)} %collective-permute-done.7.refs_1_.refs_12_), channel_id=1, source_target_pairs={{0,8},{1,9},{2,10},{3,11},{4,12},{5,13},{6,14},{7,15},{8,16},{9,17... | collective-permute-start | bytes 1179656 | tf_op jit(solution)/shard_map/ppermute | solution.py:42
  54.7 11.3 %copy-start.10 = (bf16[8,8,3072]{2,1,0:T(8,128)(2,1)}, bf16[8,8,3072]{2,1,0:T(8,128)(2,1)S(1)}, u32[]{:S(2)}) copy-start(bf16[8,8,3072]{2,1,0:T(8,128)(2,1)S(1)} %collective-permute-done.31.refs_23_) | copy-start | bytes 1179652
  54.8 15.3 %collective-permute-start.28 = (bf16[8,8,3072]{2,1,0:T(8,128)(2,1)}, bf16[8,8,3072]{2,1,0:T(8,128)(2,1)}, u32[]{:S(2)}, u32[]{:S(2)}) collective-permute-start(bf16[8,8,3072]{2,1,0:T(8,128)(2,1)} %collective-permute-done.22.refs_13_), channel_id=1, source_target_pairs={{0,32},{1,33},{2,34},{3,35},{4,36},{5,37},{6,38},{7,39},{8,40},{9,... | collective-permute-start | bytes 1179656 | tf_op jit(solution)/shard_map/ppermute | solution.py:42
  56.1 15.5 %collective-permute-start.30 = (bf16[8,8,3072]{2,1,0:T(8,128)(2,1)S(1)}, bf16[8,8,3072]{2,1,0:T(8,128)(2,1)}, u32[]{:S(2)}, u32[]{:S(2)}) collective-permute-start(bf16[8,8,3072]{2,1,0:T(8,128)(2,1)S(1)} %collective-permute-done.9.refs_2_.refs_15_), channel_id=1, source_target_pairs={{0,32},{1,33},{2,34},{3,35},{4,36},{5,37},{6,38},{7,39},{8,40},{9,... | collective-permute-start | bytes 1179656 | tf_op jit(solution)/shard_map/ppermute | solution.py:42
  66.8 12.7 %collective-permute-start.25 = (bf16[8,8,3072]{2,1,0:T(8,128)(2,1)S(1)}, bf16[8,8,3072]{2,1,0:T(8,128)(2,1)}, u32[]{:S(2)}, u32[]{:S(2)}) collective-permute-start(bf16[8,8,3072]{2,1,0:T(8,128)(2,1)S(1)} %collective-permute-done.9.refs_2_.refs_15_), channel_id=1, source_target_pairs={{0,24},{1,25},{2,26},{3,27},{4,28},{5,29},{6,30},{7,31},{8,0},{9,1... | collective-permute-start | bytes 1179656 | tf_op jit(solution)/shard_map/ppermute | solution.py:42
  70.0 15.9 %collective-permute-start.18 = (bf16[2,32,8,512]{3,2,1,0:T(8,128)(2,1)}, bf16[2,32,8,512]{3,2,1,0:T(8,128)(2,1)}, u32[]{:S(2)}, u32[]{:S(2)}) collective-permute-start(bf16[2,32,8,512]{3,2,1,0:T(8,128)(2,1)} %get-tuple-element.31), channel_id=1, source_target_pairs={{0,31},{1,0},{2,1},{3,2},{4,3},{5,4},{6,5},{7,6},{8,7},{9,8},{10,9... | collective-permute-start | bytes 1572872 | tf_op jit(solution)/shard_map/ppermute | solution.py:46
  71.6 17.0 %collective-permute-start.17 = (bf16[2,32,8,512]{3,2,1,0:T(8,128)(2,1)}, bf16[2,32,8,512]{3,2,1,0:T(8,128)(2,1)}, u32[]{:S(2)}, u32[]{:S(2)}) collective-permute-start(bf16[2,32,8,512]{3,2,1,0:T(8,128)(2,1)} %get-tuple-element.23.refs_1_), channel_id=1, source_target_pairs={{0,1},{1,2},{2,3},{3,4},{4,5},{5,6},{6,7},{7,8},{8,9},{9,10},{10,1... | collective-permute-start | bytes 1572872 | tf_op jit(solution)/shard_map/ppermute | solution.py:46
  71.6 14.2 %collective-permute-start.33 = (bf16[8,8,3072]{2,1,0:T(8,128)(2,1)}, bf16[8,8,3072]{2,1,0:T(8,128)(2,1)S(1)}, u32[]{:S(2)}, u32[]{:S(2)}) collective-permute-start(bf16[8,8,3072]{2,1,0:T(8,128)(2,1)} %copy-done.12), channel_id=1, source_target_pairs={{0,32},{1,33},{2,34},{3,35},{4,36},{5,37},{6,38},{7,39},{8,40},{9,... | collective-permute-start | bytes 1179656 | tf_op jit(solution)/shard_map/ppermute | solution.py:42
  79.6 26.3 %collective-permute-start.21 = (bf16[2,8,8,3072]{3,2,1,0:T(8,128)(2,1)}, bf16[2,8,8,3072]{3,2,1,0:T(8,128)(2,1)S(1)}, u32[]{:S(2)}, u32[]{:S(2)}) collective-permute-start(bf16[2,8,8,3072]{3,2,1,0:T(8,128)(2,1)} %get-tuple-element.32), channel_id=1, source_target_pairs={{32,63},{33,32},{34,33},{35,34},{36,35},{37,36},{38,37},{39,38},{4... | collective-permute-start | bytes 2359304 | tf_op jit(solution)/shard_map/ppermute | solution.py:33
  85.8 18.0 %collective-permute-start.32 = (bf16[8,8,3072]{2,1,0:T(8,128)(2,1)}, bf16[8,8,3072]{2,1,0:T(8,128)(2,1)}, u32[]{:S(2)}, u32[]{:S(2)}) collective-permute-start(bf16[8,8,3072]{2,1,0:T(8,128)(2,1)} %collective-permute-done.25.refs_17_), channel_id=1, source_target_pairs={{0,32},{1,33},{2,34},{3,35},{4,36},{5,37},{6,38},{7,39},{8,40},{9,... | collective-permute-start | bytes 1179656 | tf_op jit(solution)/shard_map/ppermute | solution.py:42
  86.0 53.0 %collective-permute-start.15 = (bf16[2,32,8,1024]{3,2,1,0:T(8,128)(2,1)}, bf16[2,32,8,1024]{3,2,1,0:T(8,128)(2,1)}, u32[]{:S(2)}, u32[]{:S(2)}) collective-permute-start(bf16[2,32,8,1024]{3,2,1,0:T(8,128)(2,1)} %get-tuple-element.24.refs_1_), channel_id=1, source_target_pairs={{0,1},{1,2},{2,3},{3,4},{4,5},{5,6},{6,7},{7,8},{8,9},{9,10},{10,1... | collective-permute-start | bytes 3145736 | tf_op jit(solution)/shard_map/ppermute | solution.py:46
  88.6 50.3 %collective-permute-start.16 = (bf16[2,32,8,1024]{3,2,1,0:T(8,128)(2,1)}, bf16[2,32,8,1024]{3,2,1,0:T(8,128)(2,1)}, u32[]{:S(2)}, u32[]{:S(2)}) collective-permute-start(bf16[2,32,8,1024]{3,2,1,0:T(8,128)(2,1)} %get-tuple-element.30), channel_id=1, source_target_pairs={{0,31},{1,0},{2,1},{3,2},{4,3},{5,4},{6,5},{7,6},{8,7},{9,8},{10,9... | collective-permute-start | bytes 3145736 | tf_op jit(solution)/shard_map/ppermute | solution.py:46
  95.3 16.6 %copy-start.27 = (pred[128]{0:T(512)(128)(4,1)S(1)}, pred[128]{0:T(512)(128)(4,1)}, u32[]{:S(2)}) copy-start(pred[128]{0:T(512)(128)(4,1)} %iota_compare_fusion) | copy-start | bytes 388
  99.4 30.5 %copy-start.1 = (bf16[2,8,16,3072]{3,2,1,0:T(8,128)(2,1)}, bf16[2,8,16,3072]{3,2,1,0:T(8,128)(2,1)S(1)}, u32[]{:S(2)}) copy-start(bf16[2,8,16,3072]{3,2,1,0:T(8,128)(2,1)S(1)} %collective-permute-done.12.refs_5_) | copy-start | bytes 4718596
  99.4 6.5 %collective-permute-start.19 = (bf16[2,2,8,8,512]{4,3,2,1,0:T(8,128)(2,1)}, bf16[2,2,8,8,512]{4,3,2,1,0:T(8,128)(2,1)S(1)}, u32[]{:S(2)}, u32[]{:S(2)}) collective-permute-start(bf16[2,2,8,8,512]{4,3,2,1,0:T(8,128)(2,1)} %shard_map.54), channel_id=1, source_target_pairs={{0,32},{1,33},{2,34},{3,35},{4,36},{5,37},{6,38},{7,39},{8,40},{9,... | collective-permute-start | bytes 786440 | tf_op jit(solution)/shard_map/ppermute | solution.py:42
  103.8 26.0 %collective-permute-start.20 = (bf16[2,8,8,3072]{3,2,1,0:T(8,128)(2,1)}, bf16[2,8,8,3072]{3,2,1,0:T(8,128)(2,1)S(1)}, u32[]{:S(2)}, u32[]{:S(2)}) collective-permute-start(bf16[2,8,8,3072]{3,2,1,0:T(8,128)(2,1)} %get-tuple-element.25.refs_1_), channel_id=1, source_target_pairs={{32,33},{33,34},{34,35},{35,36},{36,37},{37,38},{38,39},{39,40},{4... | collective-permute-start | bytes 2359304 | tf_op jit(solution)/shard_map/ppermute | solution.py:33
  105.8 24.0 %copy-start.19 = (bf16[2,2,8,8,512]{4,3,2,1,0:T(8,128)(2,1)}, bf16[2,2,8,8,512]{4,3,2,1,0:T(8,128)(2,1)S(1)}, u32[]{:S(2)}) copy-start(bf16[2,2,8,8,512]{4,3,2,1,0:T(8,128)(2,1)S(1)} %collective-permute-done.19.refs_7_) | copy-start | bytes 786436
  105.8 51.3 %collective-permute-start.13 = (bf16[2,32,8,1024]{3,2,1,0:T(8,128)(2,1)}, bf16[2,32,8,1024]{3,2,1,0:T(8,128)(2,1)}, u32[]{:S(2)}, u32[]{:S(2)}) collective-permute-start(bf16[2,32,8,1024]{3,2,1,0:T(8,128)(2,1)} %get-tuple-element.26.refs_1_), channel_id=1, source_target_pairs={{0,1},{1,2},{2,3},{3,4},{4,5},{5,6},{6,7},{7,8},{8,9},{9,10},{10,1... | collective-permute-start | bytes 3145736 | tf_op jit(solution)/shard_map/ppermute | solution.py:46
  105.9 23.9 %copy-start.2 = (bf16[2,8,8,3072]{3,2,1,0:T(8,128)(2,1)}, bf16[2,8,8,3072]{3,2,1,0:T(8,128)(2,1)S(1)}, u32[]{:S(2)}) copy-start(bf16[2,8,8,3072]{3,2,1,0:T(8,128)(2,1)S(1)} %collective-permute-done.21.refs_9_) | copy-start | bytes 2359300
  105.9 51.1 %collective-permute-start.14 = (bf16[2,32,8,1024]{3,2,1,0:T(8,128)(2,1)}, bf16[2,32,8,1024]{3,2,1,0:T(8,128)(2,1)}, u32[]{:S(2)}, u32[]{:S(2)}) collective-permute-start(bf16[2,32,8,1024]{3,2,1,0:T(8,128)(2,1)} %get-tuple-element.29), channel_id=1, source_target_pairs={{0,31},{1,0},{2,1},{3,2},{4,3},{5,4},{6,5},{7,6},{8,7},{9,8},{10,9... | collective-permute-start | bytes 3145736 | tf_op jit(solution)/shard_map/ppermute | solution.py:46
  141.0 2.1 %collective-permute-start.34 = (bf16[2,2,8,8,1024]{4,3,2,1,0:T(8,128)(2,1)}, bf16[2,2,8,8,1024]{4,3,2,1,0:T(8,128)(2,1)S(1)}, u32[]{:S(2)}, u32[]{:S(2)}) collective-permute-start(bf16[2,2,8,8,1024]{4,3,2,1,0:T(8,128)(2,1)} %shard_map.56), channel_id=1, source_target_pairs={{0,32},{1,33},{2,34},{3,35},{4,36},{5,37},{6,38},{7,39},{8,40},{9,... | collective-permute-start | bytes 1572872 | tf_op jit(solution)/shard_map/ppermute | solution.py:42
  159.2 2.1 %collective-permute-start.35 = (bf16[2,2,8,8,1024]{4,3,2,1,0:T(8,128)(2,1)}, bf16[2,2,8,8,1024]{4,3,2,1,0:T(8,128)(2,1)S(1)}, u32[]{:S(2)}, u32[]{:S(2)}) collective-permute-start(bf16[2,2,8,8,1024]{4,3,2,1,0:T(8,128)(2,1)} %shard_map.58), channel_id=1, source_target_pairs={{0,32},{1,33},{2,34},{3,35},{4,36},{5,37},{6,38},{7,39},{8,40},{9,... | collective-permute-start | bytes 1572872 | tf_op jit(solution)/shard_map/ppermute | solution.py:42
  159.4 16.0 %collective-permute-start.11 = (bf16[2,32,8,512]{3,2,1,0:T(8,128)(2,1)S(1)}, bf16[2,32,8,512]{3,2,1,0:T(8,128)(2,1)S(1)}, u32[]{:S(2)}, u32[]{:S(2)}) collective-permute-start(bf16[2,32,8,512]{3,2,1,0:T(8,128)(2,1)S(1)} %copy-done.28), channel_id=1, source_target_pairs={{0,31},{1,0},{2,1},{3,2},{4,3},{5,4},{6,5},{7,6},{8,7},{9,8},{10,9... | collective-permute-start | bytes 1572872 | tf_op jit(solution)/shard_map/ppermute | solution.py:46
  159.4 17.6 %collective-permute-start.10 = (bf16[2,32,8,512]{3,2,1,0:T(8,128)(2,1)S(1)}, bf16[2,32,8,512]{3,2,1,0:T(8,128)(2,1)S(1)}, u32[]{:S(2)}, u32[]{:S(2)}) collective-permute-start(bf16[2,32,8,512]{3,2,1,0:T(8,128)(2,1)S(1)} %copy-done.18), channel_id=1, source_target_pairs={{0,1},{1,2},{2,3},{3,4},{4,5},{5,6},{6,7},{7,8},{8,9},{9,10},{10,1... | collective-permute-start | bytes 1572872 | tf_op jit(solution)/shard_map/ppermute | solution.py:46
  179.6 2.6 %collective-permute-start.36 = (bf16[2,2,8,8,512]{4,3,2,1,0:T(8,128)(2,1)}, bf16[2,2,8,8,512]{4,3,2,1,0:T(8,128)(2,1)S(1)}, u32[]{:S(2)}, u32[]{:S(2)}) collective-permute-start(bf16[2,2,8,8,512]{4,3,2,1,0:T(8,128)(2,1)} %shard_map.60), channel_id=1, source_target_pairs={{0,32},{1,33},{2,34},{3,35},{4,36},{5,37},{6,38},{7,39},{8,40},{9,... | collective-permute-start | bytes 786440 | tf_op jit(solution)/shard_map/ppermute | solution.py:42
  (18 other events, 46.9 us)

commit v3 on v2

--- a/solution.py
+++ b/solution.py
@@ -18,7 +18,7 @@
 PER_STEP = 4
 WIDE = PER_STEP * HD
 BLOCK = 16
-VMEM_LIMIT = 60 << 20
+VMEM_LIMIT = 66_800_000
 PIECES = 8
 
 

time: 194 us -> 192 us (0.990)
  local copies, waits for them, and re-layouts: 6.1 us -> 1.4 us
  waiting for transfers between devices: 60.1 us -> 63.3 us
    ppermute x3, waiting for transfers between devices: 17 us -> 22 us  [send_where(): return lax.ppermute(x, ('lat', 'lon'), pairs)]
    unnamed x58 -> x24, local copies, waits for them, and re-layouts: 6.1 us -> 1.4 us
    ppermute x8, starting transfers between devices: 12.5 us -> 15.2 us  [send_lon(): lax.ppermute(x, 'lon', [(i, (i + step) % N_LON) for i in range(N_LON)])]
    ppermute x26, starting transfers between devices: 28.5 us -> 26.1 us  [send(): return lax.ppermute(x, ('lat', 'lon'), pairs)]
  transfers between devices with their start and end apart: 37 -> 37, of which waited for: 16 -> 15; matrix products, arithmetic and copies ran while one was open for 1% -> 1% of each run, Pallas kernels for 29% -> 29%
where the time goes in v3:
time: 192 us; the launch traced here: 191 us
  Pallas kernels  71.1 us (37%)
  waiting for transfers between devices  63.3 us (33%)
  starting transfers between devices  53.3 us (28%)
    pallas_call x4, Pallas kernels, attend(): pl.pallas_call(functools.partial(attend_body, len(deps) + (output is not...  42.6 us
    ppermute x26, waiting for transfers between devices, send(): return lax.ppermute(x, ('lat', 'lon'), pairs)  37.7 us
    pallas_call x12, Pallas kernels, glue(): pl.pallas_call(kernel, grid=grid or (), in_specs=list(specs) + [pl.BlockS...  28.5 us
    ppermute x26, starting transfers between devices, send(): return lax.ppermute(x, ('lat', 'lon'), pairs)  26.1 us
    ppermute x3, waiting for transfers between devices, send_where(): return lax.ppermute(x, ('lat', 'lon'), pairs)  22 us
    ppermute x8, starting transfers between devices, send_lon(): lax.ppermute(x, 'lon', [(i, (i + step) % N_LON) for i in range(N_LON)])  15.2 us
    ppermute x3, starting transfers between devices, send_where(): return lax.ppermute(x, ('lat', 'lon'), pairs)  12 us
  transfers between devices with their start and end apart: 37, of which 15 were waited for; matrix products, arithmetic and copies ran while one was open for 1% of the time, Pallas kernels for 29%

profile of v3, /device:TPU:1, one launch (start us, length us, event | category | flops | bytes accessed | tf_op | source)
XLA Modules:
  0.0 190.5 jit_solution(18197949214672331254)
XLA Ops:
  0.0 4.4 %collective-permute-start.1 = (bf16[2,1,4,3072]{3,2,1,0:T(4,128)(2,1)}, bf16[2,1,4,3072]{3,2,1,0:T(4,128)(2,1)S(1)}, u32[]{:S(2)}, u32[]{:S(2)}) collective-permute-start(bf16[2,1,4,3072]{3,2,1,0:T(4,128)(2,1)} %refs_0_.5), channel_id=1, source_target_pairs={{0,64},{1,65},{2,66},{3,67},{4,68},{5,69},{6,70},{7,71},{8,72},{9,... | collective-permute-start | bytes 147464 | tf_op jit(solution)/shard_map/ppermute | solution.py:42
  5.2 0.9 collective-permute-done.1.refs_2_
  6.1 1.7 collective-permute-done.refs_1_
  7.8 1.7 collective-permute-done.2.refs_3_
  10.2 1.6 shard_map.46.refs_3_.refs_1_
  11.7 2.9 %collective-permute-start.6 = (bf16[4,2,4,3072]{3,2,1,0:T(4,128)(2,1)}, bf16[4,2,4,3072]{3,2,1,0:T(4,128)(2,1)S(1)}, u32[]{:S(2)}, u32[]{:S(2)}) collective-permute-start(bf16[4,2,4,3072]{3,2,1,0:T(4,128)(2,1)} %shard_map.46.refs_3_.refs_1_), channel_id=1, source_target_pairs={{0,2},{1,3},{2,0},{3,1},{4,6},{5,7},{6,4},{7,5},{8,10},{9,11},{10,... | collective-permute-start | bytes 589832 | tf_op jit(solution)/shard_map/ppermute | solution.py:42
  16.1 4.5 %shard_map.47 = (bf16[2,8,16,3072]{3,2,1,0:T(8,128)(2,1)}, bf16[2,8,16,3072]{3,2,1,0:T(8,128)(2,1)}) custom-call(s32[1]{0:T(128)} %bitcast.refs_0_, bf16[2,1,32,16,3072]{4,3,2,1,0:T(8,128)(2,1)} %refs_2_.9, bf16[2,1,32,16,3072]{4,3,2,1,0:T(8,128)(2,1)} %refs_2_.9, bf16[4,2,4,3072]{3,2,1,0:T(4,128)(2,1)} %shard_map.46.refs_3_.refs_1_), custom_call_target="tpu_custom_call" | custom-call | flops 1000 | bytes 1000 | tf_op jit(solution)/shard_map/pallas_call | solution.py:58
  20.6 2.0 %collective-permute-done.5.refs_3_ = bf16[4,2,4,3072]{3,2,1,0:T(4,128)(2,1)} collective-permute-done((bf16[4,2,4,3072]{3,2,1,0:T(4,128)(2,1)}, bf16[4,2,4,3072]{3,2,1,0:T(4,128)(2,1)}, u32[]{:S(2)}, u32[]{:S(2)}) %collective-permute-start.5) | collective-permute-done | bytes 196640 | tf_op jit(solution)/shard_map/ppermute | solution.py:42
  22.5 1.4 collective-permute-done.4.refs_2_
  24.0 2.4 %shard_map.48 = (bf16[8,8,3072]{2,1,0:T(8,128)(2,1)}, bf16[8,8,3072]{2,1,0:T(8,128)(2,1)}) custom-call(s32[1]{0:T(128)} %bitcast.refs_0_, bf16[4,2,4,3072]{3,2,1,0:T(4,128)(2,1)} %shard_map.46.refs_3_.refs_1_, bf16[4,2,4,3072]{3,2,1,0:T(4,128)(2,1)} %collective-permute-done.4.refs_2_, bf16[4,2,4,3072]{3,2,1,0:T(4,128)(2,1)} %collective-permute-done.5.refs_3_, ...), custom_call_target="tpu_custom_call" | custom-call | flops 1000 | bytes 1000 | tf_op jit(solution)/shard_map/pallas_call | solution.py:58
  26.3 2.1 %collective-permute-start.8 = (bf16[8,8,3072]{2,1,0:T(8,128)(2,1)}, bf16[8,8,3072]{2,1,0:T(8,128)(2,1)S(1)}, u32[]{:S(2)}, u32[]{:S(2)}) collective-permute-start(bf16[8,8,3072]{2,1,0:T(8,128)(2,1)} %get-tuple-element.22), channel_id=1, source_target_pairs={{0,32},{1,33},{2,34},{3,35},{4,36},{5,37},{6,38},{7,39},{8,40},{9,... | collective-permute-start | bytes 1179656 | tf_op jit(solution)/shard_map/ppermute | solution.py:42
  28.4 2.3 %collective-permute-start.3 = (bf16[2,8,16,3072]{3,2,1,0:T(8,128)(2,1)}, bf16[2,8,16,3072]{3,2,1,0:T(8,128)(2,1)}, u32[]{:S(2)}, u32[]{:S(2)}) collective-permute-start(bf16[2,8,16,3072]{3,2,1,0:T(8,128)(2,1)} %get-tuple-element.19), channel_id=1, source_target_pairs={{32,64},{33,65},{34,66},{35,67},{36,68},{37,69},{38,70},{39,71},{4... | collective-permute-start | bytes 4718600 | tf_op jit(solution)/shard_map/ppermute | solution.py:33
  30.7 2.5 %collective-permute-start.23 = (bf16[8,8,3072]{2,1,0:T(8,128)(2,1)}, bf16[8,8,3072]{2,1,0:T(8,128)(2,1)S(1)}, u32[]{:S(2)}, u32[]{:S(2)}) collective-permute-start(bf16[8,8,3072]{2,1,0:T(8,128)(2,1)} %get-tuple-element.21.refs_10_), channel_id=1, source_target_pairs={{0,24},{1,25},{2,26},{3,27},{4,28},{5,29},{6,30},{7,31},{8,0},{9,1... | collective-permute-start | bytes 1179656 | tf_op jit(solution)/shard_map/ppermute | solution.py:42
  34.0 8.1 %collective-permute-done.23.refs_14_ = bf16[8,8,3072]{2,1,0:T(8,128)(2,1)S(1)} collective-permute-done((bf16[8,8,3072]{2,1,0:T(8,128)(2,1)}, bf16[8,8,3072]{2,1,0:T(8,128)(2,1)S(1)}, u32[]{:S(2)}, u32[]{:S(2)}) %collective-permute-start.23) | collective-permute-done | bytes 393248 | tf_op jit(solution)/shard_map/ppermute | solution.py:42
  42.2 3.3 %collective-permute-start.9 = (bf16[8,8,3072]{2,1,0:T(8,128)(2,1)S(1)}, bf16[8,8,3072]{2,1,0:T(8,128)(2,1)}, u32[]{:S(2)}, u32[]{:S(2)}) collective-permute-start(bf16[8,8,3072]{2,1,0:T(8,128)(2,1)S(1)} %collective-permute-done.8.refs_11_), channel_id=1, source_target_pairs={{0,24},{1,25},{2,26},{3,27},{4,28},{5,29},{6,30},{7,31},{8,0},{9,1... | collective-permute-start | bytes 1179656 | tf_op jit(solution)/shard_map/ppermute | solution.py:42
  45.5 1.4 collective-permute-start.12
  47.0 6.7 %collective-permute-done.22.refs_13_ = bf16[8,8,3072]{2,1,0:T(8,128)(2,1)} collective-permute-done((bf16[8,8,3072]{2,1,0:T(8,128)(2,1)S(1)}, bf16[8,8,3072]{2,1,0:T(8,128)(2,1)}, u32[]{:S(2)}, u32[]{:S(2)}) %collective-permute-start.22) | collective-permute-done | bytes 393248 | tf_op jit(solution)/shard_map/ppermute | solution.py:42
  53.7 1.1 collective-permute-start.29
  54.9 1.2 collective-permute-done.29.refs_21_
  56.5 9.6 %collective-permute-done.24.refs_16_ = bf16[8,8,3072]{2,1,0:T(8,128)(2,1)S(1)} collective-permute-done((bf16[8,8,3072]{2,1,0:T(8,128)(2,1)S(1)}, bf16[8,8,3072]{2,1,0:T(8,128)(2,1)S(1)}, u32[]{:S(2)}, u32[]{:S(2)}) %collective-permute-start.24) | collective-permute-done | bytes 393248 | tf_op jit(solution)/shard_map/ppermute | solution.py:42
  66.8 2.2 %shard_map.49 = (bf16[2,32,8,512]{3,2,1,0:T(8,128)(2,1)}, bf16[2,32,8,512]{3,2,1,0:T(8,128)(2,1)}) custom-call(bf16[2,1,32,16,3072]{4,3,2,1,0:T(8,128)(2,1)} %refs_2_.9, bf16[8,8,3072]{2,1,0:T(8,128)(2,1)} %copy-done, bf16[8,8,3072]{2,1,0:T(8,128)(2,1)} %collective-permute-done.9.refs_2_.refs_15_), custom_call_target="tpu_custom_call" | custom-call | flops 1000 | bytes 1000 | tf_op jit(solution)/shard_map/pallas_call | solution.py:58
  69.1 2.8 %collective-permute-start.18 = (bf16[2,32,8,512]{3,2,1,0:T(8,128)(2,1)}, bf16[2,32,8,512]{3,2,1,0:T(8,128)(2,1)}, u32[]{:S(2)}, u32[]{:S(2)}) collective-permute-start(bf16[2,32,8,512]{3,2,1,0:T(8,128)(2,1)} %get-tuple-element.31), channel_id=1, source_target_pairs={{0,31},{1,0},{2,1},{3,2},{4,3},{5,4},{6,5},{7,6},{8,7},{9,8},{10,9... | collective-permute-start | bytes 1572872 | tf_op jit(solution)/shard_map/ppermute | solution.py:46
  71.9 1.9 %collective-permute-start.33 = (bf16[8,8,3072]{2,1,0:T(8,128)(2,1)}, bf16[8,8,3072]{2,1,0:T(8,128)(2,1)}, u32[]{:S(2)}, u32[]{:S(2)}) collective-permute-start(bf16[8,8,3072]{2,1,0:T(8,128)(2,1)} %copy-done.7), channel_id=1, source_target_pairs={{0,32},{1,33},{2,34},{3,35},{4,36},{5,37},{6,38},{7,39},{8,40},{9,... | collective-permute-start | bytes 1179656 | tf_op jit(solution)/shard_map/ppermute | solution.py:42
  73.9 2.7 %shard_map.50 = (bf16[2,32,8,1024]{3,2,1,0:T(8,128)(2,1)}, bf16[2,32,8,1024]{3,2,1,0:T(8,128)(2,1)}) custom-call(bf16[2,1,32,16,3072]{4,3,2,1,0:T(8,128)(2,1)} %refs_2_.9, bf16[2,32,8,512]{3,2,1,0:T(8,128)(2,1)} %get-tuple-element.23.refs_1_), custom_call_target="tpu_custom_call" | custom-call | flops 1000 | bytes 1000 | tf_op jit(solution)/shard_map/pallas_call | solution.py:58
  76.6 2.6 %shard_map.51 = (bf16[2,8,8,3072]{3,2,1,0:T(8,128)(2,1)}, bf16[2,8,8,3072]{3,2,1,0:T(8,128)(2,1)}) custom-call(bf16[2,8,16,3072]{3,2,1,0:T(8,128)(2,1)} %collective-permute-done.3.refs_0_.refs_6_, bf16[2,32,8,1024]{3,2,1,0:T(8,128)(2,1)} %get-tuple-element.24.refs_1_), custom_call_target="tpu_custom_call" | custom-call | flops 1000 | bytes 1000 | tf_op jit(solution)/shard_map/pallas_call | solution.py:58
  79.2 7.8 %collective-permute-start.21 = (bf16[2,8,8,3072]{3,2,1,0:T(8,128)(2,1)}, bf16[2,8,8,3072]{3,2,1,0:T(8,128)(2,1)}, u32[]{:S(2)}, u32[]{:S(2)}) collective-permute-start(bf16[2,8,8,3072]{3,2,1,0:T(8,128)(2,1)} %get-tuple-element.32), channel_id=1, source_target_pairs={{32,63},{33,32},{34,33},{35,34},{36,35},{37,36},{38,37},{39,38},{4... | collective-permute-start | bytes 2359304 | tf_op jit(solution)/shard_map/ppermute | solution.py:33
  87.2 0.8 collective-permute-done.17.refs_1_.refs_2_.refs_3_
  88.0 4.8 %collective-permute-start.16 = (bf16[2,32,8,1024]{3,2,1,0:T(8,128)(2,1)}, bf16[2,32,8,1024]{3,2,1,0:T(8,128)(2,1)}, u32[]{:S(2)}, u32[]{:S(2)}) collective-permute-start(bf16[2,32,8,1024]{3,2,1,0:T(8,128)(2,1)} %get-tuple-element.30), channel_id=1, source_target_pairs={{0,31},{1,0},{2,1},{3,2},{4,3},{5,4},{6,5},{7,6},{8,7},{9,8},{10,9... | collective-permute-start | bytes 3145736 | tf_op jit(solution)/shard_map/ppermute | solution.py:46
  92.9 2.6 %shard_map.52 = (bf16[2,32,8,1024]{3,2,1,0:T(8,128)(2,1)}, bf16[2,32,8,1024]{3,2,1,0:T(8,128)(2,1)}) custom-call(bf16[2,1,32,16,3072]{4,3,2,1,0:T(8,128)(2,1)} %refs_2_.9, bf16[2,8,8,3072]{3,2,1,0:T(8,128)(2,1)} %get-tuple-element.25.refs_1_), custom_call_target="tpu_custom_call" | custom-call | flops 1000 | bytes 1000 | tf_op jit(solution)/shard_map/pallas_call | solution.py:58
  95.5 2.2 %shard_map.53 = (bf16[2,32,8,512]{3,2,1,0:T(8,128)(2,1)}, bf16[2,32,8,512]{3,2,1,0:T(8,128)(2,1)}) custom-call(bf16[2,1,32,16,3072]{4,3,2,1,0:T(8,128)(2,1)} %refs_2_.9, bf16[2,32,8,1024]{3,2,1,0:T(8,128)(2,1)} %get-tuple-element.26.refs_1_), custom_call_target="tpu_custom_call" | custom-call | flops 1000 | bytes 1000 | tf_op jit(solution)/shard_map/pallas_call | solution.py:58
  97.7 1.8 shard_map.54
  99.6 1.6 collective-permute-start.19
  101.1 1.9 %collective-permute-start.20 = (bf16[2,8,8,3072]{3,2,1,0:T(8,128)(2,1)}, bf16[2,8,8,3072]{3,2,1,0:T(8,128)(2,1)}, u32[]{:S(2)}, u32[]{:S(2)}) collective-permute-start(bf16[2,8,8,3072]{3,2,1,0:T(8,128)(2,1)} %get-tuple-element.25.refs_1_), channel_id=1, source_target_pairs={{32,33},{33,34},{34,35},{35,36},{36,37},{37,38},{38,39},{39,40},{4... | collective-permute-start | bytes 2359304 | tf_op jit(solution)/shard_map/ppermute | solution.py:33
  103.3 5.9 %collective-permute-start.14 = (bf16[2,32,8,1024]{3,2,1,0:T(8,128)(2,1)}, bf16[2,32,8,1024]{3,2,1,0:T(8,128)(2,1)}, u32[]{:S(2)}, u32[]{:S(2)}) collective-permute-start(bf16[2,32,8,1024]{3,2,1,0:T(8,128)(2,1)} %get-tuple-element.29), channel_id=1, source_target_pairs={{0,31},{1,0},{2,1},{3,2},{4,3},{5,4},{6,5},{7,6},{8,7},{9,8},{10,9... | collective-permute-start | bytes 3145736 | tf_op jit(solution)/shard_map/ppermute | solution.py:46
  109.3 0.9 select_convert_fusion.refs_27_
  110.2 22.0 %collective-permute-done.20.refs_8_ = bf16[2,8,8,3072]{3,2,1,0:T(8,128)(2,1)} collective-permute-done((bf16[2,8,8,3072]{3,2,1,0:T(8,128)(2,1)}, bf16[2,8,8,3072]{3,2,1,0:T(8,128)(2,1)}, u32[]{:S(2)}, u32[]{:S(2)}) %collective-permute-start.20) | collective-permute-done | bytes 786464 | tf_op jit(solution)/shard_map/ppermute | solution.py:33
  132.2 8.2 %shard_map.55.refs_5_.refs_28_ = bf16[1,32,16,3072]{3,2,1,0:T(8,128)(2,1)} custom-call(s32[1]{0:T(128)} %bitcast.refs_0_, bf16[1,32,16,3072]{3,2,1,0:T(8,128)(2,1)} %refs_1_.9, bf16[2,1,32,16,3072]{4,3,2,1,0:T(8,128)(2,1)} %refs_2_.9, bf16[2,32,8,512]{3,2,1,0:T(8,128)(2,1)} %collective-permute-done.17.refs_1_.refs_2_.refs_3_, ...), custom_call_target="tpu_custom_call" | custom-call | flops 1000 | bytes 1000 | tf_op jit(solution)/shard_map/pallas_call | solution.py:253
  140.4 2.0 %shard_map.56 = bf16[2,2,8,8,1024]{4,3,2,1,0:T(8,128)(2,1)} custom-call(s32[1]{0:T(128)} %bitcast.refs_0_, bf16[2,32,8,1024]{3,2,1,0:T(8,128)(2,1)} %collective-permute-done.15.refs_1_.refs_2_.refs_3_, bf16[2,32,8,1024]{3,2,1,0:T(8,128)(2,1)} %collective-permute-done.15.refs_1_.refs_2_.refs_3_, ...), custom_call_target="tpu_custom_call" | custom-call | flops 1000 | bytes 1000 | tf_op jit(solution)/shard_map/pallas_call | solution.py:58
  142.4 2.2 %collective-permute-done.34.refs_7_ = bf16[2,2,8,8,1024]{4,3,2,1,0:T(8,128)(2,1)} collective-permute-done((bf16[2,2,8,8,1024]{4,3,2,1,0:T(8,128)(2,1)}, bf16[2,2,8,8,1024]{4,3,2,1,0:T(8,128)(2,1)}, u32[]{:S(2)}, u32[]{:S(2)}) %collective-permute-start.34) | collective-permute-done | bytes 524320 | tf_op jit(solution)/shard_map/ppermute | solution.py:42
  144.7 13.2 %shard_map.57.refs_5_.refs_28_ = bf16[1,32,16,3072]{3,2,1,0:T(8,128)(2,1)} custom-call(s32[1]{0:T(128)} %bitcast.refs_0_, bf16[1,32,16,3072]{3,2,1,0:T(8,128)(2,1)} %refs_1_.9, bf16[2,1,32,16,3072]{4,3,2,1,0:T(8,128)(2,1)} %refs_2_.9, bf16[2,32,8,1024]{3,2,1,0:T(8,128)(2,1)} %collective-permute-done.15.refs_1_.refs_2_.refs_3_, ...), custom_call_target="tpu_custom_call", output_to_operand_aliasing={{}: (28, {})} | custom-call | flops 1000 | bytes 1000 | tf_op jit(solution)/shard_map/pallas_call | solution.py:253
  157.8 2.0 %shard_map.58 = bf16[2,2,8,8,1024]{4,3,2,1,0:T(8,128)(2,1)} custom-call(s32[1]{0:T(128)} %bitcast.refs_0_, bf16[2,32,8,1024]{3,2,1,0:T(8,128)(2,1)} %collective-permute-done.13.refs_1_.refs_2_.refs_3_, bf16[2,32,8,1024]{3,2,1,0:T(8,128)(2,1)} %collective-permute-done.13.refs_1_.refs_2_.refs_3_, ...), custom_call_target="tpu_custom_call" | custom-call | flops 1000 | bytes 1000 | tf_op jit(solution)/shard_map/pallas_call | solution.py:58
  160.0 1.5 collective-permute-start.10
  162.1 13.2 %shard_map.59.refs_5_.refs_28_ = bf16[1,32,16,3072]{3,2,1,0:T(8,128)(2,1)} custom-call(s32[1]{0:T(128)} %bitcast.refs_0_, bf16[1,32,16,3072]{3,2,1,0:T(8,128)(2,1)} %refs_1_.9, bf16[2,1,32,16,3072]{4,3,2,1,0:T(8,128)(2,1)} %refs_2_.9, bf16[2,32,8,1024]{3,2,1,0:T(8,128)(2,1)} %collective-permute-done.13.refs_1_.refs_2_.refs_3_, ...), custom_call_target="tpu_custom_call", output_to_operand_aliasing={{}: (28, {})} | custom-call | flops 1000 | bytes 1000 | tf_op jit(solution)/shard_map/pallas_call | solution.py:253
  175.3 2.7 %collective-permute-done.10.refs_1_.refs_2_.refs_3_ = bf16[2,32,8,512]{3,2,1,0:T(8,128)(2,1)} collective-permute-done((bf16[2,32,8,512]{3,2,1,0:T(8,128)(2,1)}, bf16[2,32,8,512]{3,2,1,0:T(8,128)(2,1)}, u32[]{:S(2)}, u32[]{:S(2)}) %collective-permute-start.10) | collective-permute-done | bytes 524320 | tf_op jit(solution)/shard_map/ppermute | solution.py:46
  178.0 1.8 shard_map.60
  179.8 1.0 collective-permute-start.36
  180.9 1.5 collective-permute-done.36.refs_7_
  182.4 8.2 %shard_map.61 = bf16[1,32,16,3072]{3,2,1,0:T(8,128)(2,1)} custom-call(s32[1]{0:T(128)} %bitcast.refs_0_, bf16[1,32,16,3072]{3,2,1,0:T(8,128)(2,1)} %refs_1_.9, bf16[2,1,32,16,3072]{4,3,2,1,0:T(8,128)(2,1)} %refs_2_.9, bf16[2,32,8,512]{3,2,1,0:T(8,128)(2,1)} %collective-permute-done.10.refs_1_.refs_2_.refs_3_, ...), custom_call_target="tpu_custom_call", output_to_operand_aliasing={{}: (28, {})} | custom-call | flops 1000 | bytes 1000 | tf_op jit(solution)/shard_map/pallas_call | solution.py:253
  (76 shorter events, 6.3 us)
Async XLA Ops:
  0.0 6.1 %collective-permute-start.1 = (bf16[2,1,4,3072]{3,2,1,0:T(4,128)(2,1)}, bf16[2,1,4,3072]{3,2,1,0:T(4,128)(2,1)S(1)}, u32[]{:S(2)}, u32[]{:S(2)}) collective-permute-start(bf16[2,1,4,3072]{3,2,1,0:T(4,128)(2,1)} %refs_0_.5), channel_id=1, source_target_pairs={{0,64},{1,65},{2,66},{3,67},{4,68},{5,69},{6,70},{7,71},{8,72},{9,... | collective-permute-start | bytes 147464 | tf_op jit(solution)/shard_map/ppermute | solution.py:42
  4.4 3.4 %collective-permute-start = (bf16[2,1,4,3072]{3,2,1,0:T(4,128)(2,1)}, bf16[2,1,4,3072]{3,2,1,0:T(4,128)(2,1)S(1)}, u32[]{:S(2)}, u32[]{:S(2)}) collective-permute-start(bf16[2,1,4,3072]{3,2,1,0:T(4,128)(2,1)} %refs_0_.5), channel_id=1, source_target_pairs={{0,4},{1,5},{2,6},{3,7},{4,0},{5,1},{6,2},{7,3},{8,12},{9,13},{10,... | collective-permute-start | bytes 147464 | tf_op jit(solution)/shard_map/ppermute | solution.py:42
  5.2 4.4 %collective-permute-start.2 = (bf16[2,1,4,3072]{3,2,1,0:T(4,128)(2,1)}, bf16[2,1,4,3072]{3,2,1,0:T(4,128)(2,1)S(1)}, u32[]{:S(2)}, u32[]{:S(2)}) collective-permute-start(bf16[2,1,4,3072]{3,2,1,0:T(4,128)(2,1)} %refs_0_.5), channel_id=1, source_target_pairs={{0,68},{1,69},{2,70},{3,71},{4,64},{5,65},{6,66},{7,67},{8,76},{9,... | collective-permute-start | bytes 147464 | tf_op jit(solution)/shard_map/ppermute | solution.py:42
  6.1 3.4 %copy-start.9 = (bf16[2,1,4,3072]{3,2,1,0:T(4,128)(2,1)}, bf16[2,1,4,3072]{3,2,1,0:T(4,128)(2,1)S(1)}, u32[]{:S(2)}) copy-start(bf16[2,1,4,3072]{3,2,1,0:T(4,128)(2,1)S(1)} %collective-permute-done.1.refs_2_) | copy-start | bytes 147460
  7.8 1.8 copy-start.10
  11.7 8.8 %collective-permute-start.6 = (bf16[4,2,4,3072]{3,2,1,0:T(4,128)(2,1)}, bf16[4,2,4,3072]{3,2,1,0:T(4,128)(2,1)S(1)}, u32[]{:S(2)}, u32[]{:S(2)}) collective-permute-start(bf16[4,2,4,3072]{3,2,1,0:T(4,128)(2,1)} %shard_map.46.refs_3_.refs_1_), channel_id=1, source_target_pairs={{0,2},{1,3},{2,0},{3,1},{4,6},{5,7},{6,4},{7,5},{8,10},{9,11},{10,... | collective-permute-start | bytes 589832 | tf_op jit(solution)/shard_map/ppermute | solution.py:42
  14.6 7.9 %collective-permute-start.5 = (bf16[4,2,4,3072]{3,2,1,0:T(4,128)(2,1)}, bf16[4,2,4,3072]{3,2,1,0:T(4,128)(2,1)}, u32[]{:S(2)}, u32[]{:S(2)}) collective-permute-start(bf16[4,2,4,3072]{3,2,1,0:T(4,128)(2,1)} %shard_map.46.refs_3_.refs_1_), channel_id=1, source_target_pairs={{0,3},{1,0},{2,1},{3,2},{4,7},{5,4},{6,5},{7,6},{8,11},{9,8},{10,9... | collective-permute-start | bytes 589832 | tf_op jit(solution)/shard_map/ppermute | solution.py:42
  15.4 8.6 %collective-permute-start.4 = (bf16[4,2,4,3072]{3,2,1,0:T(4,128)(2,1)}, bf16[4,2,4,3072]{3,2,1,0:T(4,128)(2,1)}, u32[]{:S(2)}, u32[]{:S(2)}) collective-permute-start(bf16[4,2,4,3072]{3,2,1,0:T(4,128)(2,1)} %shard_map.46.refs_3_.refs_1_), channel_id=1, source_target_pairs={{0,1},{1,2},{2,3},{3,0},{4,5},{5,6},{6,7},{7,4},{8,9},{9,10},{10,1... | collective-permute-start | bytes 589832 | tf_op jit(solution)/shard_map/ppermute | solution.py:42
  20.5 3.4 %copy-start.8 = (bf16[4,2,4,3072]{3,2,1,0:T(4,128)(2,1)}, bf16[4,2,4,3072]{3,2,1,0:T(4,128)(2,1)S(1)}, u32[]{:S(2)}) copy-start(bf16[4,2,4,3072]{3,2,1,0:T(4,128)(2,1)S(1)} %collective-permute-done.6.refs_4_) | copy-start | bytes 589828
  26.3 6.9 %collective-permute-start.8 = (bf16[8,8,3072]{2,1,0:T(8,128)(2,1)}, bf16[8,8,3072]{2,1,0:T(8,128)(2,1)S(1)}, u32[]{:S(2)}, u32[]{:S(2)}) collective-permute-start(bf16[8,8,3072]{2,1,0:T(8,128)(2,1)} %get-tuple-element.22), channel_id=1, source_target_pairs={{0,32},{1,33},{2,34},{3,35},{4,36},{5,37},{6,38},{7,39},{8,40},{9,... | collective-permute-start | bytes 1179656 | tf_op jit(solution)/shard_map/ppermute | solution.py:42
  28.4 5.2 %collective-permute-start.27 = (bf16[8,8,3072]{2,1,0:T(8,128)(2,1)}, bf16[8,8,3072]{2,1,0:T(8,128)(2,1)S(1)}, u32[]{:S(2)}, u32[]{:S(2)}) collective-permute-start(bf16[8,8,3072]{2,1,0:T(8,128)(2,1)} %get-tuple-element.21.refs_10_), channel_id=1, source_target_pairs={{0,32},{1,33},{2,34},{3,35},{4,36},{5,37},{6,38},{7,39},{8,40},{9,... | collective-permute-start | bytes 1179656 | tf_op jit(solution)/shard_map/ppermute | solution.py:42
  28.4 43.5 %collective-permute-start.3 = (bf16[2,8,16,3072]{3,2,1,0:T(8,128)(2,1)}, bf16[2,8,16,3072]{3,2,1,0:T(8,128)(2,1)}, u32[]{:S(2)}, u32[]{:S(2)}) collective-permute-start(bf16[2,8,16,3072]{3,2,1,0:T(8,128)(2,1)} %get-tuple-element.19), channel_id=1, source_target_pairs={{32,64},{33,65},{34,66},{35,67},{36,68},{37,69},{38,70},{39,71},{4... | collective-permute-start | bytes 4718600 | tf_op jit(solution)/shard_map/ppermute | solution.py:33
  30.7 11.4 %collective-permute-start.23 = (bf16[8,8,3072]{2,1,0:T(8,128)(2,1)}, bf16[8,8,3072]{2,1,0:T(8,128)(2,1)S(1)}, u32[]{:S(2)}, u32[]{:S(2)}) collective-permute-start(bf16[8,8,3072]{2,1,0:T(8,128)(2,1)} %get-tuple-element.21.refs_10_), channel_id=1, source_target_pairs={{0,24},{1,25},{2,26},{3,27},{4,28},{5,29},{6,30},{7,31},{8,0},{9,1... | collective-permute-start | bytes 1179656 | tf_op jit(solution)/shard_map/ppermute | solution.py:42
  33.3 12.2 %collective-permute-start.7 = (bf16[8,8,3072]{2,1,0:T(8,128)(2,1)}, bf16[8,8,3072]{2,1,0:T(8,128)(2,1)S(1)}, u32[]{:S(2)}, u32[]{:S(2)}) collective-permute-start(bf16[8,8,3072]{2,1,0:T(8,128)(2,1)} %get-tuple-element.21.refs_10_), channel_id=1, source_target_pairs={{0,8},{1,9},{2,10},{3,11},{4,12},{5,13},{6,14},{7,15},{8,16},{9,17... | collective-permute-start | bytes 1179656 | tf_op jit(solution)/shard_map/ppermute | solution.py:42
  33.3 32.8 %copy-start.1 = (bf16[8,8,3072]{2,1,0:T(8,128)(2,1)}, bf16[8,8,3072]{2,1,0:T(8,128)(2,1)S(1)}, u32[]{:S(2)}) copy-start(bf16[8,8,3072]{2,1,0:T(8,128)(2,1)S(1)} %collective-permute-done.8.refs_11_) | copy-start | bytes 1179652
  33.3 13.6 %collective-permute-start.26 = (bf16[8,8,3072]{2,1,0:T(8,128)(2,1)S(1)}, bf16[8,8,3072]{2,1,0:T(8,128)(2,1)S(1)}, u32[]{:S(2)}, u32[]{:S(2)}) collective-permute-start(bf16[8,8,3072]{2,1,0:T(8,128)(2,1)S(1)} %collective-permute-done.8.refs_11_), channel_id=1, source_target_pairs={{0,32},{1,33},{2,34},{3,35},{4,36},{5,37},{6,38},{7,39},{8,40},{9,... | collective-permute-start | bytes 1179656 | tf_op jit(solution)/shard_map/ppermute | solution.py:42
  33.6 32.4 %copy-start.2 = (bf16[8,8,3072]{2,1,0:T(8,128)(2,1)}, bf16[8,8,3072]{2,1,0:T(8,128)(2,1)S(1)}, u32[]{:S(2)}) copy-start(bf16[8,8,3072]{2,1,0:T(8,128)(2,1)S(1)} %collective-permute-done.27.refs_19_) | copy-start | bytes 1179652
  33.6 20.0 %collective-permute-start.22 = (bf16[8,8,3072]{2,1,0:T(8,128)(2,1)S(1)}, bf16[8,8,3072]{2,1,0:T(8,128)(2,1)}, u32[]{:S(2)}, u32[]{:S(2)}) collective-permute-start(bf16[8,8,3072]{2,1,0:T(8,128)(2,1)S(1)} %collective-permute-done.8.refs_11_), channel_id=1, source_target_pairs={{0,8},{1,9},{2,10},{3,11},{4,12},{5,13},{6,14},{7,15},{8,16},{9,17... | collective-permute-start | bytes 1179656 | tf_op jit(solution)/shard_map/ppermute | solution.py:42
  42.1 23.9 %copy-start.3 = (bf16[8,8,3072]{2,1,0:T(8,128)(2,1)}, bf16[8,8,3072]{2,1,0:T(8,128)(2,1)S(1)}, u32[]{:S(2)}) copy-start(bf16[8,8,3072]{2,1,0:T(8,128)(2,1)S(1)} %collective-permute-done.23.refs_14_) | copy-start | bytes 1179652
  42.2 12.6 %collective-permute-start.9 = (bf16[8,8,3072]{2,1,0:T(8,128)(2,1)S(1)}, bf16[8,8,3072]{2,1,0:T(8,128)(2,1)}, u32[]{:S(2)}, u32[]{:S(2)}) collective-permute-start(bf16[8,8,3072]{2,1,0:T(8,128)(2,1)S(1)} %collective-permute-done.8.refs_11_), channel_id=1, source_target_pairs={{0,24},{1,25},{2,26},{3,27},{4,28},{5,29},{6,30},{7,31},{8,0},{9,1... | collective-permute-start | bytes 1179656 | tf_op jit(solution)/shard_map/ppermute | solution.py:42
  45.5 9.3 %copy-start = (bf16[8,8,3072]{2,1,0:T(8,128)(2,1)}, bf16[8,8,3072]{2,1,0:T(8,128)(2,1)S(1)}, u32[]{:S(2)}) copy-start(bf16[8,8,3072]{2,1,0:T(8,128)(2,1)S(1)} %collective-permute-done.7.refs_1_.refs_12_) | copy-start | bytes 1179652
  45.5 54.1 %collective-permute-start.12 = (bf16[2,8,16,3072]{3,2,1,0:T(8,128)(2,1)}, bf16[2,8,16,3072]{3,2,1,0:T(8,128)(2,1)}, u32[]{:S(2)}, u32[]{:S(2)}) collective-permute-start(bf16[2,8,16,3072]{3,2,1,0:T(8,128)(2,1)} %get-tuple-element.20.refs_5_), channel_id=1, source_target_pairs={{0,32},{1,33},{2,34},{3,35},{4,36},{5,37},{6,38},{7,39},{8,40},{9,... | collective-permute-start | bytes 4718600 | tf_op jit(solution)/shard_map/ppermute | solution.py:42
  46.9 19.1 %copy-start.4 = (bf16[8,8,3072]{2,1,0:T(8,128)(2,1)}, bf16[8,8,3072]{2,1,0:T(8,128)(2,1)S(1)}, u32[]{:S(2)}) copy-start(bf16[8,8,3072]{2,1,0:T(8,128)(2,1)S(1)} %collective-permute-done.26.refs_18_) | copy-start | bytes 1179652
  46.9 7.9 %collective-permute-start.31 = (bf16[8,8,3072]{2,1,0:T(8,128)(2,1)S(1)}, bf16[8,8,3072]{2,1,0:T(8,128)(2,1)S(1)}, u32[]{:S(2)}, u32[]{:S(2)}) collective-permute-start(bf16[8,8,3072]{2,1,0:T(8,128)(2,1)S(1)} %collective-permute-done.23.refs_14_), channel_id=1, source_target_pairs={{0,32},{1,33},{2,34},{3,35},{4,36},{5,37},{6,38},{7,39},{8,40},{9,... | collective-permute-start | bytes 1179656 | tf_op jit(solution)/shard_map/ppermute | solution.py:42
  53.7 2.4 %collective-permute-start.29 = (bf16[8,8,3072]{2,1,0:T(8,128)(2,1)S(1)}, bf16[8,8,3072]{2,1,0:T(8,128)(2,1)S(1)}, u32[]{:S(2)}, u32[]{:S(2)}) collective-permute-start(bf16[8,8,3072]{2,1,0:T(8,128)(2,1)S(1)} %collective-permute-done.7.refs_1_.refs_12_), channel_id=1, source_target_pairs={{0,32},{1,33},{2,34},{3,35},{4,36},{5,37},{6,38},{7,39},{8,40},{9,... | collective-permute-start | bytes 1179656 | tf_op jit(solution)/shard_map/ppermute | solution.py:42
  54.7 11.3 %collective-permute-start.24 = (bf16[8,8,3072]{2,1,0:T(8,128)(2,1)S(1)}, bf16[8,8,3072]{2,1,0:T(8,128)(2,1)S(1)}, u32[]{:S(2)}, u32[]{:S(2)}) collective-permute-start(bf16[8,8,3072]{2,1,0:T(8,128)(2,1)S(1)} %collective-permute-done.7.refs_1_.refs_12_), channel_id=1, source_target_pairs={{0,8},{1,9},{2,10},{3,11},{4,12},{5,13},{6,14},{7,15},{8,16},{9,17... | collective-permute-start | bytes 1179656 | tf_op jit(solution)/shard_map/ppermute | solution.py:42
  54.8 11.3 %copy-start.5 = (bf16[8,8,3072]{2,1,0:T(8,128)(2,1)}, bf16[8,8,3072]{2,1,0:T(8,128)(2,1)S(1)}, u32[]{:S(2)}) copy-start(bf16[8,8,3072]{2,1,0:T(8,128)(2,1)S(1)} %collective-permute-done.31.refs_23_) | copy-start | bytes 1179652
  54.8 14.3 %collective-permute-start.28 = (bf16[8,8,3072]{2,1,0:T(8,128)(2,1)}, bf16[8,8,3072]{2,1,0:T(8,128)(2,1)}, u32[]{:S(2)}, u32[]{:S(2)}) collective-permute-start(bf16[8,8,3072]{2,1,0:T(8,128)(2,1)} %collective-permute-done.22.refs_13_), channel_id=1, source_target_pairs={{0,32},{1,33},{2,34},{3,35},{4,36},{5,37},{6,38},{7,39},{8,40},{9,... | collective-permute-start | bytes 1179656 | tf_op jit(solution)/shard_map/ppermute | solution.py:42
  56.1 10.0 %copy-start.6 = (bf16[8,8,3072]{2,1,0:T(8,128)(2,1)}, bf16[8,8,3072]{2,1,0:T(8,128)(2,1)S(1)}, u32[]{:S(2)}) copy-start(bf16[8,8,3072]{2,1,0:T(8,128)(2,1)S(1)} %collective-permute-done.29.refs_21_) | copy-start | bytes 1179652
  56.1 15.8 %collective-permute-start.30 = (bf16[8,8,3072]{2,1,0:T(8,128)(2,1)}, bf16[8,8,3072]{2,1,0:T(8,128)(2,1)}, u32[]{:S(2)}, u32[]{:S(2)}) collective-permute-start(bf16[8,8,3072]{2,1,0:T(8,128)(2,1)} %collective-permute-done.9.refs_2_.refs_15_), channel_id=1, source_target_pairs={{0,32},{1,33},{2,34},{3,35},{4,36},{5,37},{6,38},{7,39},{8,40},{9,... | collective-permute-start | bytes 1179656 | tf_op jit(solution)/shard_map/ppermute | solution.py:42
  66.1 0.8 copy-start.7
  66.8 12.3 %collective-permute-start.25 = (bf16[8,8,3072]{2,1,0:T(8,128)(2,1)}, bf16[8,8,3072]{2,1,0:T(8,128)(2,1)}, u32[]{:S(2)}, u32[]{:S(2)}) collective-permute-start(bf16[8,8,3072]{2,1,0:T(8,128)(2,1)} %collective-permute-done.9.refs_2_.refs_15_), channel_id=1, source_target_pairs={{0,24},{1,25},{2,26},{3,27},{4,28},{5,29},{6,30},{7,31},{8,0},{9,1... | collective-permute-start | bytes 1179656 | tf_op jit(solution)/shard_map/ppermute | solution.py:42
  69.1 18.0 %collective-permute-start.18 = (bf16[2,32,8,512]{3,2,1,0:T(8,128)(2,1)}, bf16[2,32,8,512]{3,2,1,0:T(8,128)(2,1)}, u32[]{:S(2)}, u32[]{:S(2)}) collective-permute-start(bf16[2,32,8,512]{3,2,1,0:T(8,128)(2,1)} %get-tuple-element.31), channel_id=1, source_target_pairs={{0,31},{1,0},{2,1},{3,2},{4,3},{5,4},{6,5},{7,6},{8,7},{9,8},{10,9... | collective-permute-start | bytes 1572872 | tf_op jit(solution)/shard_map/ppermute | solution.py:46
  71.9 16.1 %collective-permute-start.17 = (bf16[2,32,8,512]{3,2,1,0:T(8,128)(2,1)}, bf16[2,32,8,512]{3,2,1,0:T(8,128)(2,1)}, u32[]{:S(2)}, u32[]{:S(2)}) collective-permute-start(bf16[2,32,8,512]{3,2,1,0:T(8,128)(2,1)} %get-tuple-element.23.refs_1_), channel_id=1, source_target_pairs={{0,1},{1,2},{2,3},{3,4},{4,5},{5,6},{6,7},{7,8},{8,9},{9,10},{10,1... | collective-permute-start | bytes 1572872 | tf_op jit(solution)/shard_map/ppermute | solution.py:46
  71.9 15.0 %collective-permute-start.33 = (bf16[8,8,3072]{2,1,0:T(8,128)(2,1)}, bf16[8,8,3072]{2,1,0:T(8,128)(2,1)}, u32[]{:S(2)}, u32[]{:S(2)}) collective-permute-start(bf16[8,8,3072]{2,1,0:T(8,128)(2,1)} %copy-done.7), channel_id=1, source_target_pairs={{0,32},{1,33},{2,34},{3,35},{4,36},{5,37},{6,38},{7,39},{8,40},{9,... | collective-permute-start | bytes 1179656 | tf_op jit(solution)/shard_map/ppermute | solution.py:42
  79.2 24.1 %collective-permute-start.21 = (bf16[2,8,8,3072]{3,2,1,0:T(8,128)(2,1)}, bf16[2,8,8,3072]{3,2,1,0:T(8,128)(2,1)}, u32[]{:S(2)}, u32[]{:S(2)}) collective-permute-start(bf16[2,8,8,3072]{3,2,1,0:T(8,128)(2,1)} %get-tuple-element.32), channel_id=1, source_target_pairs={{32,63},{33,32},{34,33},{35,34},{36,35},{37,36},{38,37},{39,38},{4... | collective-permute-start | bytes 2359304 | tf_op jit(solution)/shard_map/ppermute | solution.py:33
  87.0 14.2 %collective-permute-start.32 = (bf16[8,8,3072]{2,1,0:T(8,128)(2,1)}, bf16[8,8,3072]{2,1,0:T(8,128)(2,1)}, u32[]{:S(2)}, u32[]{:S(2)}) collective-permute-start(bf16[8,8,3072]{2,1,0:T(8,128)(2,1)} %collective-permute-done.25.refs_17_), channel_id=1, source_target_pairs={{0,32},{1,33},{2,34},{3,35},{4,36},{5,37},{6,38},{7,39},{8,40},{9,... | collective-permute-start | bytes 1179656 | tf_op jit(solution)/shard_map/ppermute | solution.py:42
  87.1 53.3 %collective-permute-start.15 = (bf16[2,32,8,1024]{3,2,1,0:T(8,128)(2,1)}, bf16[2,32,8,1024]{3,2,1,0:T(8,128)(2,1)}, u32[]{:S(2)}, u32[]{:S(2)}) collective-permute-start(bf16[2,32,8,1024]{3,2,1,0:T(8,128)(2,1)} %get-tuple-element.24.refs_1_), channel_id=1, source_target_pairs={{0,1},{1,2},{2,3},{3,4},{4,5},{5,6},{6,7},{7,8},{8,9},{9,10},{10,1... | collective-permute-start | bytes 3145736 | tf_op jit(solution)/shard_map/ppermute | solution.py:46
  88.0 52.3 %collective-permute-start.16 = (bf16[2,32,8,1024]{3,2,1,0:T(8,128)(2,1)}, bf16[2,32,8,1024]{3,2,1,0:T(8,128)(2,1)}, u32[]{:S(2)}, u32[]{:S(2)}) collective-permute-start(bf16[2,32,8,1024]{3,2,1,0:T(8,128)(2,1)} %get-tuple-element.30), channel_id=1, source_target_pairs={{0,31},{1,0},{2,1},{3,2},{4,3},{5,4},{6,5},{7,6},{8,7},{9,8},{10,9... | collective-permute-start | bytes 3145736 | tf_op jit(solution)/shard_map/ppermute | solution.py:46
  99.6 3.6 %collective-permute-start.19 = (bf16[2,2,8,8,512]{4,3,2,1,0:T(8,128)(2,1)}, bf16[2,2,8,8,512]{4,3,2,1,0:T(8,128)(2,1)}, u32[]{:S(2)}, u32[]{:S(2)}) collective-permute-start(bf16[2,2,8,8,512]{4,3,2,1,0:T(8,128)(2,1)} %shard_map.54), channel_id=1, source_target_pairs={{0,32},{1,33},{2,34},{3,35},{4,36},{5,37},{6,38},{7,39},{8,40},{9,... | collective-permute-start | bytes 786440 | tf_op jit(solution)/shard_map/ppermute | solution.py:42
  101.1 31.0 %collective-permute-start.20 = (bf16[2,8,8,3072]{3,2,1,0:T(8,128)(2,1)}, bf16[2,8,8,3072]{3,2,1,0:T(8,128)(2,1)}, u32[]{:S(2)}, u32[]{:S(2)}) collective-permute-start(bf16[2,8,8,3072]{3,2,1,0:T(8,128)(2,1)} %get-tuple-element.25.refs_1_), channel_id=1, source_target_pairs={{32,33},{33,34},{34,35},{35,36},{36,37},{37,38},{38,39},{39,40},{4... | collective-permute-start | bytes 2359304 | tf_op jit(solution)/shard_map/ppermute | solution.py:33
  103.2 54.7 %collective-permute-start.13 = (bf16[2,32,8,1024]{3,2,1,0:T(8,128)(2,1)}, bf16[2,32,8,1024]{3,2,1,0:T(8,128)(2,1)}, u32[]{:S(2)}, u32[]{:S(2)}) collective-permute-start(bf16[2,32,8,1024]{3,2,1,0:T(8,128)(2,1)} %get-tuple-element.26.refs_1_), channel_id=1, source_target_pairs={{0,1},{1,2},{2,3},{3,4},{4,5},{5,6},{6,7},{7,8},{8,9},{9,10},{10,1... | collective-permute-start | bytes 3145736 | tf_op jit(solution)/shard_map/ppermute | solution.py:46
  103.3 54.6 %collective-permute-start.14 = (bf16[2,32,8,1024]{3,2,1,0:T(8,128)(2,1)}, bf16[2,32,8,1024]{3,2,1,0:T(8,128)(2,1)}, u32[]{:S(2)}, u32[]{:S(2)}) collective-permute-start(bf16[2,32,8,1024]{3,2,1,0:T(8,128)(2,1)} %get-tuple-element.29), channel_id=1, source_target_pairs={{0,31},{1,0},{2,1},{3,2},{4,3},{5,4},{6,5},{7,6},{8,7},{9,8},{10,9... | collective-permute-start | bytes 3145736 | tf_op jit(solution)/shard_map/ppermute | solution.py:46
  142.4 2.3 %collective-permute-start.34 = (bf16[2,2,8,8,1024]{4,3,2,1,0:T(8,128)(2,1)}, bf16[2,2,8,8,1024]{4,3,2,1,0:T(8,128)(2,1)}, u32[]{:S(2)}, u32[]{:S(2)}) collective-permute-start(bf16[2,2,8,8,1024]{4,3,2,1,0:T(8,128)(2,1)} %shard_map.56), channel_id=1, source_target_pairs={{0,32},{1,33},{2,34},{3,35},{4,36},{5,37},{6,38},{7,39},{8,40},{9,... | collective-permute-start | bytes 1572872 | tf_op jit(solution)/shard_map/ppermute | solution.py:42
  159.9 2.3 %collective-permute-start.35 = (bf16[2,2,8,8,1024]{4,3,2,1,0:T(8,128)(2,1)}, bf16[2,2,8,8,1024]{4,3,2,1,0:T(8,128)(2,1)}, u32[]{:S(2)}, u32[]{:S(2)}) collective-permute-start(bf16[2,2,8,8,1024]{4,3,2,1,0:T(8,128)(2,1)} %shard_map.58), channel_id=1, source_target_pairs={{0,32},{1,33},{2,34},{3,35},{4,36},{5,37},{6,38},{7,39},{8,40},{9,... | collective-permute-start | bytes 1572872 | tf_op jit(solution)/shard_map/ppermute | solution.py:42
  160.0 15.3 %collective-permute-start.11 = (bf16[2,32,8,512]{3,2,1,0:T(8,128)(2,1)}, bf16[2,32,8,512]{3,2,1,0:T(8,128)(2,1)}, u32[]{:S(2)}, u32[]{:S(2)}) collective-permute-start(bf16[2,32,8,512]{3,2,1,0:T(8,128)(2,1)} %get-tuple-element.28), channel_id=1, source_target_pairs={{0,31},{1,0},{2,1},{3,2},{4,3},{5,4},{6,5},{7,6},{8,7},{9,8},{10,9... | collective-permute-start | bytes 1572872 | tf_op jit(solution)/shard_map/ppermute | solution.py:46
  160.0 18.0 %collective-permute-start.10 = (bf16[2,32,8,512]{3,2,1,0:T(8,128)(2,1)}, bf16[2,32,8,512]{3,2,1,0:T(8,128)(2,1)}, u32[]{:S(2)}, u32[]{:S(2)}) collective-permute-start(bf16[2,32,8,512]{3,2,1,0:T(8,128)(2,1)} %get-tuple-element.27.refs_5_), channel_id=1, source_target_pairs={{0,1},{1,2},{2,3},{3,4},{4,5},{5,6},{6,7},{7,8},{8,9},{9,10},{10,1... | collective-permute-start | bytes 1572872 | tf_op jit(solution)/shard_map/ppermute | solution.py:46
  179.8 2.5 %collective-permute-start.36 = (bf16[2,2,8,8,512]{4,3,2,1,0:T(8,128)(2,1)}, bf16[2,2,8,8,512]{4,3,2,1,0:T(8,128)(2,1)}, u32[]{:S(2)}, u32[]{:S(2)}) collective-permute-start(bf16[2,2,8,8,512]{4,3,2,1,0:T(8,128)(2,1)} %shard_map.60), channel_id=1, source_target_pairs={{0,32},{1,33},{2,34},{3,35},{4,36},{5,37},{6,38},{7,39},{8,40},{9,... | collective-permute-start | bytes 786440 | tf_op jit(solution)/shard_map/ppermute | solution.py:42
  (1 other events, 0.6 us)

commit v4 on v3

--- a/solution.py
+++ b/solution.py
@@ -14,7 +14,7 @@
 NEG = -1e30
 ZH, CORE, NX, ZL, NY = 2, 2, 4, 2, 4
 N_LAT, N_LON = ZH * CORE, NX * ZL * NY
-CHUNKS = (4, 8, 8, 4)
+CHUNKS = (8, 8, 4, 4)
 PER_STEP = 4
 WIDE = PER_STEP * HD
 BLOCK = 16

time: 192 us -> 193 us (level)
  starting transfers between devices: 53.3 us -> 56.2 us
    ppermute x3, waiting for transfers between devices: 22 us -> 14.5 us  [send_where(): return lax.ppermute(x, ('lat', 'lon'), pairs)]
    ppermute x8, waiting for transfers between devices: 3.55 us -> 10.1 us  [send_lon(): lax.ppermute(x, 'lon', [(i, (i + step) % N_LON) for i in range(N_LON)])]
    ppermute x3, starting transfers between devices: 12 us -> 14.3 us  [send_where(): return lax.ppermute(x, ('lat', 'lon'), pairs)]
  transfers between devices with their start and end apart: 37 -> 37, of which waited for: 15 -> 14; matrix products, arithmetic and copies ran while one was open for 1% -> 1% of each run, Pallas kernels for 29% -> 29%
where the time goes in v4:
time: 193 us
  Pallas kernels  71.3 us (37%)
  waiting for transfers between devices  62.5 us (32%)
  starting transfers between devices  56.2 us (29%)
    pallas_call x4, Pallas kernels, attend(): pl.pallas_call(functools.partial(attend_body, len(deps) + (output is not...  42.6 us
    ppermute x26, waiting for transfers between devices, send(): return lax.ppermute(x, ('lat', 'lon'), pairs)  37.9 us
    pallas_call x12, Pallas kernels, glue(): pl.pallas_call(kernel, grid=grid or (), in_specs=list(specs) + [pl.BlockS...  28.6 us
    ppermute x26, starting transfers between devices, send(): return lax.ppermute(x, ('lat', 'lon'), pairs)  27.5 us
    ppermute x3, waiting for transfers between devices, send_where(): return lax.ppermute(x, ('lat', 'lon'), pairs)  14.5 us
    ppermute x3, starting transfers between devices, send_where(): return lax.ppermute(x, ('lat', 'lon'), pairs)  14.3 us
    ppermute x8, starting transfers between devices, send_lon(): lax.ppermute(x, 'lon', [(i, (i + step) % N_LON) for i in range(N_LON)])  14.3 us
    ppermute x8, waiting for transfers between devices, send_lon(): lax.ppermute(x, 'lon', [(i, (i + step) % N_LON) for i in range(N_LON)])  10.1 us
  transfers between devices with their start and end apart: 37, of which 14 were waited for; matrix products, arithmetic and copies ran while one was open for 1% of the time, Pallas kernels for 29%

profile of v4, /device:TPU:1, one launch (start us, length us, event | category | flops | bytes accessed | tf_op | source)
XLA Modules:
  0.0 192.7 jit_solution(12141754655072635664)
XLA Ops:
  0.0 4.4 %collective-permute-start.1 = (bf16[2,1,4,3072]{3,2,1,0:T(4,128)(2,1)}, bf16[2,1,4,3072]{3,2,1,0:T(4,128)(2,1)S(1)}, u32[]{:S(2)}, u32[]{:S(2)}) collective-permute-start(bf16[2,1,4,3072]{3,2,1,0:T(4,128)(2,1)} %refs_0_.5), channel_id=1, source_target_pairs={{0,64},{1,65},{2,66},{3,67},{4,68},{5,69},{6,70},{7,71},{8,72},{9,... | collective-permute-start | bytes 147464 | tf_op jit(solution)/shard_map/ppermute | solution.py:42
  5.2 0.9 collective-permute-done.1.refs_2_
  6.1 1.7 collective-permute-done.refs_1_
  7.8 1.7 collective-permute-done.2.refs_3_
  10.2 1.6 shard_map.46.refs_3_.refs_1_
  11.7 2.9 %collective-permute-start.6 = (bf16[4,2,4,3072]{3,2,1,0:T(4,128)(2,1)}, bf16[4,2,4,3072]{3,2,1,0:T(4,128)(2,1)S(1)}, u32[]{:S(2)}, u32[]{:S(2)}) collective-permute-start(bf16[4,2,4,3072]{3,2,1,0:T(4,128)(2,1)} %shard_map.46.refs_3_.refs_1_), channel_id=1, source_target_pairs={{0,2},{1,3},{2,0},{3,1},{4,6},{5,7},{6,4},{7,5},{8,10},{9,11},{10,... | collective-permute-start | bytes 589832 | tf_op jit(solution)/shard_map/ppermute | solution.py:42
  14.6 0.8 collective-permute-start.5
  16.1 4.5 %shard_map.47 = (bf16[2,8,16,3072]{3,2,1,0:T(8,128)(2,1)}, bf16[2,8,16,3072]{3,2,1,0:T(8,128)(2,1)}) custom-call(s32[1]{0:T(128)} %bitcast.refs_0_, bf16[2,1,32,16,3072]{4,3,2,1,0:T(8,128)(2,1)} %refs_2_.9, bf16[2,1,32,16,3072]{4,3,2,1,0:T(8,128)(2,1)} %refs_2_.9, bf16[4,2,4,3072]{3,2,1,0:T(4,128)(2,1)} %shard_map.46.refs_3_.refs_1_), custom_call_target="tpu_custom_call" | custom-call | flops 1000 | bytes 1000 | tf_op jit(solution)/shard_map/pallas_call | solution.py:58
  20.6 2.0 %collective-permute-done.5.refs_3_ = bf16[4,2,4,3072]{3,2,1,0:T(4,128)(2,1)} collective-permute-done((bf16[4,2,4,3072]{3,2,1,0:T(4,128)(2,1)}, bf16[4,2,4,3072]{3,2,1,0:T(4,128)(2,1)}, u32[]{:S(2)}, u32[]{:S(2)}) %collective-permute-start.5) | collective-permute-done | bytes 196640 | tf_op jit(solution)/shard_map/ppermute | solution.py:42
  22.5 1.4 collective-permute-done.4.refs_2_
  24.0 2.4 %shard_map.48 = (bf16[8,8,3072]{2,1,0:T(8,128)(2,1)}, bf16[8,8,3072]{2,1,0:T(8,128)(2,1)}) custom-call(s32[1]{0:T(128)} %bitcast.refs_0_, bf16[4,2,4,3072]{3,2,1,0:T(4,128)(2,1)} %shard_map.46.refs_3_.refs_1_, bf16[4,2,4,3072]{3,2,1,0:T(4,128)(2,1)} %collective-permute-done.4.refs_2_, bf16[4,2,4,3072]{3,2,1,0:T(4,128)(2,1)} %collective-permute-done.5.refs_3_, ...), custom_call_target="tpu_custom_call" | custom-call | flops 1000 | bytes 1000 | tf_op jit(solution)/shard_map/pallas_call | solution.py:58
  26.4 2.1 %collective-permute-start.8 = (bf16[8,8,3072]{2,1,0:T(8,128)(2,1)}, bf16[8,8,3072]{2,1,0:T(8,128)(2,1)S(1)}, u32[]{:S(2)}, u32[]{:S(2)}) collective-permute-start(bf16[8,8,3072]{2,1,0:T(8,128)(2,1)} %get-tuple-element.22), channel_id=1, source_target_pairs={{0,32},{1,33},{2,34},{3,35},{4,36},{5,37},{6,38},{7,39},{8,40},{9,... | collective-permute-start | bytes 1179656 | tf_op jit(solution)/shard_map/ppermute | solution.py:42
  28.4 2.5 %collective-permute-start.23 = (bf16[8,8,3072]{2,1,0:T(8,128)(2,1)}, bf16[8,8,3072]{2,1,0:T(8,128)(2,1)S(1)}, u32[]{:S(2)}, u32[]{:S(2)}) collective-permute-start(bf16[8,8,3072]{2,1,0:T(8,128)(2,1)} %get-tuple-element.21.refs_10_), channel_id=1, source_target_pairs={{0,24},{1,25},{2,26},{3,27},{4,28},{5,29},{6,30},{7,31},{8,0},{9,1... | collective-permute-start | bytes 1179656 | tf_op jit(solution)/shard_map/ppermute | solution.py:42
  30.9 0.9 collective-permute-start.26
  32.2 2.6 %collective-permute-start.9 = (bf16[8,8,3072]{2,1,0:T(8,128)(2,1)S(1)}, bf16[8,8,3072]{2,1,0:T(8,128)(2,1)}, u32[]{:S(2)}, u32[]{:S(2)}) collective-permute-start(bf16[8,8,3072]{2,1,0:T(8,128)(2,1)S(1)} %collective-permute-done.8.refs_11_), channel_id=1, source_target_pairs={{0,24},{1,25},{2,26},{3,27},{4,28},{5,29},{6,30},{7,31},{8,0},{9,1... | collective-permute-start | bytes 1179656 | tf_op jit(solution)/shard_map/ppermute | solution.py:42
  34.8 4.4 %collective-permute-done.23.refs_14_ = bf16[8,8,3072]{2,1,0:T(8,128)(2,1)S(1)} collective-permute-done((bf16[8,8,3072]{2,1,0:T(8,128)(2,1)}, bf16[8,8,3072]{2,1,0:T(8,128)(2,1)S(1)}, u32[]{:S(2)}, u32[]{:S(2)}) %collective-permute-start.23) | collective-permute-done | bytes 393248 | tf_op jit(solution)/shard_map/ppermute | solution.py:42
  39.2 4.1 %collective-permute-start.3 = (bf16[2,8,16,3072]{3,2,1,0:T(8,128)(2,1)}, bf16[2,8,16,3072]{3,2,1,0:T(8,128)(2,1)}, u32[]{:S(2)}, u32[]{:S(2)}) collective-permute-start(bf16[2,8,16,3072]{3,2,1,0:T(8,128)(2,1)} %get-tuple-element.19), channel_id=1, source_target_pairs={{32,64},{33,65},{34,66},{35,67},{36,68},{37,69},{38,70},{39,71},{4... | collective-permute-start | bytes 4718600 | tf_op jit(solution)/shard_map/ppermute | solution.py:33
  43.3 1.8 collective-permute-start.31
  45.2 5.5 %collective-permute-done.22.refs_13_ = bf16[8,8,3072]{2,1,0:T(8,128)(2,1)} collective-permute-done((bf16[8,8,3072]{2,1,0:T(8,128)(2,1)S(1)}, bf16[8,8,3072]{2,1,0:T(8,128)(2,1)}, u32[]{:S(2)}, u32[]{:S(2)}) %collective-permute-start.22) | collective-permute-done | bytes 393248 | tf_op jit(solution)/shard_map/ppermute | solution.py:42
  50.7 1.7 collective-permute-start.12
  53.0 11.3 %collective-permute-done.24.refs_16_ = bf16[8,8,3072]{2,1,0:T(8,128)(2,1)S(1)} collective-permute-done((bf16[8,8,3072]{2,1,0:T(8,128)(2,1)S(1)}, bf16[8,8,3072]{2,1,0:T(8,128)(2,1)S(1)}, u32[]{:S(2)}, u32[]{:S(2)}) %collective-permute-start.24) | collective-permute-done | bytes 393248 | tf_op jit(solution)/shard_map/ppermute | solution.py:42
  65.1 2.7 %shard_map.49 = (bf16[2,32,8,1024]{3,2,1,0:T(8,128)(2,1)}, bf16[2,32,8,1024]{3,2,1,0:T(8,128)(2,1)}) custom-call(bf16[2,1,32,16,3072]{4,3,2,1,0:T(8,128)(2,1)} %refs_2_.9, bf16[8,8,3072]{2,1,0:T(8,128)(2,1)} %copy-done, bf16[8,8,3072]{2,1,0:T(8,128)(2,1)} %collective-permute-done.9.refs_2_.refs_15_), custom_call_target="tpu_custom_call" | custom-call | flops 1000 | bytes 1000 | tf_op jit(solution)/shard_map/pallas_call | solution.py:58
  67.8 1.4 collective-permute-start.17
  69.2 5.9 %collective-permute-done.25.refs_17_ = bf16[8,8,3072]{2,1,0:T(8,128)(2,1)} collective-permute-done((bf16[8,8,3072]{2,1,0:T(8,128)(2,1)}, bf16[8,8,3072]{2,1,0:T(8,128)(2,1)}, u32[]{:S(2)}, u32[]{:S(2)}) %collective-permute-start.25) | collective-permute-done | bytes 393248 | tf_op jit(solution)/shard_map/ppermute | solution.py:42
  75.1 3.1 %collective-permute-start.33 = (bf16[8,8,3072]{2,1,0:T(8,128)(2,1)}, bf16[8,8,3072]{2,1,0:T(8,128)(2,1)}, u32[]{:S(2)}, u32[]{:S(2)}) collective-permute-start(bf16[8,8,3072]{2,1,0:T(8,128)(2,1)} %copy-done.7), channel_id=1, source_target_pairs={{0,32},{1,33},{2,34},{3,35},{4,36},{5,37},{6,38},{7,39},{8,40},{9,... | collective-permute-start | bytes 1179656 | tf_op jit(solution)/shard_map/ppermute | solution.py:42
  78.3 2.7 %shard_map.50 = (bf16[2,32,8,1024]{3,2,1,0:T(8,128)(2,1)}, bf16[2,32,8,1024]{3,2,1,0:T(8,128)(2,1)}) custom-call(bf16[2,1,32,16,3072]{4,3,2,1,0:T(8,128)(2,1)} %refs_2_.9, bf16[2,32,8,1024]{3,2,1,0:T(8,128)(2,1)} %get-tuple-element.23.refs_1_), custom_call_target="tpu_custom_call" | custom-call | flops 1000 | bytes 1000 | tf_op jit(solution)/shard_map/pallas_call | solution.py:58
  81.7 0.8 collective-permute-start.15
  83.1 2.6 %shard_map.51 = (bf16[2,8,8,3072]{3,2,1,0:T(8,128)(2,1)}, bf16[2,8,8,3072]{3,2,1,0:T(8,128)(2,1)}) custom-call(bf16[2,8,16,3072]{3,2,1,0:T(8,128)(2,1)} %collective-permute-done.3.refs_0_.refs_6_, bf16[2,32,8,1024]{3,2,1,0:T(8,128)(2,1)} %get-tuple-element.24.refs_1_), custom_call_target="tpu_custom_call" | custom-call | flops 1000 | bytes 1000 | tf_op jit(solution)/shard_map/pallas_call | solution.py:58
  85.7 10.0 %collective-permute-done.18.refs_3_.refs_4_ = bf16[2,32,8,1024]{3,2,1,0:T(8,128)(2,1)} collective-permute-done((bf16[2,32,8,1024]{3,2,1,0:T(8,128)(2,1)}, bf16[2,32,8,1024]{3,2,1,0:T(8,128)(2,1)}, u32[]{:S(2)}, u32[]{:S(2)}) %collective-permute-start.18) | collective-permute-done | bytes 1048608 | tf_op jit(solution)/shard_map/ppermute | solution.py:46
  95.7 8.3 %collective-permute-start.21 = (bf16[2,8,8,3072]{3,2,1,0:T(8,128)(2,1)}, bf16[2,8,8,3072]{3,2,1,0:T(8,128)(2,1)}, u32[]{:S(2)}, u32[]{:S(2)}) collective-permute-start(bf16[2,8,8,3072]{3,2,1,0:T(8,128)(2,1)} %get-tuple-element.32), channel_id=1, source_target_pairs={{32,63},{33,32},{34,33},{35,34},{36,35},{37,36},{38,37},{39,38},{4... | collective-permute-start | bytes 2359304 | tf_op jit(solution)/shard_map/ppermute | solution.py:33
  104.1 1.9 collective-permute-start.20
  106.1 2.2 %shard_map.52 = (bf16[2,32,8,512]{3,2,1,0:T(8,128)(2,1)}, bf16[2,32,8,512]{3,2,1,0:T(8,128)(2,1)}) custom-call(bf16[2,1,32,16,3072]{4,3,2,1,0:T(8,128)(2,1)} %refs_2_.9, bf16[2,8,8,3072]{3,2,1,0:T(8,128)(2,1)} %get-tuple-element.25.refs_1_), custom_call_target="tpu_custom_call" | custom-call | flops 1000 | bytes 1000 | tf_op jit(solution)/shard_map/pallas_call | solution.py:58
  108.3 2.2 %shard_map.53 = (bf16[2,32,8,512]{3,2,1,0:T(8,128)(2,1)}, bf16[2,32,8,512]{3,2,1,0:T(8,128)(2,1)}) custom-call(bf16[2,1,32,16,3072]{4,3,2,1,0:T(8,128)(2,1)} %refs_2_.9, bf16[2,32,8,512]{3,2,1,0:T(8,128)(2,1)} %get-tuple-element.26.refs_1_), custom_call_target="tpu_custom_call" | custom-call | flops 1000 | bytes 1000 | tf_op jit(solution)/shard_map/pallas_call | solution.py:58
  110.5 2.1 %shard_map.54 = bf16[2,2,8,8,1024]{4,3,2,1,0:T(8,128)(2,1)} custom-call(s32[1]{0:T(128)} %bitcast.refs_0_, bf16[2,32,8,1024]{3,2,1,0:T(8,128)(2,1)} %collective-permute-done.17.refs_1_.refs_2_.refs_3_, bf16[2,32,8,1024]{3,2,1,0:T(8,128)(2,1)} %collective-permute-done.17.refs_1_.refs_2_.refs_3_, ...), custom_call_target="tpu_custom_call" | custom-call | flops 1000 | bytes 1000 | tf_op jit(solution)/shard_map/pallas_call | solution.py:58
  112.7 0.9 select_convert_fusion.refs_27_
  113.6 14.1 %collective-permute-done.21.refs_9_ = bf16[2,8,8,3072]{3,2,1,0:T(8,128)(2,1)} collective-permute-done((bf16[2,8,8,3072]{3,2,1,0:T(8,128)(2,1)}, bf16[2,8,8,3072]{3,2,1,0:T(8,128)(2,1)}, u32[]{:S(2)}, u32[]{:S(2)}) %collective-permute-start.21) | collective-permute-done | bytes 786464 | tf_op jit(solution)/shard_map/ppermute | solution.py:33
  128.1 13.1 %shard_map.55.refs_5_.refs_28_ = bf16[1,32,16,3072]{3,2,1,0:T(8,128)(2,1)} custom-call(s32[1]{0:T(128)} %bitcast.refs_0_, bf16[1,32,16,3072]{3,2,1,0:T(8,128)(2,1)} %refs_1_.9, bf16[2,1,32,16,3072]{4,3,2,1,0:T(8,128)(2,1)} %refs_2_.9, bf16[2,32,8,1024]{3,2,1,0:T(8,128)(2,1)} %collective-permute-done.17.refs_1_.refs_2_.refs_3_, ...), custom_call_target="tpu_custom_call" | custom-call | flops 1000 | bytes 1000 | tf_op jit(solution)/shard_map/pallas_call | solution.py:253
  141.3 2.1 %shard_map.56 = bf16[2,2,8,8,1024]{4,3,2,1,0:T(8,128)(2,1)} custom-call(s32[1]{0:T(128)} %bitcast.refs_0_, bf16[2,32,8,1024]{3,2,1,0:T(8,128)(2,1)} %collective-permute-done.15.refs_1_.refs_2_.refs_3_, bf16[2,32,8,1024]{3,2,1,0:T(8,128)(2,1)} %collective-permute-done.15.refs_1_.refs_2_.refs_3_, ...), custom_call_target="tpu_custom_call" | custom-call | flops 1000 | bytes 1000 | tf_op jit(solution)/shard_map/pallas_call | solution.py:58
  143.4 5.7 %collective-permute-start.14 = (bf16[2,32,8,512]{3,2,1,0:T(8,128)(2,1)}, bf16[2,32,8,512]{3,2,1,0:T(8,128)(2,1)}, u32[]{:S(2)}, u32[]{:S(2)}) collective-permute-start(bf16[2,32,8,512]{3,2,1,0:T(8,128)(2,1)} %get-tuple-element.29), channel_id=1, source_target_pairs={{0,31},{1,0},{2,1},{3,2},{4,3},{5,4},{6,5},{7,6},{8,7},{9,8},{10,9... | collective-permute-start | bytes 1572872 | tf_op jit(solution)/shard_map/ppermute | solution.py:46
  149.1 5.7 %collective-permute-start.11 = (bf16[2,32,8,512]{3,2,1,0:T(8,128)(2,1)}, bf16[2,32,8,512]{3,2,1,0:T(8,128)(2,1)}, u32[]{:S(2)}, u32[]{:S(2)}) collective-permute-start(bf16[2,32,8,512]{3,2,1,0:T(8,128)(2,1)} %get-tuple-element.28), channel_id=1, source_target_pairs={{0,31},{1,0},{2,1},{3,2},{4,3},{5,4},{6,5},{7,6},{8,7},{9,8},{10,9... | collective-permute-start | bytes 1572872 | tf_op jit(solution)/shard_map/ppermute | solution.py:46
  154.8 13.2 %shard_map.57.refs_5_.refs_28_ = bf16[1,32,16,3072]{3,2,1,0:T(8,128)(2,1)} custom-call(s32[1]{0:T(128)} %bitcast.refs_0_, bf16[1,32,16,3072]{3,2,1,0:T(8,128)(2,1)} %refs_1_.9, bf16[2,1,32,16,3072]{4,3,2,1,0:T(8,128)(2,1)} %refs_2_.9, bf16[2,32,8,1024]{3,2,1,0:T(8,128)(2,1)} %collective-permute-done.15.refs_1_.refs_2_.refs_3_, ...), custom_call_target="tpu_custom_call", output_to_operand_aliasing={{}: (28, {})} | custom-call | flops 1000 | bytes 1000 | tf_op jit(solution)/shard_map/pallas_call | solution.py:253
  167.9 1.8 shard_map.58
  169.8 1.3 collective-permute-start.35
  171.1 1.5 collective-permute-done.35.refs_7_
  172.6 8.2 %shard_map.59.refs_5_.refs_28_ = bf16[1,32,16,3072]{3,2,1,0:T(8,128)(2,1)} custom-call(s32[1]{0:T(128)} %bitcast.refs_0_, bf16[1,32,16,3072]{3,2,1,0:T(8,128)(2,1)} %refs_1_.9, bf16[2,1,32,16,3072]{4,3,2,1,0:T(8,128)(2,1)} %refs_2_.9, bf16[2,32,8,512]{3,2,1,0:T(8,128)(2,1)} %collective-permute-done.13.refs_1_.refs_2_.refs_3_, ...), custom_call_target="tpu_custom_call", output_to_operand_aliasing={{}: (28, {})} | custom-call | flops 1000 | bytes 1000 | tf_op jit(solution)/shard_map/pallas_call | solution.py:253
  180.8 1.8 shard_map.60
  183.0 1.5 collective-permute-done.36.refs_7_
  184.5 8.2 %shard_map.61 = bf16[1,32,16,3072]{3,2,1,0:T(8,128)(2,1)} custom-call(s32[1]{0:T(128)} %bitcast.refs_0_, bf16[1,32,16,3072]{3,2,1,0:T(8,128)(2,1)} %refs_1_.9, bf16[2,1,32,16,3072]{4,3,2,1,0:T(8,128)(2,1)} %refs_2_.9, bf16[2,32,8,512]{3,2,1,0:T(8,128)(2,1)} %collective-permute-done.10.refs_1_.refs_2_.refs_3_, ...), custom_call_target="tpu_custom_call", output_to_operand_aliasing={{}: (28, {})} | custom-call | flops 1000 | bytes 1000 | tf_op jit(solution)/shard_map/pallas_call | solution.py:253
  (76 shorter events, 6.3 us)
Async XLA Ops:
  0.0 6.1 %collective-permute-start.1 = (bf16[2,1,4,3072]{3,2,1,0:T(4,128)(2,1)}, bf16[2,1,4,3072]{3,2,1,0:T(4,128)(2,1)S(1)}, u32[]{:S(2)}, u32[]{:S(2)}) collective-permute-start(bf16[2,1,4,3072]{3,2,1,0:T(4,128)(2,1)} %refs_0_.5), channel_id=1, source_target_pairs={{0,64},{1,65},{2,66},{3,67},{4,68},{5,69},{6,70},{7,71},{8,72},{9,... | collective-permute-start | bytes 147464 | tf_op jit(solution)/shard_map/ppermute | solution.py:42
  4.4 3.4 %collective-permute-start = (bf16[2,1,4,3072]{3,2,1,0:T(4,128)(2,1)}, bf16[2,1,4,3072]{3,2,1,0:T(4,128)(2,1)S(1)}, u32[]{:S(2)}, u32[]{:S(2)}) collective-permute-start(bf16[2,1,4,3072]{3,2,1,0:T(4,128)(2,1)} %refs_0_.5), channel_id=1, source_target_pairs={{0,4},{1,5},{2,6},{3,7},{4,0},{5,1},{6,2},{7,3},{8,12},{9,13},{10,... | collective-permute-start | bytes 147464 | tf_op jit(solution)/shard_map/ppermute | solution.py:42
  5.2 4.4 %collective-permute-start.2 = (bf16[2,1,4,3072]{3,2,1,0:T(4,128)(2,1)}, bf16[2,1,4,3072]{3,2,1,0:T(4,128)(2,1)S(1)}, u32[]{:S(2)}, u32[]{:S(2)}) collective-permute-start(bf16[2,1,4,3072]{3,2,1,0:T(4,128)(2,1)} %refs_0_.5), channel_id=1, source_target_pairs={{0,68},{1,69},{2,70},{3,71},{4,64},{5,65},{6,66},{7,67},{8,76},{9,... | collective-permute-start | bytes 147464 | tf_op jit(solution)/shard_map/ppermute | solution.py:42
  6.1 3.4 %copy-start.9 = (bf16[2,1,4,3072]{3,2,1,0:T(4,128)(2,1)}, bf16[2,1,4,3072]{3,2,1,0:T(4,128)(2,1)S(1)}, u32[]{:S(2)}) copy-start(bf16[2,1,4,3072]{3,2,1,0:T(4,128)(2,1)S(1)} %collective-permute-done.1.refs_2_) | copy-start | bytes 147460
  7.8 1.8 copy-start.10
  11.7 8.8 %collective-permute-start.6 = (bf16[4,2,4,3072]{3,2,1,0:T(4,128)(2,1)}, bf16[4,2,4,3072]{3,2,1,0:T(4,128)(2,1)S(1)}, u32[]{:S(2)}, u32[]{:S(2)}) collective-permute-start(bf16[4,2,4,3072]{3,2,1,0:T(4,128)(2,1)} %shard_map.46.refs_3_.refs_1_), channel_id=1, source_target_pairs={{0,2},{1,3},{2,0},{3,1},{4,6},{5,7},{6,4},{7,5},{8,10},{9,11},{10,... | collective-permute-start | bytes 589832 | tf_op jit(solution)/shard_map/ppermute | solution.py:42
  14.6 7.9 %collective-permute-start.5 = (bf16[4,2,4,3072]{3,2,1,0:T(4,128)(2,1)}, bf16[4,2,4,3072]{3,2,1,0:T(4,128)(2,1)}, u32[]{:S(2)}, u32[]{:S(2)}) collective-permute-start(bf16[4,2,4,3072]{3,2,1,0:T(4,128)(2,1)} %shard_map.46.refs_3_.refs_1_), channel_id=1, source_target_pairs={{0,3},{1,0},{2,1},{3,2},{4,7},{5,4},{6,5},{7,6},{8,11},{9,8},{10,9... | collective-permute-start | bytes 589832 | tf_op jit(solution)/shard_map/ppermute | solution.py:42
  15.4 8.6 %collective-permute-start.4 = (bf16[4,2,4,3072]{3,2,1,0:T(4,128)(2,1)}, bf16[4,2,4,3072]{3,2,1,0:T(4,128)(2,1)}, u32[]{:S(2)}, u32[]{:S(2)}) collective-permute-start(bf16[4,2,4,3072]{3,2,1,0:T(4,128)(2,1)} %shard_map.46.refs_3_.refs_1_), channel_id=1, source_target_pairs={{0,1},{1,2},{2,3},{3,0},{4,5},{5,6},{6,7},{7,4},{8,9},{9,10},{10,1... | collective-permute-start | bytes 589832 | tf_op jit(solution)/shard_map/ppermute | solution.py:42
  20.6 3.4 %copy-start.8 = (bf16[4,2,4,3072]{3,2,1,0:T(4,128)(2,1)}, bf16[4,2,4,3072]{3,2,1,0:T(4,128)(2,1)S(1)}, u32[]{:S(2)}) copy-start(bf16[4,2,4,3072]{3,2,1,0:T(4,128)(2,1)S(1)} %collective-permute-done.6.refs_4_) | copy-start | bytes 589828
  26.4 4.6 %collective-permute-start.8 = (bf16[8,8,3072]{2,1,0:T(8,128)(2,1)}, bf16[8,8,3072]{2,1,0:T(8,128)(2,1)S(1)}, u32[]{:S(2)}, u32[]{:S(2)}) collective-permute-start(bf16[8,8,3072]{2,1,0:T(8,128)(2,1)} %get-tuple-element.22), channel_id=1, source_target_pairs={{0,32},{1,33},{2,34},{3,35},{4,36},{5,37},{6,38},{7,39},{8,40},{9,... | collective-permute-start | bytes 1179656 | tf_op jit(solution)/shard_map/ppermute | solution.py:42
  28.4 3.8 %collective-permute-start.27 = (bf16[8,8,3072]{2,1,0:T(8,128)(2,1)}, bf16[8,8,3072]{2,1,0:T(8,128)(2,1)S(1)}, u32[]{:S(2)}, u32[]{:S(2)}) collective-permute-start(bf16[8,8,3072]{2,1,0:T(8,128)(2,1)} %get-tuple-element.21.refs_10_), channel_id=1, source_target_pairs={{0,32},{1,33},{2,34},{3,35},{4,36},{5,37},{6,38},{7,39},{8,40},{9,... | collective-permute-start | bytes 1179656 | tf_op jit(solution)/shard_map/ppermute | solution.py:42
  28.4 10.8 %collective-permute-start.23 = (bf16[8,8,3072]{2,1,0:T(8,128)(2,1)}, bf16[8,8,3072]{2,1,0:T(8,128)(2,1)S(1)}, u32[]{:S(2)}, u32[]{:S(2)}) collective-permute-start(bf16[8,8,3072]{2,1,0:T(8,128)(2,1)} %get-tuple-element.21.refs_10_), channel_id=1, source_target_pairs={{0,24},{1,25},{2,26},{3,27},{4,28},{5,29},{6,30},{7,31},{8,0},{9,1... | collective-permute-start | bytes 1179656 | tf_op jit(solution)/shard_map/ppermute | solution.py:42
  30.9 12.4 %collective-permute-start.7 = (bf16[8,8,3072]{2,1,0:T(8,128)(2,1)}, bf16[8,8,3072]{2,1,0:T(8,128)(2,1)S(1)}, u32[]{:S(2)}, u32[]{:S(2)}) collective-permute-start(bf16[8,8,3072]{2,1,0:T(8,128)(2,1)} %get-tuple-element.21.refs_10_), channel_id=1, source_target_pairs={{0,8},{1,9},{2,10},{3,11},{4,12},{5,13},{6,14},{7,15},{8,16},{9,17... | collective-permute-start | bytes 1179656 | tf_op jit(solution)/shard_map/ppermute | solution.py:42
  30.9 33.4 %copy-start.1 = (bf16[8,8,3072]{2,1,0:T(8,128)(2,1)}, bf16[8,8,3072]{2,1,0:T(8,128)(2,1)S(1)}, u32[]{:S(2)}) copy-start(bf16[8,8,3072]{2,1,0:T(8,128)(2,1)S(1)} %collective-permute-done.8.refs_11_) | copy-start | bytes 1179652
  30.9 14.2 %collective-permute-start.26 = (bf16[8,8,3072]{2,1,0:T(8,128)(2,1)S(1)}, bf16[8,8,3072]{2,1,0:T(8,128)(2,1)S(1)}, u32[]{:S(2)}, u32[]{:S(2)}) collective-permute-start(bf16[8,8,3072]{2,1,0:T(8,128)(2,1)S(1)} %collective-permute-done.8.refs_11_), channel_id=1, source_target_pairs={{0,32},{1,33},{2,34},{3,35},{4,36},{5,37},{6,38},{7,39},{8,40},{9,... | collective-permute-start | bytes 1179656 | tf_op jit(solution)/shard_map/ppermute | solution.py:42
  31.8 18.9 %collective-permute-start.22 = (bf16[8,8,3072]{2,1,0:T(8,128)(2,1)S(1)}, bf16[8,8,3072]{2,1,0:T(8,128)(2,1)}, u32[]{:S(2)}, u32[]{:S(2)}) collective-permute-start(bf16[8,8,3072]{2,1,0:T(8,128)(2,1)S(1)} %collective-permute-done.8.refs_11_), channel_id=1, source_target_pairs={{0,8},{1,9},{2,10},{3,11},{4,12},{5,13},{6,14},{7,15},{8,16},{9,17... | collective-permute-start | bytes 1179656 | tf_op jit(solution)/shard_map/ppermute | solution.py:42
  32.2 32.1 %copy-start.2 = (bf16[8,8,3072]{2,1,0:T(8,128)(2,1)}, bf16[8,8,3072]{2,1,0:T(8,128)(2,1)S(1)}, u32[]{:S(2)}) copy-start(bf16[8,8,3072]{2,1,0:T(8,128)(2,1)S(1)} %collective-permute-done.27.refs_19_) | copy-start | bytes 1179652
  32.2 20.2 %collective-permute-start.9 = (bf16[8,8,3072]{2,1,0:T(8,128)(2,1)S(1)}, bf16[8,8,3072]{2,1,0:T(8,128)(2,1)}, u32[]{:S(2)}, u32[]{:S(2)}) collective-permute-start(bf16[8,8,3072]{2,1,0:T(8,128)(2,1)S(1)} %collective-permute-done.8.refs_11_), channel_id=1, source_target_pairs={{0,24},{1,25},{2,26},{3,27},{4,28},{5,29},{6,30},{7,31},{8,0},{9,1... | collective-permute-start | bytes 1179656 | tf_op jit(solution)/shard_map/ppermute | solution.py:42
  39.2 25.1 %copy-start.3 = (bf16[8,8,3072]{2,1,0:T(8,128)(2,1)}, bf16[8,8,3072]{2,1,0:T(8,128)(2,1)S(1)}, u32[]{:S(2)}) copy-start(bf16[8,8,3072]{2,1,0:T(8,128)(2,1)S(1)} %collective-permute-done.23.refs_14_) | copy-start | bytes 1179652
  39.2 42.5 %collective-permute-start.3 = (bf16[2,8,16,3072]{3,2,1,0:T(8,128)(2,1)}, bf16[2,8,16,3072]{3,2,1,0:T(8,128)(2,1)}, u32[]{:S(2)}, u32[]{:S(2)}) collective-permute-start(bf16[2,8,16,3072]{3,2,1,0:T(8,128)(2,1)} %get-tuple-element.19), channel_id=1, source_target_pairs={{32,64},{33,65},{34,66},{35,67},{36,68},{37,69},{38,70},{39,71},{4... | collective-permute-start | bytes 4718600 | tf_op jit(solution)/shard_map/ppermute | solution.py:33
  43.3 9.1 %copy-start = (bf16[8,8,3072]{2,1,0:T(8,128)(2,1)}, bf16[8,8,3072]{2,1,0:T(8,128)(2,1)S(1)}, u32[]{:S(2)}) copy-start(bf16[8,8,3072]{2,1,0:T(8,128)(2,1)S(1)} %collective-permute-done.7.refs_1_.refs_12_) | copy-start | bytes 1179652
  43.3 9.1 %collective-permute-start.31 = (bf16[8,8,3072]{2,1,0:T(8,128)(2,1)S(1)}, bf16[8,8,3072]{2,1,0:T(8,128)(2,1)S(1)}, u32[]{:S(2)}, u32[]{:S(2)}) collective-permute-start(bf16[8,8,3072]{2,1,0:T(8,128)(2,1)S(1)} %collective-permute-done.23.refs_14_), channel_id=1, source_target_pairs={{0,32},{1,33},{2,34},{3,35},{4,36},{5,37},{6,38},{7,39},{8,40},{9,... | collective-permute-start | bytes 1179656 | tf_op jit(solution)/shard_map/ppermute | solution.py:42
  45.1 19.1 %copy-start.4 = (bf16[8,8,3072]{2,1,0:T(8,128)(2,1)}, bf16[8,8,3072]{2,1,0:T(8,128)(2,1)S(1)}, u32[]{:S(2)}) copy-start(bf16[8,8,3072]{2,1,0:T(8,128)(2,1)S(1)} %collective-permute-done.26.refs_18_) | copy-start | bytes 1179652
  45.1 7.4 %collective-permute-start.29 = (bf16[8,8,3072]{2,1,0:T(8,128)(2,1)S(1)}, bf16[8,8,3072]{2,1,0:T(8,128)(2,1)S(1)}, u32[]{:S(2)}, u32[]{:S(2)}) collective-permute-start(bf16[8,8,3072]{2,1,0:T(8,128)(2,1)S(1)} %collective-permute-done.7.refs_1_.refs_12_), channel_id=1, source_target_pairs={{0,32},{1,33},{2,34},{3,35},{4,36},{5,37},{6,38},{7,39},{8,40},{9,... | collective-permute-start | bytes 1179656 | tf_op jit(solution)/shard_map/ppermute | solution.py:42
  50.7 31.8 %collective-permute-start.12 = (bf16[2,8,16,3072]{3,2,1,0:T(8,128)(2,1)}, bf16[2,8,16,3072]{3,2,1,0:T(8,128)(2,1)}, u32[]{:S(2)}, u32[]{:S(2)}) collective-permute-start(bf16[2,8,16,3072]{3,2,1,0:T(8,128)(2,1)} %get-tuple-element.20.refs_5_), channel_id=1, source_target_pairs={{0,32},{1,33},{2,34},{3,35},{4,36},{5,37},{6,38},{7,39},{8,40},{9,... | collective-permute-start | bytes 4718600 | tf_op jit(solution)/shard_map/ppermute | solution.py:42
  52.4 11.9 %collective-permute-start.24 = (bf16[8,8,3072]{2,1,0:T(8,128)(2,1)S(1)}, bf16[8,8,3072]{2,1,0:T(8,128)(2,1)S(1)}, u32[]{:S(2)}, u32[]{:S(2)}) collective-permute-start(bf16[8,8,3072]{2,1,0:T(8,128)(2,1)S(1)} %collective-permute-done.7.refs_1_.refs_12_), channel_id=1, source_target_pairs={{0,8},{1,9},{2,10},{3,11},{4,12},{5,13},{6,14},{7,15},{8,16},{9,17... | collective-permute-start | bytes 1179656 | tf_op jit(solution)/shard_map/ppermute | solution.py:42
  52.4 11.9 %copy-start.5 = (bf16[8,8,3072]{2,1,0:T(8,128)(2,1)}, bf16[8,8,3072]{2,1,0:T(8,128)(2,1)S(1)}, u32[]{:S(2)}) copy-start(bf16[8,8,3072]{2,1,0:T(8,128)(2,1)S(1)} %collective-permute-done.31.refs_23_) | copy-start | bytes 1179652
  52.4 15.3 %collective-permute-start.28 = (bf16[8,8,3072]{2,1,0:T(8,128)(2,1)}, bf16[8,8,3072]{2,1,0:T(8,128)(2,1)}, u32[]{:S(2)}, u32[]{:S(2)}) collective-permute-start(bf16[8,8,3072]{2,1,0:T(8,128)(2,1)} %collective-permute-done.22.refs_13_), channel_id=1, source_target_pairs={{0,32},{1,33},{2,34},{3,35},{4,36},{5,37},{6,38},{7,39},{8,40},{9,... | collective-permute-start | bytes 1179656 | tf_op jit(solution)/shard_map/ppermute | solution.py:42
  52.6 11.7 %copy-start.6 = (bf16[8,8,3072]{2,1,0:T(8,128)(2,1)}, bf16[8,8,3072]{2,1,0:T(8,128)(2,1)S(1)}, u32[]{:S(2)}) copy-start(bf16[8,8,3072]{2,1,0:T(8,128)(2,1)S(1)} %collective-permute-done.29.refs_21_) | copy-start | bytes 1179652
  52.6 15.2 %collective-permute-start.30 = (bf16[8,8,3072]{2,1,0:T(8,128)(2,1)}, bf16[8,8,3072]{2,1,0:T(8,128)(2,1)}, u32[]{:S(2)}, u32[]{:S(2)}) collective-permute-start(bf16[8,8,3072]{2,1,0:T(8,128)(2,1)} %collective-permute-done.9.refs_2_.refs_15_), channel_id=1, source_target_pairs={{0,32},{1,33},{2,34},{3,35},{4,36},{5,37},{6,38},{7,39},{8,40},{9,... | collective-permute-start | bytes 1179656 | tf_op jit(solution)/shard_map/ppermute | solution.py:42
  64.3 0.8 copy-start.7
  65.1 10.1 %collective-permute-start.25 = (bf16[8,8,3072]{2,1,0:T(8,128)(2,1)}, bf16[8,8,3072]{2,1,0:T(8,128)(2,1)}, u32[]{:S(2)}, u32[]{:S(2)}) collective-permute-start(bf16[8,8,3072]{2,1,0:T(8,128)(2,1)} %collective-permute-done.9.refs_2_.refs_15_), channel_id=1, source_target_pairs={{0,24},{1,25},{2,26},{3,27},{4,28},{5,29},{6,30},{7,31},{8,0},{9,1... | collective-permute-start | bytes 1179656 | tf_op jit(solution)/shard_map/ppermute | solution.py:42
  67.7 28.0 %collective-permute-start.18 = (bf16[2,32,8,1024]{3,2,1,0:T(8,128)(2,1)}, bf16[2,32,8,1024]{3,2,1,0:T(8,128)(2,1)}, u32[]{:S(2)}, u32[]{:S(2)}) collective-permute-start(bf16[2,32,8,1024]{3,2,1,0:T(8,128)(2,1)} %get-tuple-element.31), channel_id=1, source_target_pairs={{0,31},{1,0},{2,1},{3,2},{4,3},{5,4},{6,5},{7,6},{8,7},{9,8},{10,9... | collective-permute-start | bytes 3145736 | tf_op jit(solution)/shard_map/ppermute | solution.py:46
  67.8 36.2 %collective-permute-start.17 = (bf16[2,32,8,1024]{3,2,1,0:T(8,128)(2,1)}, bf16[2,32,8,1024]{3,2,1,0:T(8,128)(2,1)}, u32[]{:S(2)}, u32[]{:S(2)}) collective-permute-start(bf16[2,32,8,1024]{3,2,1,0:T(8,128)(2,1)} %get-tuple-element.23.refs_1_), channel_id=1, source_target_pairs={{0,1},{1,2},{2,3},{3,4},{4,5},{5,6},{6,7},{7,8},{8,9},{9,10},{10,1... | collective-permute-start | bytes 3145736 | tf_op jit(solution)/shard_map/ppermute | solution.py:46
  75.1 5.9 %collective-permute-start.33 = (bf16[8,8,3072]{2,1,0:T(8,128)(2,1)}, bf16[8,8,3072]{2,1,0:T(8,128)(2,1)}, u32[]{:S(2)}, u32[]{:S(2)}) collective-permute-start(bf16[8,8,3072]{2,1,0:T(8,128)(2,1)} %copy-done.7), channel_id=1, source_target_pairs={{0,32},{1,33},{2,34},{3,35},{4,36},{5,37},{6,38},{7,39},{8,40},{9,... | collective-permute-start | bytes 1179656 | tf_op jit(solution)/shard_map/ppermute | solution.py:42
  81.0 60.3 %collective-permute-start.16 = (bf16[2,32,8,1024]{3,2,1,0:T(8,128)(2,1)}, bf16[2,32,8,1024]{3,2,1,0:T(8,128)(2,1)}, u32[]{:S(2)}, u32[]{:S(2)}) collective-permute-start(bf16[2,32,8,1024]{3,2,1,0:T(8,128)(2,1)} %get-tuple-element.30), channel_id=1, source_target_pairs={{0,31},{1,0},{2,1},{3,2},{4,3},{5,4},{6,5},{7,6},{8,7},{9,8},{10,9... | collective-permute-start | bytes 3145736 | tf_op jit(solution)/shard_map/ppermute | solution.py:46
  81.7 59.6 %collective-permute-start.15 = (bf16[2,32,8,1024]{3,2,1,0:T(8,128)(2,1)}, bf16[2,32,8,1024]{3,2,1,0:T(8,128)(2,1)}, u32[]{:S(2)}, u32[]{:S(2)}) collective-permute-start(bf16[2,32,8,1024]{3,2,1,0:T(8,128)(2,1)} %get-tuple-element.24.refs_1_), channel_id=1, source_target_pairs={{0,1},{1,2},{2,3},{3,4},{4,5},{5,6},{6,7},{7,8},{8,9},{9,10},{10,1... | collective-permute-start | bytes 3145736 | tf_op jit(solution)/shard_map/ppermute | solution.py:46
  82.5 30.1 %collective-permute-start.32 = (bf16[8,8,3072]{2,1,0:T(8,128)(2,1)}, bf16[8,8,3072]{2,1,0:T(8,128)(2,1)}, u32[]{:S(2)}, u32[]{:S(2)}) collective-permute-start(bf16[8,8,3072]{2,1,0:T(8,128)(2,1)} %collective-permute-done.25.refs_17_), channel_id=1, source_target_pairs={{0,32},{1,33},{2,34},{3,35},{4,36},{5,37},{6,38},{7,39},{8,40},{9,... | collective-permute-start | bytes 1179656 | tf_op jit(solution)/shard_map/ppermute | solution.py:42
  95.7 31.9 %collective-permute-start.21 = (bf16[2,8,8,3072]{3,2,1,0:T(8,128)(2,1)}, bf16[2,8,8,3072]{3,2,1,0:T(8,128)(2,1)}, u32[]{:S(2)}, u32[]{:S(2)}) collective-permute-start(bf16[2,8,8,3072]{3,2,1,0:T(8,128)(2,1)} %get-tuple-element.32), channel_id=1, source_target_pairs={{32,63},{33,32},{34,33},{35,34},{36,35},{37,36},{38,37},{39,38},{4... | collective-permute-start | bytes 2359304 | tf_op jit(solution)/shard_map/ppermute | solution.py:33
  104.1 24.1 %collective-permute-start.20 = (bf16[2,8,8,3072]{3,2,1,0:T(8,128)(2,1)}, bf16[2,8,8,3072]{3,2,1,0:T(8,128)(2,1)}, u32[]{:S(2)}, u32[]{:S(2)}) collective-permute-start(bf16[2,8,8,3072]{3,2,1,0:T(8,128)(2,1)} %get-tuple-element.25.refs_1_), channel_id=1, source_target_pairs={{32,33},{33,34},{34,35},{35,36},{36,37},{37,38},{38,39},{39,40},{4... | collective-permute-start | bytes 2359304 | tf_op jit(solution)/shard_map/ppermute | solution.py:33
  112.6 15.5 %collective-permute-start.19 = (bf16[2,2,8,8,1024]{4,3,2,1,0:T(8,128)(2,1)}, bf16[2,2,8,8,1024]{4,3,2,1,0:T(8,128)(2,1)}, u32[]{:S(2)}, u32[]{:S(2)}) collective-permute-start(bf16[2,2,8,8,1024]{4,3,2,1,0:T(8,128)(2,1)} %shard_map.54), channel_id=1, source_target_pairs={{0,32},{1,33},{2,34},{3,35},{4,36},{5,37},{6,38},{7,39},{8,40},{9,... | collective-permute-start | bytes 1572872 | tf_op jit(solution)/shard_map/ppermute | solution.py:42
  143.4 11.4 %collective-permute-start.34 = (bf16[2,2,8,8,1024]{4,3,2,1,0:T(8,128)(2,1)}, bf16[2,2,8,8,1024]{4,3,2,1,0:T(8,128)(2,1)}, u32[]{:S(2)}, u32[]{:S(2)}) collective-permute-start(bf16[2,2,8,8,1024]{4,3,2,1,0:T(8,128)(2,1)} %shard_map.56), channel_id=1, source_target_pairs={{0,32},{1,33},{2,34},{3,35},{4,36},{5,37},{6,38},{7,39},{8,40},{9,... | collective-permute-start | bytes 1572872 | tf_op jit(solution)/shard_map/ppermute | solution.py:42
  143.4 24.5 %collective-permute-start.14 = (bf16[2,32,8,512]{3,2,1,0:T(8,128)(2,1)}, bf16[2,32,8,512]{3,2,1,0:T(8,128)(2,1)}, u32[]{:S(2)}, u32[]{:S(2)}) collective-permute-start(bf16[2,32,8,512]{3,2,1,0:T(8,128)(2,1)} %get-tuple-element.29), channel_id=1, source_target_pairs={{0,31},{1,0},{2,1},{3,2},{4,3},{5,4},{6,5},{7,6},{8,7},{9,8},{10,9... | collective-permute-start | bytes 1572872 | tf_op jit(solution)/shard_map/ppermute | solution.py:46
  149.1 18.9 %collective-permute-start.13 = (bf16[2,32,8,512]{3,2,1,0:T(8,128)(2,1)}, bf16[2,32,8,512]{3,2,1,0:T(8,128)(2,1)}, u32[]{:S(2)}, u32[]{:S(2)}) collective-permute-start(bf16[2,32,8,512]{3,2,1,0:T(8,128)(2,1)} %get-tuple-element.26.refs_1_), channel_id=1, source_target_pairs={{0,1},{1,2},{2,3},{3,4},{4,5},{5,6},{6,7},{7,8},{8,9},{9,10},{10,1... | collective-permute-start | bytes 1572872 | tf_op jit(solution)/shard_map/ppermute | solution.py:46
  149.1 31.7 %collective-permute-start.11 = (bf16[2,32,8,512]{3,2,1,0:T(8,128)(2,1)}, bf16[2,32,8,512]{3,2,1,0:T(8,128)(2,1)}, u32[]{:S(2)}, u32[]{:S(2)}) collective-permute-start(bf16[2,32,8,512]{3,2,1,0:T(8,128)(2,1)} %get-tuple-element.28), channel_id=1, source_target_pairs={{0,31},{1,0},{2,1},{3,2},{4,3},{5,4},{6,5},{7,6},{8,7},{9,8},{10,9... | collective-permute-start | bytes 1572872 | tf_op jit(solution)/shard_map/ppermute | solution.py:46
  154.7 26.0 %collective-permute-start.10 = (bf16[2,32,8,512]{3,2,1,0:T(8,128)(2,1)}, bf16[2,32,8,512]{3,2,1,0:T(8,128)(2,1)}, u32[]{:S(2)}, u32[]{:S(2)}) collective-permute-start(bf16[2,32,8,512]{3,2,1,0:T(8,128)(2,1)} %get-tuple-element.27.refs_5_), channel_id=1, source_target_pairs={{0,1},{1,2},{2,3},{3,4},{4,5},{5,6},{6,7},{7,8},{8,9},{9,10},{10,1... | collective-permute-start | bytes 1572872 | tf_op jit(solution)/shard_map/ppermute | solution.py:46
  169.8 2.9 %collective-permute-start.35 = (bf16[2,2,8,8,512]{4,3,2,1,0:T(8,128)(2,1)}, bf16[2,2,8,8,512]{4,3,2,1,0:T(8,128)(2,1)}, u32[]{:S(2)}, u32[]{:S(2)}) collective-permute-start(bf16[2,2,8,8,512]{4,3,2,1,0:T(8,128)(2,1)} %shard_map.58), channel_id=1, source_target_pairs={{0,32},{1,33},{2,34},{3,35},{4,36},{5,37},{6,38},{7,39},{8,40},{9,... | collective-permute-start | bytes 786440 | tf_op jit(solution)/shard_map/ppermute | solution.py:42
  182.6 1.9 collective-permute-start.36
  (1 other events, 0.6 us)
